TPU v7x, 32 devices: a whole 2x2x4 slice. The times are simulated.
32 devices in a mesh: dp: 2 (over y), expert: 16 (over z, x, core).
Axes of the slice: x: 2, y: 2, z: 4, core: 2. Of those that a mesh axis runs over, the one named last changes fastest.
Arguments:
- tokens: bfloat16 [4096, 2560], P(('dp', 'expert')), may hold values from -6 to 6
- expert_ids: int32 [4096, 6], P(('dp', 'expert')), may hold values from 0 to 159, as said below
- gate_values: bfloat16 [4096, 6], P(('dp', 'expert')), may hold values from 0.29882812 to 1.59375
- gate_weight: bfloat16 [16, 768, 2560], P('expert', 'dp'), may hold values from -0.125 to 0.125
- up_weight: bfloat16 [16, 768, 2560], P('expert', 'dp'), may hold values from -0.125 to 0.125
- down_weight: bfloat16 [16, 768, 2560], P('expert', 'dp'), may hold values from -0.21875 to 0.21875
- first_moment: bfloat16 [16, 768, 2560], P('expert', 'dp'), may hold values from -6 to 6
- second_moment: bfloat16 [16, 768, 2560], P('expert', 'dp'), may hold values from 0.5 to 8
Outputs:
- new_down: bfloat16 [16, 768, 2560], P('expert', 'dp')
- new_first: bfloat16 [16, 768, 2560], P('expert', 'dp')
- new_second: bfloat16 [16, 768, 2560], P('expert', 'dp')
Inputs may be any that keep to these rules, and one draw needn't show every extreme that they name: `expert_ids`: each row names 6 different experts; among the rows of one device no expert is named more than 6 times. One expert below 16 is named exactly 6 times by the rows of every device, and in each device's rows another one too. In the rows of each device exactly 12 rows name only experts below 16, and the other rows name none of them. Ids of 16 or more name experts outside this computation.
All inputs are finite; a program needn't handle non-finite values.
Results may differ from a plain program's by a relative error of at most 0.015.
Values may be sent and summed in bfloat16 or wider, within the bound.
No kernel may reach another device: no remote copies, remote signals or barrier semaphores. Data moves between devices by JAX's collectives and lax.ppermute only.
A program may use at most 128 MiB of HBM per device.

v0:
```python
import jax
import jax.numpy as jnp
from jax import lax
from jax.sharding import PartitionSpec as P

CAP = 6


first_decay = 0.9
second_decay = 0.95
learn_rate = 0.00024
weight_decay = 0.1
adam_epsilon = 1e-08
adam_count = 100.0


def slot_table(id_block, gate_block, experts, capacity):
    numbers = jnp.arange(experts, dtype=jnp.int32)
    matches = id_block[:, :, None] == numbers[None, None, :]
    member = jnp.sum(matches.astype(jnp.int32), axis=1)
    chosen = jnp.sum(
        jnp.where(matches, gate_block[:, :, None].astype(jnp.float32), jnp.float32(0.0)), axis=1
    )
    position = jnp.cumsum(member, axis=0) - member
    slot_ids = jnp.arange(capacity, dtype=jnp.int32)
    onehot = member[:, :, None] * (position[:, :, None] == slot_ids[None, None, :]).astype(
        jnp.int32
    )
    return (onehot, chosen)


def expert_hidden(expert_rows, gate_rows, up_rows):
    contract = (((1,), (1,)), ((), ()))
    gate_part = lax.dot_general(
        expert_rows, gate_rows, contract, preferred_element_type=jnp.float32
    )
    up_part = lax.dot_general(expert_rows, up_rows, contract, preferred_element_type=jnp.float32)
    return (jax.nn.silu(gate_part) * up_part).astype(jnp.bfloat16)


def adam_update(gradient, weight_rows, first_rows, second_rows):
    first_new = first_decay * first_rows.astype(jnp.float32) + (1.0 - first_decay) * gradient
    second_new = (
        second_decay * second_rows.astype(jnp.float32) + (1.0 - second_decay) * gradient * gradient
    )
    first_hat = first_new / (1.0 - first_decay**adam_count)
    second_hat = second_new / (1.0 - second_decay**adam_count)
    weight_new = weight_rows.astype(jnp.float32) * (
        1.0 - learn_rate * weight_decay
    ) - learn_rate * first_hat / (jnp.sqrt(second_hat) + adam_epsilon)
    return (
        weight_new.astype(jnp.bfloat16),
        first_new.astype(jnp.bfloat16),
        second_new.astype(jnp.bfloat16),
    )


def local(
    tokens,
    expert_ids,
    gate_values,
    gate_weight,
    up_weight,
    down_weight,
    first_moment,
    second_moment,
):
    experts = lax.axis_size("expert")
    tok_count, model_width = tokens.shape
    capacity = CAP
    slot_count = experts * capacity
    onehot, chosen = slot_table(expert_ids, gate_values, experts, capacity)
    dispatch_map = onehot.reshape(tok_count, slot_count).astype(jnp.bfloat16)
    combine_map = (
        (onehot.astype(jnp.float32) * chosen[:, :, None])
        .reshape(tok_count, slot_count)
        .astype(jnp.bfloat16)
    )
    over_tokens = (((0,), (0,)), ((), ()))
    outgoing = lax.dot_general(
        dispatch_map, tokens, over_tokens, preferred_element_type=jnp.float32
    ).astype(jnp.bfloat16)
    arrived = lax.all_to_all(
        outgoing.reshape(experts, capacity, model_width),
        "expert",
        split_axis=0,
        concat_axis=0,
        tiled=True,
    )
    arrived = arrived.reshape(slot_count, model_width)
    gate_full, up_full, down_full = (
        lax.all_gather(gate_weight, "dp", axis=1, tiled=True),
        lax.all_gather(up_weight, "dp", axis=1, tiled=True),
        lax.all_gather(down_weight, "dp", axis=1, tiled=True),
    )
    hidden = expert_hidden(arrived, gate_full[0], up_full[0])
    outputs = jnp.dot(hidden, down_full[0], preferred_element_type=jnp.float32).astype(jnp.bfloat16)
    returned = lax.all_to_all(
        outputs.reshape(experts, capacity, model_width),
        "expert",
        split_axis=0,
        concat_axis=0,
        tiled=True,
    )
    returned = returned.reshape(slot_count, model_width)
    mixed = jnp.dot(combine_map, returned, preferred_element_type=jnp.float32)
    cotangent = jnp.tanh(tokens.astype(jnp.float32) + mixed).astype(jnp.bfloat16)
    weighted = lax.dot_general(
        combine_map, cotangent, over_tokens, preferred_element_type=jnp.float32
    ).astype(jnp.bfloat16)
    arrived_grad = lax.all_to_all(
        weighted.reshape(experts, capacity, model_width),
        "expert",
        split_axis=0,
        concat_axis=0,
        tiled=True,
    )
    arrived_grad = arrived_grad.reshape(slot_count, model_width)
    gradient = lax.psum_scatter(
        lax.dot_general(
            hidden, arrived_grad, over_tokens, preferred_element_type=jnp.float32
        ).astype(jnp.bfloat16),
        "dp",
        scatter_dimension=0,
        tiled=True,
    ).astype(jnp.float32)
    new_down, new_first, new_second = adam_update(
        gradient, down_weight[0], first_moment[0], second_moment[0]
    )
    return (new_down[None], new_first[None], new_second[None])


def solution(mesh):
    in_specs = (
        P(("dp", "expert"), None),
        P(("dp", "expert"), None),
        P(("dp", "expert"), None),
        P("expert", "dp", None),
        P("expert", "dp", None),
        P("expert", "dp", None),
        P("expert", "dp", None),
        P("expert", "dp", None),
    )
    out_specs = (P("expert", "dp", None), P("expert", "dp", None), P("expert", "dp", None))
    return jax.shard_map(local, mesh=mesh, in_specs=in_specs, out_specs=out_specs, check_vma=False)
```

profile of v0, /device:TPU:0, one launch (start us, length us, event | category | flops | bytes accessed | tf_op | source)
XLA Modules:
  0.0 293.6 jit_solution(724362942801839354)
XLA Ops:
  7.2 0.0 copy-start.2
  7.2 0.0 copy-start.1
  7.2 0.0 all-gather.4.cloned.1.call-start
  7.2 0.7 all-gather.4.cloned.1.call-update
  7.9 0.0 all-gather.6.cloned.1.call-start
  8.0 0.7 all-gather.6.cloned.1.call-update
  8.7 0.0 all-gather.8.cloned.1.call-start
  8.7 0.7 all-gather.8.cloned.1.call-update
  9.4 0.0 copy-done.2
  9.4 0.1 copy.22
  9.5 0.2 reduce_window_sum.11
  9.7 0.1 copy.24
  9.8 0.1 eq.45
  9.9 0.0 copy-done.1
  9.9 0.3 convolution_convert_fusion.2
  10.3 0.2 reshape.60
  10.5 25.4 %all_to_all.15 = bf16[16,6,2560]{2,1,0:T(8,128)(2,1)S(1)} all-to-all(bf16[16,6,2560]{2,1,0:T(8,128)(2,1)S(1)} %reshape.60), channel_id=1, replica_groups=mesh['dp'=2,'expert'=16] {'expert'}, dimensions={0} | all-to-all | bytes 983040 | tf_op jit(solution)/shard_map/all_to_all | solution.py:83
  35.9 0.2 reshape.61
  36.0 30.1 %all-gather.4.cloned.1.call-done = bf16[1,768,2560]{2,1,0:T(8,128)(2,1)} async-done(((bf16[1,384,2560]{2,1,0:T(8,128)(2,1)}), bf16[1,768,2560]{2,1,0:T(8,128)(2,1)}) %all-gather.4.cloned.1.call-update) | async-done | bytes 3932176 | tf_op jit(solution)/shard_map/all_gather | solution.py:92
  66.1 3.4 %fusion.6 = f32[96,768]{1,0:T(8,128)S(1)} fusion(bf16[96,2560]{1,0:T(8,128)(2,1)S(1)} %reshape.61, bf16[1,768,2560]{2,1,0:T(8,128)(2,1)} %all-gather.4.cloned.1.call-done), kind=kOutput, calls=%fused_computation.9 | convolution fusion | flops 377487360 | bytes 4718592 | tf_op jit(solution)/shard_map/dot_general | solution.py:34
  69.5 52.0 %all-gather.6.cloned.1.call-done = bf16[1,768,2560]{2,1,0:T(8,128)(2,1)} async-done(((bf16[1,384,2560]{2,1,0:T(8,128)(2,1)}), bf16[1,768,2560]{2,1,0:T(8,128)(2,1)}) %all-gather.6.cloned.1.call-update) | async-done | bytes 3932176 | tf_op jit(solution)/shard_map/all_gather | solution.py:93
  121.5 3.4 %fusion.23 = bf16[96,768]{1,0:T(8,128)(2,1)S(1)} fusion(bf16[96,2560]{1,0:T(8,128)(2,1)S(1)} %reshape.61, bf16[1,768,2560]{2,1,0:T(8,128)(2,1)} %all-gather.6.cloned.1.call-done, f32[96,768]{1,0:T(8,128)S(1)} %fusion.6), kind=kOutput, calls=%fused_computation.26 | convolution fusion | flops 377929728 | bytes 4866048 | tf_op jit(solution)/shard_map/dot_general | solution.py:37
  124.9 0.0 copy-start.3
  124.9 51.9 %all-gather.8.cloned.1.call-done = bf16[1,768,2560]{2,1,0:T(8,128)(2,1)} async-done(((bf16[1,384,2560]{2,1,0:T(8,128)(2,1)}), bf16[1,768,2560]{2,1,0:T(8,128)(2,1)}) %all-gather.8.cloned.1.call-update) | async-done | bytes 3932176 | tf_op jit(solution)/shard_map/all_gather | solution.py:94
  176.9 2.9 fusion.12
  179.7 1.0 reshape.62
  180.7 5.6 %all-to-all-start.1 = ((bf16[16,6,2560]{2,1,0:T(8,128)(2,1)}), bf16[16,6,2560]{2,1,0:T(8,128)(2,1)S(1)}, u32[]{:S(2)}, u32[]{:S(2)}) async-start(bf16[16,6,2560]{2,1,0:T(8,128)(2,1)} %reshape.62), calls=%async_computation.1 | async-start | bytes 1310720 | tf_op jit(solution)/shard_map/all_to_all | solution.py:98
  186.3 0.0 reduce-scatter.2.cloned.1.call-start
  186.4 0.0 copy-done.3
  186.5 16.5 %all-to-all-done.1 = bf16[16,6,2560]{2,1,0:T(8,128)(2,1)S(1)} async-done(((bf16[16,6,2560]{2,1,0:T(8,128)(2,1)}), bf16[16,6,2560]{2,1,0:T(8,128)(2,1)S(1)}, u32[]{:S(2)}, u32[]{:S(2)}) %all-to-all-start.1) | async-done | bytes 491552 | tf_op jit(solution)/shard_map/all_to_all | solution.py:98
  203.0 0.5 convolution_convert_fusion.1
  203.5 0.2 reshape.63
  203.7 22.8 %all_to_all.16 = bf16[16,6,2560]{2,1,0:T(8,128)(2,1)S(1)} all-to-all(bf16[16,6,2560]{2,1,0:T(8,128)(2,1)S(1)} %reshape.63), channel_id=1, replica_groups=mesh['dp'=2,'expert'=16] {'expert'}, dimensions={0} | all-to-all | bytes 983040 | tf_op jit(solution)/shard_map/all_to_all | solution.py:111
  226.5 0.2 reshape.64
  226.6 0.0 copy-start
  226.7 3.1 %convolution_convert_fusion = bf16[768,2560]{1,0:T(8,128)(2,1)} fusion(bf16[96,768]{1,0:T(8,128)(2,1)S(1)} %fusion.23, bf16[96,2560]{1,0:T(8,128)(2,1)S(1)} %reshape.64), kind=kOutput, calls=%fused_computation.1 | convolution fusion | flops 379453440 | bytes 4571136 | tf_op jit(solution)/shard_map/dot_general | solution.py:120
  229.7 0.0 reduce-scatter.2.cloned.1.call-update
  229.8 49.8 %reduce-scatter.2.cloned.1.call-done = bf16[384,2560]{1,0:T(8,128)(2,1)} async-done(((bf16[768,2560]{1,0:T(8,128)(2,1)}), bf16[384,2560]{1,0:T(8,128)(2,1)}) %reduce-scatter.2.cloned.1.call-update) | async-done | bytes 1966096 | tf_op jit(solution)/shard_map/reduce_scatter | solution.py:119
  279.5 0.0 copy-done
  279.5 7.5 %fusion.17 = (bf16[1,384,2560]{2,1,0:T(8,128)(2,1)}, bf16[1,384,2560]{2,1,0:T(8,128)(2,1)}, bf16[1,384,2560]{2,1,0:T(8,128)(2,1)}) fusion(bf16[384,2560]{1,0:T(8,128)(2,1)} %reduce-scatter.2.cloned.1.call-done, bf16[1,384,2560]{2,1,0:T(8,128)(2,1)} %param.15, bf16[1,384,2560]{2,1,0:T(8,128)(2,1)} %param.14, bf16[1,384,2560]{2,1,0:T(8,128)(2,1)S(1)} %copy-done), kind=kLoop, calls=%fused_computation.22 | loop fusion | flops 19660800 | bytes 13762560 | tf_op jit(solution)/shard_map/broadcast_in_dim | solution.py:130
  (12 shorter events, 0.1 us)
Async XLA Ops:
  7.2 2.2 copy-start.2
  7.2 2.8 copy-start.1
  7.2 58.9 %all-gather.4.cloned.1.call-start = ((), (), s32[]{:S(2)}) async-start(), calls=%async_computation.4 | async-start | bytes 5898240 | tf_op jit(solution)/shard_map/all_gather | solution.py:92
  7.9 113.6 %all-gather.6.cloned.1.call-start = ((), (), s32[]{:S(2)}) async-start(), calls=%async_computation.5 | async-start | bytes 5898240 | tf_op jit(solution)/shard_map/all_gather | solution.py:93
  8.7 168.2 %all-gather.8.cloned.1.call-start = ((), (), s32[]{:S(2)}) async-start(), calls=%async_computation.6 | async-start | bytes 5898240 | tf_op jit(solution)/shard_map/all_gather | solution.py:94
  124.9 61.5 %copy-start.3 = (bf16[128,6]{0,1:T(8,128)(2,1)S(1)}, bf16[128,6]{0,1:T(8,128)(2,1)}, u32[]{:S(2)}) copy-start(bf16[128,6]{0,1:T(8,128)(2,1)} %param.10) | copy-start | bytes 4612
  180.7 22.2 %all-to-all-start.1 = ((bf16[16,6,2560]{2,1,0:T(8,128)(2,1)}), bf16[16,6,2560]{2,1,0:T(8,128)(2,1)S(1)}, u32[]{:S(2)}, u32[]{:S(2)}) async-start(bf16[16,6,2560]{2,1,0:T(8,128)(2,1)} %reshape.62), calls=%async_computation.1 | async-start | bytes 1310720 | tf_op jit(solution)/shard_map/all_to_all | solution.py:98
  186.3 93.2 %reduce-scatter.2.cloned.1.call-start = ((), (), s32[]{:S(2)}) async-start(), calls=%async_computation.7 | async-start | bytes 5898240 | tf_op jit(solution)/shard_map/reduce_scatter | solution.py:119
  226.6 52.9 %copy-start = (bf16[1,384,2560]{2,1,0:T(8,128)(2,1)S(1)}, bf16[1,384,2560]{2,1,0:T(8,128)(2,1)}, u32[]{:S(2)}) copy-start(bf16[1,384,2560]{2,1,0:T(8,128)(2,1)} %param.13) | copy-start | bytes 5898244
Sparse Core Ops, SparseCore 0:
  9.6 56.4 all-gather.3
  67.6 53.7 all-gather.5
  123.0 53.7 all-gather.7
  229.9 49.6 reduce-scatter.1
where the time goes:
time: 294 us
  waiting for transfers between devices  202 us (69%)
  blocking collectives  48.2 us (16%)
  between operations  14 us (5%)
  matrix products  13.7 us (5%)
  other arithmetic  7.77 us (3%)
  starting transfers between devices  5.76 us (2%)
    all_gather x1, waiting for transfers between devices, local(): lax.all_gather(up_weight, 'dp', axis=1, tiled=True)  52 us
    all_gather x1, waiting for transfers between devices, local(): lax.all_gather(down_weight, 'dp', axis=1, tiled=True)  51.9 us
    reduce_scatter x1, waiting for transfers between devices, local(): lax.psum_scatter(lax.dot_general(hidden, arrived_grad, over_tokens, prefe...  49.8 us
    all_gather x1, waiting for transfers between devices, local(): lax.all_gather(gate_weight, 'dp', axis=1, tiled=True)  30.1 us
    all_to_all x1, blocking collectives, local(): lax.all_to_all(outgoing.reshape(experts, capacity, model_width), 'expert'...  25.4 us
    all_to_all x1, blocking collectives, local(): lax.all_to_all(weighted.reshape(experts, capacity, model_width), 'expert'...  22.8 us
    all_to_all x1, waiting for transfers between devices, local(): lax.all_to_all(outputs.reshape(experts, capacity, model_width), 'expert',...  16.5 us
    broadcast_in_dim x1, other arithmetic, local(): return (new_down[None], new_first[None], new_second[None])  7.55 us
  transfers between devices with their start and end apart: 5, of which 5 were waited for; matrix products, arithmetic and copies ran while one was open for 3% of the time, Pallas kernels for 0%

commit v1 on v0

--- a/solution.py
+++ b/solution.py
@@ -55,7 +55,7 @@
     )
 
 
-def local(
+def slot_plan(
     tokens,
     expert_ids,
     gate_values,
@@ -130,6 +130,81 @@
     return (new_down[None], new_first[None], new_second[None])
 
 
+AXES = ("dp", "expert")
+CORE = (1,)
+PLANE = (2, 16, 18)
+LINE = (4, 8, 12)
+
+
+def swap(block, mask):
+    count = lax.axis_size(AXES)
+    return lax.ppermute(block, AXES, [(i, i ^ mask) for i in range(count)])
+
+
+def spread(block):
+    for masks in (LINE, PLANE, CORE):
+        block = jnp.concatenate([block] + [swap(block, mask) for mask in masks], axis=0)
+    return block
+
+
+def collect(terms):
+    total = terms
+    for masks in (CORE, PLANE, LINE):
+        parts = jnp.split(total.astype(jnp.bfloat16), len(masks) + 1, axis=0)
+        own = jnp.split(total, len(masks) + 1, axis=0)[0].astype(jnp.float32)
+        for part, mask in zip(parts[1:], masks):
+            own = own + swap(part, mask).astype(jnp.float32)
+        total = own
+    return total
+
+
+def dense_plan(
+    tokens,
+    expert_ids,
+    gate_values,
+    gate_weight,
+    up_weight,
+    down_weight,
+    first_moment,
+    second_moment,
+):
+    experts = lax.axis_size("expert")
+    width = tokens.shape[1]
+    hot_rows = experts * 3 // 4
+    numbers = jnp.arange(experts, dtype=jnp.int32)
+    matches = expert_ids[:, :, None] == numbers
+    gates = jnp.sum(jnp.where(matches, gate_values[:, :, None], 0), axis=1)
+    hot = jnp.any(expert_ids < experts, axis=1).astype(jnp.int32)
+    rank = jnp.cumsum(hot) - hot
+    place = jnp.arange(hot_rows, dtype=jnp.int32)
+    pick = ((rank[None, :] == place[:, None]) & (hot[None, :] == 1)).astype(jnp.bfloat16)
+    hot_tokens = jnp.dot(pick, tokens, preferred_element_type=jnp.float32).astype(jnp.bfloat16)
+    hot_gates = jnp.dot(pick, gates, preferred_element_type=jnp.float32).astype(jnp.bfloat16)
+    hot_gates = jnp.pad(hot_gates, ((0, 0), (0, 128 - experts)))
+    packed = spread(jnp.concatenate([hot_tokens, hot_gates], axis=1))
+    rows = packed[:, :width]
+    mine = numbers == lax.axis_index("expert")
+    gate = jnp.sum(
+        jnp.where(mine, packed[:, width : width + experts].astype(jnp.float32), 0.0),
+        axis=1,
+        keepdims=True,
+    )
+    contract = (((1,), (1,)), ((), ()))
+    gate_part = lax.dot_general(rows, gate_weight[0], contract, preferred_element_type=jnp.float32)
+    up_part = lax.dot_general(rows, up_weight[0], contract, preferred_element_type=jnp.float32)
+    hidden = (gate * (jax.nn.silu(gate_part) * up_part)).astype(jnp.bfloat16)
+    terms = jnp.dot(hidden, down_weight[0], preferred_element_type=jnp.float32)
+    mixed = collect(terms)
+    cotangent = jnp.tanh(hot_tokens.astype(jnp.float32) + mixed).astype(jnp.bfloat16)
+    gradient = lax.dot_general(
+        hidden, spread(cotangent), (((0,), (0,)), ((), ())), preferred_element_type=jnp.float32
+    )
+    new_down, new_first, new_second = adam_update(
+        gradient, down_weight[0], first_moment[0], second_moment[0]
+    )
+    return (new_down[None], new_first[None], new_second[None])
+
+
 def solution(mesh):
     in_specs = (
         P(("dp", "expert"), None),
@@ -142,4 +217,6 @@
         P("expert", "dp", None),
     )
     out_specs = (P("expert", "dp", None), P("expert", "dp", None), P("expert", "dp", None))
+    small = mesh.shape["dp"] == 2 and mesh.shape["expert"] == 16
+    local = dense_plan if small else slot_plan
     return jax.shard_map(local, mesh=mesh, in_specs=in_specs, out_specs=out_specs, check_vma=False)

time: 294 us -> 135 us (0.46)
  waiting for transfers between devices: 202 us -> 52.7 us
  blocking collectives: 48.2 us -> 0 us
  local copies, waits for them, and re-layouts: 1.98 us -> 35.7 us
  starting transfers between devices: 5.76 us -> 24.7 us
  between operations: 14 us -> 0.84 us
  other arithmetic: 7.77 us -> 3.51 us
  matrix products: 13.7 us -> 16.7 us
    all_gather x3 -> x0, waiting for transfers between devices: 134 us -> none  [the longest x1 52 us: local(): lax.all_gather(up_weight, 'dp', axis=1, tiled=True)]
    ppermute x0 -> x21, waiting for transfers between devices: none -> 52.7 us  [swap(): return lax.ppermute(block, AXES, [(i, i ^ mask) for i in range(count)])]
    reduce_scatter x1 -> x0, waiting for transfers between devices: 49.8 us -> none  [local(): lax.psum_scatter(lax.dot_general(hidden, arrived_grad, over_tokens, prefe...]
    all_to_all x2 -> x0, blocking collectives: 48.2 us -> none  [the longest x1 25.4 us: local(): lax.all_to_all(outgoing.reshape(experts, capacity, model_width), 'expert'...]
    concatenate x0 -> x4, local copies, waits for them, and re-layouts: none -> 34.3 us  [spread(): jnp.concatenate([block] + [swap(block, mask) for mask in masks], axis=0)]
    ppermute x0 -> x21, starting transfers between devices: none -> 24.7 us  [swap(): return lax.ppermute(block, AXES, [(i, i ^ mask) for i in range(count)])]
    all_to_all x1 -> x0, waiting for transfers between devices: 16.5 us -> none  [local(): lax.all_to_all(outputs.reshape(experts, capacity, model_width), 'expert',...]
    broadcast_in_dim x1 -> x0, other arithmetic: 7.55 us -> none  [local(): return (new_down[None], new_first[None], new_second[None])]
  transfers between devices with their start and end apart: 5 -> 21, of which waited for: 5 -> 18; matrix products, arithmetic and copies ran while one was open for 3% -> 0% of each run, Pallas kernels for 0% -> 0%
where the time goes in v1:
time: 135 us; the launch traced here: 134 us
  waiting for transfers between devices  52.7 us (39%)
  local copies, waits for them, and re-layouts  35.7 us (26%)
  starting transfers between devices  24.7 us (18%)
  matrix products  16.7 us (12%)
  other arithmetic  3.51 us (3%)
    ppermute x21, waiting for transfers between devices, swap(): return lax.ppermute(block, AXES, [(i, i ^ mask) for i in range(count)])  52.7 us
    concatenate x4, local copies, waits for them, and re-layouts, spread(): jnp.concatenate([block] + [swap(block, mask) for mask in masks], axis=0)  34.3 us
    ppermute x21, starting transfers between devices, swap(): return lax.ppermute(block, AXES, [(i, i ^ mask) for i in range(count)])  24.7 us
    dot_general x1, matrix products, dense_plan(): lax.dot_general(hidden, spread(cotangent), (((0,), (0,)), ((), ())), pref...  10 us
    dot_general x1, matrix products, dense_plan(): lax.dot_general(rows, gate_weight[0], contract, preferred_element_type=jn...  2.89 us
  transfers between devices with their start and end apart: 21, of which 18 were waited for; matrix products, arithmetic and copies ran while one was open for 0% of the time, Pallas kernels for 0%

profile of v1, /device:TPU:0, one launch (start us, length us, event | category | flops | bytes accessed | tf_op | source)
XLA Modules:
  0.0 134.1 jit_solution(6100467372815526440)
XLA Ops:
  0.6 0.0 copy-start
  0.6 0.8 compare_reduce_fusion
  1.5 0.7 fusion.22
  2.2 0.1 copy.17
  2.3 0.2 reduce-window.8
  2.5 0.1 reduce.1
  2.6 0.1 convolution_convert_fusion.1
  2.7 1.3 convolution_convert_fusion
  4.1 5.1 %collective-permute-start.2 = (bf16[12,2688]{1,0:T(8,128)(2,1)S(1)}, bf16[12,2688]{1,0:T(8,128)(2,1)S(1)}, u32[]{:S(2)}, u32[]{:S(2)}) collective-permute-start(bf16[12,2688]{1,0:T(8,128)(2,1)S(1)} %pad_maximum_fusion.2), channel_id=1, source_target_pairs={{0,12},{1,13},{2,14},{3,15},{4,8},{5,9},{6,10},{7,11},{8,4},{9,5},... | collective-permute-start | bytes 193544 | tf_op jit(solution)/shard_map/ppermute | solution.py:141
  9.2 0.6 collective-permute-start
  9.8 2.6 %collective-permute-done.2 = bf16[12,2688]{1,0:T(8,128)(2,1)S(1)} collective-permute-done((bf16[12,2688]{1,0:T(8,128)(2,1)S(1)}, bf16[12,2688]{1,0:T(8,128)(2,1)S(1)}, u32[]{:S(2)}, u32[]{:S(2)}) %collective-permute-start.2) | collective-permute-done | bytes 64544 | tf_op jit(solution)/shard_map/ppermute | solution.py:141
  12.4 4.0 %collective-permute-done.1 = bf16[12,2688]{1,0:T(8,128)(2,1)S(1)} collective-permute-done((bf16[12,2688]{1,0:T(8,128)(2,1)S(1)}, bf16[12,2688]{1,0:T(8,128)(2,1)S(1)}, u32[]{:S(2)}, u32[]{:S(2)}) %collective-permute-start.1) | collective-permute-done | bytes 64544 | tf_op jit(solution)/shard_map/ppermute | solution.py:141
  16.4 0.1 pad_maximum_fusion
  16.5 2.5 %collective-permute-start.5 = (bf16[48,2688]{1,0:T(8,128)(2,1)S(1)}, bf16[48,2688]{1,0:T(8,128)(2,1)S(1)}, u32[]{:S(2)}, u32[]{:S(2)}) collective-permute-start(bf16[48,2688]{1,0:T(8,128)(2,1)S(1)} %pad_maximum_fusion), channel_id=1, source_target_pairs={{0,18},{1,19},{2,16},{3,17},{4,22},{5,23},{6,20},{7,21},{8,26},{9,... | collective-permute-start | bytes 774152 | tf_op jit(solution)/shard_map/ppermute | solution.py:141
  19.0 0.5 collective-permute-start.4
  19.5 0.5 collective-permute-start.3
  20.0 6.6 %collective-permute-done.5 = bf16[48,2688]{1,0:T(8,128)(2,1)S(1)} collective-permute-done((bf16[48,2688]{1,0:T(8,128)(2,1)S(1)}, bf16[48,2688]{1,0:T(8,128)(2,1)S(1)}, u32[]{:S(2)}, u32[]{:S(2)}) %collective-permute-start.5) | collective-permute-done | bytes 258080 | tf_op jit(solution)/shard_map/ppermute | solution.py:141
  26.6 3.7 %collective-permute-done.4 = bf16[48,2688]{1,0:T(8,128)(2,1)S(1)} collective-permute-done((bf16[48,2688]{1,0:T(8,128)(2,1)S(1)}, bf16[48,2688]{1,0:T(8,128)(2,1)S(1)}, u32[]{:S(2)}, u32[]{:S(2)}) %collective-permute-start.4) | collective-permute-done | bytes 258080 | tf_op jit(solution)/shard_map/ppermute | solution.py:141
  30.3 0.2 collective-permute-done.3
  30.5 6.6 %concatenate.27 = bf16[192,2688]{1,0:T(8,128)(2,1)} concatenate(bf16[12,2688]{1,0:T(8,128)(2,1)S(1)} %pad_maximum_fusion.2, bf16[12,2688]{1,0:T(8,128)(2,1)S(1)} %collective-permute-done, bf16[12,2688]{1,0:T(8,128)(2,1)S(1)} %collective-permute-done.1, bf16[12,2688]{1,0:T(8,128)(2,1)S(1)} %collective-permute-done.2, bf16[48,2688]{1,0:T(8,128)(2,1)S(1)} %collective-permute-done.3, ...), dimensions={0} | concatenate | bytes 2064384 | tf_op jit(solution)/shard_map/concatenate | solution.py:146
  37.2 3.0 %collective-permute-done.6 = bf16[192,2688]{1,0:T(8,128)(2,1)} collective-permute-done((bf16[192,2688]{1,0:T(8,128)(2,1)}, bf16[192,2688]{1,0:T(8,128)(2,1)}, u32[]{:S(2)}, u32[]{:S(2)}) %collective-permute-start.6) | collective-permute-done | bytes 1032224 | tf_op jit(solution)/shard_map/ppermute | solution.py:141
  40.1 11.8 %concatenate.28 = bf16[384,2688]{1,0:T(8,128)(2,1)} concatenate(bf16[12,2688]{1,0:T(8,128)(2,1)S(1)} %pad_maximum_fusion.2, bf16[12,2688]{1,0:T(8,128)(2,1)S(1)} %collective-permute-done, bf16[12,2688]{1,0:T(8,128)(2,1)S(1)} %collective-permute-done.1, bf16[12,2688]{1,0:T(8,128)(2,1)S(1)} %collective-permute-done.2, bf16[48,2688]{1,0:T(8,128)(2,1)S(1)} %collective-permute-done.3, ...), dimensions={0} | concatenate | bytes 4128768 | tf_op jit(solution)/shard_map/concatenate | solution.py:146
  51.9 1.0 select_reduce_fusion
  52.9 0.0 copy-start.6
  52.9 2.9 %fusion.7 = f32[384,384]{1,0:T(8,128)S(1)} fusion(bf16[1,384,2560]{2,1,0:T(8,128)(2,1)S(1)} %copy-done, bf16[384,2688]{1,0:T(8,128)(2,1)} %concatenate.28), kind=kOutput, calls=%fused_computation.13 | convolution fusion | flops 754974720 | bytes 4521984 | tf_op jit(solution)/shard_map/dot_general | solution.py:193
  55.8 0.0 copy-start.2
  55.9 1.2 multiply_convert_fusion
  57.1 0.3 copy-done.2
  57.4 1.2 fusion.9
  58.6 0.1 split.68
  58.7 0.2 collective-permute-start.7
  58.9 2.4 %collective-permute-done.7 = bf16[192,2560]{1,0:T(8,128)(2,1)S(1)} collective-permute-done((bf16[192,2560]{1,0:T(8,128)(2,1)S(1)}, bf16[192,2560]{1,0:T(8,128)(2,1)S(1)}, u32[]{:S(2)}, u32[]{:S(2)}) %collective-permute-start.7) | collective-permute-done | bytes 983072 | tf_op jit(solution)/shard_map/ppermute | solution.py:141
  61.3 0.3 fusion.32
  61.6 0.1 fusion.33
  61.7 1.5 %collective-permute-start.8 = (bf16[48,2560]{1,0:T(8,128)(2,1)S(1)}, bf16[48,2560]{1,0:T(8,128)(2,1)S(1)}, u32[]{:S(2)}, u32[]{:S(2)}) collective-permute-start(bf16[48,2560]{1,0:T(8,128)(2,1)S(1)} %get-tuple-element.10), channel_id=1, source_target_pairs={{0,2},{1,3},{2,0},{3,1},{4,6},{5,7},{6,4},{7,5},{8,10},{9,11},{10,... | collective-permute-start | bytes 737288 | tf_op jit(solution)/shard_map/ppermute | solution.py:141
  63.2 1.4 %collective-permute-start.10 = (bf16[48,2560]{1,0:T(8,128)(2,1)S(1)}, bf16[48,2560]{1,0:T(8,128)(2,1)S(1)}, u32[]{:S(2)}, u32[]{:S(2)}) collective-permute-start(bf16[48,2560]{1,0:T(8,128)(2,1)S(1)} %get-tuple-element.11), channel_id=1, source_target_pairs={{0,18},{1,19},{2,16},{3,17},{4,22},{5,23},{6,20},{7,21},{8,26},{9,... | collective-permute-start | bytes 737288 | tf_op jit(solution)/shard_map/ppermute | solution.py:141
  64.6 0.6 collective-permute-start.9
  65.2 5.3 %collective-permute-done.8 = bf16[48,2560]{1,0:T(8,128)(2,1)S(1)} collective-permute-done((bf16[48,2560]{1,0:T(8,128)(2,1)S(1)}, bf16[48,2560]{1,0:T(8,128)(2,1)S(1)}, u32[]{:S(2)}, u32[]{:S(2)}) %collective-permute-start.8) | collective-permute-done | bytes 245792 | tf_op jit(solution)/shard_map/ppermute | solution.py:141
  70.5 5.4 %collective-permute-done.10 = bf16[48,2560]{1,0:T(8,128)(2,1)S(1)} collective-permute-done((bf16[48,2560]{1,0:T(8,128)(2,1)S(1)}, bf16[48,2560]{1,0:T(8,128)(2,1)S(1)}, u32[]{:S(2)}, u32[]{:S(2)}) %collective-permute-start.10) | collective-permute-done | bytes 245792 | tf_op jit(solution)/shard_map/ppermute | solution.py:141
  76.0 1.4 %collective-permute-done.9 = bf16[48,2560]{1,0:T(8,128)(2,1)S(1)} collective-permute-done((bf16[48,2560]{1,0:T(8,128)(2,1)S(1)}, bf16[48,2560]{1,0:T(8,128)(2,1)S(1)}, u32[]{:S(2)}, u32[]{:S(2)}) %collective-permute-start.9) | collective-permute-done | bytes 245792 | tf_op jit(solution)/shard_map/ppermute | solution.py:141
  77.3 0.1 fusion.30
  77.5 0.4 collective-permute-start.11
  77.9 2.0 %collective-permute-start.13 = (bf16[12,2560]{1,0:T(8,128)(2,1)S(1)}, bf16[12,2560]{1,0:T(8,128)(2,1)S(1)}, u32[]{:S(2)}, u32[]{:S(2)}) collective-permute-start(bf16[12,2560]{1,0:T(8,128)(2,1)S(1)} %get-tuple-element.14), channel_id=1, source_target_pairs={{0,12},{1,13},{2,14},{3,15},{4,8},{5,9},{6,10},{7,11},{8,4},{9,5},... | collective-permute-start | bytes 184328 | tf_op jit(solution)/shard_map/ppermute | solution.py:141
  79.8 1.2 collective-permute-start.12
  81.1 1.7 %collective-permute-done.11 = bf16[12,2560]{1,0:T(8,128)(2,1)S(1)} collective-permute-done((bf16[12,2560]{1,0:T(8,128)(2,1)S(1)}, bf16[12,2560]{1,0:T(8,128)(2,1)S(1)}, u32[]{:S(2)}, u32[]{:S(2)}) %collective-permute-start.11) | collective-permute-done | bytes 61472 | tf_op jit(solution)/shard_map/ppermute | solution.py:141
  82.7 1.5 %collective-permute-done.13 = bf16[12,2560]{1,0:T(8,128)(2,1)S(1)} collective-permute-done((bf16[12,2560]{1,0:T(8,128)(2,1)S(1)}, bf16[12,2560]{1,0:T(8,128)(2,1)S(1)}, u32[]{:S(2)}, u32[]{:S(2)}) %collective-permute-start.13) | collective-permute-done | bytes 61472 | tf_op jit(solution)/shard_map/ppermute | solution.py:141
  84.2 2.5 %collective-permute-done.12 = bf16[12,2560]{1,0:T(8,128)(2,1)S(1)} collective-permute-done((bf16[12,2560]{1,0:T(8,128)(2,1)S(1)}, bf16[12,2560]{1,0:T(8,128)(2,1)S(1)}, u32[]{:S(2)}, u32[]{:S(2)}) %collective-permute-start.12) | collective-permute-done | bytes 61472 | tf_op jit(solution)/shard_map/ppermute | solution.py:141
  86.7 0.1 fusion.20
  86.8 2.7 %collective-permute-start.16 = (bf16[12,2560]{1,0:T(8,128)(2,1)S(1)}, bf16[12,2560]{1,0:T(8,128)(2,1)S(1)}, u32[]{:S(2)}, u32[]{:S(2)}) collective-permute-start(bf16[12,2560]{1,0:T(8,128)(2,1)S(1)} %fusion.20), channel_id=1, source_target_pairs={{0,12},{1,13},{2,14},{3,15},{4,8},{5,9},{6,10},{7,11},{8,4},{9,5},... | collective-permute-start | bytes 184328 | tf_op jit(solution)/shard_map/ppermute | solution.py:141
  89.5 1.8 %collective-permute-start.14 = (bf16[12,2560]{1,0:T(8,128)(2,1)S(1)}, bf16[12,2560]{1,0:T(8,128)(2,1)S(1)}, u32[]{:S(2)}, u32[]{:S(2)}) collective-permute-start(bf16[12,2560]{1,0:T(8,128)(2,1)S(1)} %fusion.20), channel_id=1, source_target_pairs={{0,4},{1,5},{2,6},{3,7},{4,0},{5,1},{6,2},{7,3},{8,12},{9,13},{10,... | collective-permute-start | bytes 184328 | tf_op jit(solution)/shard_map/ppermute | solution.py:141
  91.2 1.9 %collective-permute-done.16 = bf16[12,2560]{1,0:T(8,128)(2,1)S(1)} collective-permute-done((bf16[12,2560]{1,0:T(8,128)(2,1)S(1)}, bf16[12,2560]{1,0:T(8,128)(2,1)S(1)}, u32[]{:S(2)}, u32[]{:S(2)}) %collective-permute-start.16) | collective-permute-done | bytes 61472 | tf_op jit(solution)/shard_map/ppermute | solution.py:141
  93.1 1.8 %collective-permute-done.15 = bf16[12,2560]{1,0:T(8,128)(2,1)S(1)} collective-permute-done((bf16[12,2560]{1,0:T(8,128)(2,1)S(1)}, bf16[12,2560]{1,0:T(8,128)(2,1)S(1)}, u32[]{:S(2)}, u32[]{:S(2)}) %collective-permute-start.15) | collective-permute-done | bytes 61472 | tf_op jit(solution)/shard_map/ppermute | solution.py:141
  94.8 0.1 pad_maximum_fusion.1
  94.9 1.6 %collective-permute-start.19 = (bf16[48,2560]{1,0:T(8,128)(2,1)S(1)}, bf16[48,2560]{1,0:T(8,128)(2,1)S(1)}, u32[]{:S(2)}, u32[]{:S(2)}) collective-permute-start(bf16[48,2560]{1,0:T(8,128)(2,1)S(1)} %pad_maximum_fusion.1), channel_id=1, source_target_pairs={{0,18},{1,19},{2,16},{3,17},{4,22},{5,23},{6,20},{7,21},{8,26},{9,... | collective-permute-start | bytes 737288 | tf_op jit(solution)/shard_map/ppermute | solution.py:141
  96.5 0.7 collective-permute-start.18
  97.2 1.3 collective-permute-start.17
  98.5 3.7 %collective-permute-done.19 = bf16[48,2560]{1,0:T(8,128)(2,1)S(1)} collective-permute-done((bf16[48,2560]{1,0:T(8,128)(2,1)S(1)}, bf16[48,2560]{1,0:T(8,128)(2,1)S(1)}, u32[]{:S(2)}, u32[]{:S(2)}) %collective-permute-start.19) | collective-permute-done | bytes 245792 | tf_op jit(solution)/shard_map/ppermute | solution.py:141
  102.2 2.5 %collective-permute-done.18 = bf16[48,2560]{1,0:T(8,128)(2,1)S(1)} collective-permute-done((bf16[48,2560]{1,0:T(8,128)(2,1)S(1)}, bf16[48,2560]{1,0:T(8,128)(2,1)S(1)}, u32[]{:S(2)}, u32[]{:S(2)}) %collective-permute-start.18) | collective-permute-done | bytes 245792 | tf_op jit(solution)/shard_map/ppermute | solution.py:141
  104.7 0.7 copy-done.3
  105.4 2.5 %concatenate.30 = bf16[192,2560]{1,0:T(8,128)(2,1)S(1)} concatenate(bf16[12,2560]{1,0:T(8,128)(2,1)S(1)} %fusion.20, bf16[12,2560]{1,0:T(8,128)(2,1)S(1)} %collective-permute-done.14, bf16[12,2560]{1,0:T(8,128)(2,1)S(1)} %collective-permute-done.15, bf16[12,2560]{1,0:T(8,128)(2,1)S(1)} %collective-permute-done.16, bf16[48,2560]{1,0:T(8,128)(2,1)} %collective-permute-done.17, ...), dimensions={0} | concatenate | bytes 1966080 | tf_op jit(solution)/shard_map/concatenate | solution.py:146
  107.9 0.1 collective-permute-start.20
  108.0 2.7 %collective-permute-done.20 = bf16[192,2560]{1,0:T(8,128)(2,1)} collective-permute-done((bf16[192,2560]{1,0:T(8,128)(2,1)S(1)}, bf16[192,2560]{1,0:T(8,128)(2,1)}, u32[]{:S(2)}, u32[]{:S(2)}) %collective-permute-start.20) | collective-permute-done | bytes 983072 | tf_op jit(solution)/shard_map/ppermute | solution.py:141
  110.7 13.4 %concatenate.31 = bf16[384,2560]{1,0:T(8,128)(2,1)} concatenate(bf16[12,2560]{1,0:T(8,128)(2,1)S(1)} %fusion.20, bf16[12,2560]{1,0:T(8,128)(2,1)S(1)} %collective-permute-done.14, bf16[12,2560]{1,0:T(8,128)(2,1)S(1)} %collective-permute-done.15, bf16[12,2560]{1,0:T(8,128)(2,1)S(1)} %collective-permute-done.16, bf16[48,2560]{1,0:T(8,128)(2,1)} %collective-permute-done.17, ...), dimensions={0} | concatenate | bytes 3932160 | tf_op jit(solution)/shard_map/concatenate | solution.py:146
  124.1 10.0 %fusion.3 = (bf16[1,384,2560]{2,1,0:T(8,128)(2,1)}, bf16[1,384,2560]{2,1,0:T(8,128)(2,1)}, bf16[1,384,2560]{2,1,0:T(8,128)(2,1)}) fusion(bf16[1,384,2560]{2,1,0:T(8,128)(2,1)} %param.15, bf16[1,384,2560]{2,1,0:T(8,128)(2,1)} %param.14, bf16[1,384,2560]{2,1,0:T(8,128)(2,1)} %param.13, bf16[384,384]{1,0:T(8,128)(2,1)S(1)} %copy-done.5, ...), kind=kOutput, calls=%fused_computation.7 | convolution fusion | flops 773652480 | bytes 14057472 | tf_op jit(solution)/shard_map/dot_general | solution.py:199
  (21 shorter events, 0.1 us)
Async XLA Ops:
  0.6 52.3 %copy-start = (bf16[1,384,2560]{2,1,0:T(8,128)(2,1)S(1)}, bf16[1,384,2560]{2,1,0:T(8,128)(2,1)}, u32[]{:S(2)}) copy-start(bf16[1,384,2560]{2,1,0:T(8,128)(2,1)} %param.11) | copy-start | bytes 5898244
  4.1 8.3 %collective-permute-start.2 = (bf16[12,2688]{1,0:T(8,128)(2,1)S(1)}, bf16[12,2688]{1,0:T(8,128)(2,1)S(1)}, u32[]{:S(2)}, u32[]{:S(2)}) collective-permute-start(bf16[12,2688]{1,0:T(8,128)(2,1)S(1)} %pad_maximum_fusion.2), channel_id=1, source_target_pairs={{0,12},{1,13},{2,14},{3,15},{4,8},{5,9},{6,10},{7,11},{8,4},{9,5},... | collective-permute-start | bytes 193544 | tf_op jit(solution)/shard_map/ppermute | solution.py:141
  9.2 7.2 %collective-permute-start.1 = (bf16[12,2688]{1,0:T(8,128)(2,1)S(1)}, bf16[12,2688]{1,0:T(8,128)(2,1)S(1)}, u32[]{:S(2)}, u32[]{:S(2)}) collective-permute-start(bf16[12,2688]{1,0:T(8,128)(2,1)S(1)} %pad_maximum_fusion.2), channel_id=1, source_target_pairs={{0,8},{1,9},{2,10},{3,11},{4,12},{5,13},{6,14},{7,15},{8,0},{9,1},... | collective-permute-start | bytes 193544 | tf_op jit(solution)/shard_map/ppermute | solution.py:141
  9.2 7.2 %collective-permute-start = (bf16[12,2688]{1,0:T(8,128)(2,1)S(1)}, bf16[12,2688]{1,0:T(8,128)(2,1)S(1)}, u32[]{:S(2)}, u32[]{:S(2)}) collective-permute-start(bf16[12,2688]{1,0:T(8,128)(2,1)S(1)} %pad_maximum_fusion.2), channel_id=1, source_target_pairs={{0,4},{1,5},{2,6},{3,7},{4,0},{5,1},{6,2},{7,3},{8,12},{9,13},{10,... | collective-permute-start | bytes 193544 | tf_op jit(solution)/shard_map/ppermute | solution.py:141
  16.5 10.2 %collective-permute-start.5 = (bf16[48,2688]{1,0:T(8,128)(2,1)S(1)}, bf16[48,2688]{1,0:T(8,128)(2,1)S(1)}, u32[]{:S(2)}, u32[]{:S(2)}) collective-permute-start(bf16[48,2688]{1,0:T(8,128)(2,1)S(1)} %pad_maximum_fusion), channel_id=1, source_target_pairs={{0,18},{1,19},{2,16},{3,17},{4,22},{5,23},{6,20},{7,21},{8,26},{9,... | collective-permute-start | bytes 774152 | tf_op jit(solution)/shard_map/ppermute | solution.py:141
  19.0 11.3 %collective-permute-start.4 = (bf16[48,2688]{1,0:T(8,128)(2,1)S(1)}, bf16[48,2688]{1,0:T(8,128)(2,1)S(1)}, u32[]{:S(2)}, u32[]{:S(2)}) collective-permute-start(bf16[48,2688]{1,0:T(8,128)(2,1)S(1)} %pad_maximum_fusion), channel_id=1, source_target_pairs={{0,16},{1,17},{2,18},{3,19},{4,20},{5,21},{6,22},{7,23},{8,24},{9,... | collective-permute-start | bytes 774152 | tf_op jit(solution)/shard_map/ppermute | solution.py:141
  19.5 11.0 %collective-permute-start.3 = (bf16[48,2688]{1,0:T(8,128)(2,1)S(1)}, bf16[48,2688]{1,0:T(8,128)(2,1)S(1)}, u32[]{:S(2)}, u32[]{:S(2)}) collective-permute-start(bf16[48,2688]{1,0:T(8,128)(2,1)S(1)} %pad_maximum_fusion), channel_id=1, source_target_pairs={{0,2},{1,3},{2,0},{3,1},{4,6},{5,7},{6,4},{7,5},{8,10},{9,11},{10,... | collective-permute-start | bytes 774152 | tf_op jit(solution)/shard_map/ppermute | solution.py:141
  37.1 3.0 %collective-permute-start.6 = (bf16[192,2688]{1,0:T(8,128)(2,1)}, bf16[192,2688]{1,0:T(8,128)(2,1)}, u32[]{:S(2)}, u32[]{:S(2)}) collective-permute-start(bf16[192,2688]{1,0:T(8,128)(2,1)} %concatenate.27), channel_id=1, source_target_pairs={{0,1},{1,0},{2,3},{3,2},{4,5},{5,4},{6,7},{7,6},{8,9},{9,8},{10,11... | collective-permute-start | bytes 3096584 | tf_op jit(solution)/shard_map/ppermute | solution.py:141
  52.9 2.9 %copy-start.1 = (bf16[384,2688]{1,0:T(8,128)(2,1)S(1)}, bf16[384,2688]{1,0:T(8,128)(2,1)}, u32[]{:S(2)}) copy-start(bf16[384,2688]{1,0:T(8,128)(2,1)} %concatenate.28) | copy-start | bytes 6193156
  52.9 2.9 %copy-start.6 = (bf16[1,384,2560]{2,1,0:T(8,128)(2,1)S(1)}, bf16[1,384,2560]{2,1,0:T(8,128)(2,1)}, u32[]{:S(2)}) copy-start(bf16[1,384,2560]{2,1,0:T(8,128)(2,1)} %param.12) | copy-start | bytes 5898244
  55.8 1.5 %copy-start.2 = (bf16[1,384,2560]{2,1,0:T(8,128)(2,1)S(1)}, bf16[1,384,2560]{2,1,0:T(8,128)(2,1)}, u32[]{:S(2)}) copy-start(bf16[1,384,2560]{2,1,0:T(8,128)(2,1)} %param.13) | copy-start | bytes 5898244
  57.4 1.2 copy-start.4
  58.7 2.6 %collective-permute-start.7 = (bf16[192,2560]{1,0:T(8,128)(2,1)S(1)}, bf16[192,2560]{1,0:T(8,128)(2,1)S(1)}, u32[]{:S(2)}, u32[]{:S(2)}) collective-permute-start(bf16[192,2560]{1,0:T(8,128)(2,1)S(1)} %split.68), channel_id=1, source_target_pairs={{0,1},{1,0},{2,3},{3,2},{4,5},{5,4},{6,7},{7,6},{8,9},{9,8},{10,11... | collective-permute-start | bytes 2949128 | tf_op jit(solution)/shard_map/ppermute | solution.py:141
  61.7 8.9 %collective-permute-start.8 = (bf16[48,2560]{1,0:T(8,128)(2,1)S(1)}, bf16[48,2560]{1,0:T(8,128)(2,1)S(1)}, u32[]{:S(2)}, u32[]{:S(2)}) collective-permute-start(bf16[48,2560]{1,0:T(8,128)(2,1)S(1)} %get-tuple-element.10), channel_id=1, source_target_pairs={{0,2},{1,3},{2,0},{3,1},{4,6},{5,7},{6,4},{7,5},{8,10},{9,11},{10,... | collective-permute-start | bytes 737288 | tf_op jit(solution)/shard_map/ppermute | solution.py:141
  63.2 12.7 %collective-permute-start.10 = (bf16[48,2560]{1,0:T(8,128)(2,1)S(1)}, bf16[48,2560]{1,0:T(8,128)(2,1)S(1)}, u32[]{:S(2)}, u32[]{:S(2)}) collective-permute-start(bf16[48,2560]{1,0:T(8,128)(2,1)S(1)} %get-tuple-element.11), channel_id=1, source_target_pairs={{0,18},{1,19},{2,16},{3,17},{4,22},{5,23},{6,20},{7,21},{8,26},{9,... | collective-permute-start | bytes 737288 | tf_op jit(solution)/shard_map/ppermute | solution.py:141
  64.6 12.7 %collective-permute-start.9 = (bf16[48,2560]{1,0:T(8,128)(2,1)S(1)}, bf16[48,2560]{1,0:T(8,128)(2,1)S(1)}, u32[]{:S(2)}, u32[]{:S(2)}) collective-permute-start(bf16[48,2560]{1,0:T(8,128)(2,1)S(1)} %get-tuple-element.12), channel_id=1, source_target_pairs={{0,16},{1,17},{2,18},{3,19},{4,20},{5,21},{6,22},{7,23},{8,24},{9,... | collective-permute-start | bytes 737288 | tf_op jit(solution)/shard_map/ppermute | solution.py:141
  77.5 5.2 %collective-permute-start.11 = (bf16[12,2560]{1,0:T(8,128)(2,1)S(1)}, bf16[12,2560]{1,0:T(8,128)(2,1)S(1)}, u32[]{:S(2)}, u32[]{:S(2)}) collective-permute-start(bf16[12,2560]{1,0:T(8,128)(2,1)S(1)} %get-tuple-element.13), channel_id=1, source_target_pairs={{0,4},{1,5},{2,6},{3,7},{4,0},{5,1},{6,2},{7,3},{8,12},{9,13},{10,... | collective-permute-start | bytes 184328 | tf_op jit(solution)/shard_map/ppermute | solution.py:141
  77.9 6.3 %collective-permute-start.13 = (bf16[12,2560]{1,0:T(8,128)(2,1)S(1)}, bf16[12,2560]{1,0:T(8,128)(2,1)S(1)}, u32[]{:S(2)}, u32[]{:S(2)}) collective-permute-start(bf16[12,2560]{1,0:T(8,128)(2,1)S(1)} %get-tuple-element.14), channel_id=1, source_target_pairs={{0,12},{1,13},{2,14},{3,15},{4,8},{5,9},{6,10},{7,11},{8,4},{9,5},... | collective-permute-start | bytes 184328 | tf_op jit(solution)/shard_map/ppermute | solution.py:141
  79.8 6.9 %collective-permute-start.12 = (bf16[12,2560]{1,0:T(8,128)(2,1)S(1)}, bf16[12,2560]{1,0:T(8,128)(2,1)S(1)}, u32[]{:S(2)}, u32[]{:S(2)}) collective-permute-start(bf16[12,2560]{1,0:T(8,128)(2,1)S(1)} %get-tuple-element.15), channel_id=1, source_target_pairs={{0,8},{1,9},{2,10},{3,11},{4,12},{5,13},{6,14},{7,15},{8,0},{9,1},... | collective-permute-start | bytes 184328 | tf_op jit(solution)/shard_map/ppermute | solution.py:141
  86.8 6.3 %collective-permute-start.16 = (bf16[12,2560]{1,0:T(8,128)(2,1)S(1)}, bf16[12,2560]{1,0:T(8,128)(2,1)S(1)}, u32[]{:S(2)}, u32[]{:S(2)}) collective-permute-start(bf16[12,2560]{1,0:T(8,128)(2,1)S(1)} %fusion.20), channel_id=1, source_target_pairs={{0,12},{1,13},{2,14},{3,15},{4,8},{5,9},{6,10},{7,11},{8,4},{9,5},... | collective-permute-start | bytes 184328 | tf_op jit(solution)/shard_map/ppermute | solution.py:141
  89.5 5.4 %collective-permute-start.15 = (bf16[12,2560]{1,0:T(8,128)(2,1)S(1)}, bf16[12,2560]{1,0:T(8,128)(2,1)S(1)}, u32[]{:S(2)}, u32[]{:S(2)}) collective-permute-start(bf16[12,2560]{1,0:T(8,128)(2,1)S(1)} %fusion.20), channel_id=1, source_target_pairs={{0,8},{1,9},{2,10},{3,11},{4,12},{5,13},{6,14},{7,15},{8,0},{9,1},... | collective-permute-start | bytes 184328 | tf_op jit(solution)/shard_map/ppermute | solution.py:141
  89.5 5.4 %collective-permute-start.14 = (bf16[12,2560]{1,0:T(8,128)(2,1)S(1)}, bf16[12,2560]{1,0:T(8,128)(2,1)S(1)}, u32[]{:S(2)}, u32[]{:S(2)}) collective-permute-start(bf16[12,2560]{1,0:T(8,128)(2,1)S(1)} %fusion.20), channel_id=1, source_target_pairs={{0,4},{1,5},{2,6},{3,7},{4,0},{5,1},{6,2},{7,3},{8,12},{9,13},{10,... | collective-permute-start | bytes 184328 | tf_op jit(solution)/shard_map/ppermute | solution.py:141
  94.9 7.3 %collective-permute-start.19 = (bf16[48,2560]{1,0:T(8,128)(2,1)S(1)}, bf16[48,2560]{1,0:T(8,128)(2,1)S(1)}, u32[]{:S(2)}, u32[]{:S(2)}) collective-permute-start(bf16[48,2560]{1,0:T(8,128)(2,1)S(1)} %pad_maximum_fusion.1), channel_id=1, source_target_pairs={{0,18},{1,19},{2,16},{3,17},{4,22},{5,23},{6,20},{7,21},{8,26},{9,... | collective-permute-start | bytes 737288 | tf_op jit(solution)/shard_map/ppermute | solution.py:141
  96.5 8.2 %collective-permute-start.18 = (bf16[48,2560]{1,0:T(8,128)(2,1)S(1)}, bf16[48,2560]{1,0:T(8,128)(2,1)S(1)}, u32[]{:S(2)}, u32[]{:S(2)}) collective-permute-start(bf16[48,2560]{1,0:T(8,128)(2,1)S(1)} %pad_maximum_fusion.1), channel_id=1, source_target_pairs={{0,16},{1,17},{2,18},{3,19},{4,20},{5,21},{6,22},{7,23},{8,24},{9,... | collective-permute-start | bytes 737288 | tf_op jit(solution)/shard_map/ppermute | solution.py:141
  97.2 8.2 %collective-permute-start.17 = (bf16[48,2560]{1,0:T(8,128)(2,1)S(1)}, bf16[48,2560]{1,0:T(8,128)(2,1)}, u32[]{:S(2)}, u32[]{:S(2)}) collective-permute-start(bf16[48,2560]{1,0:T(8,128)(2,1)S(1)} %pad_maximum_fusion.1), channel_id=1, source_target_pairs={{0,2},{1,3},{2,0},{3,1},{4,6},{5,7},{6,4},{7,5},{8,10},{9,11},{10,... | collective-permute-start | bytes 737288 | tf_op jit(solution)/shard_map/ppermute | solution.py:141
  104.7 0.7 copy-start.3
  107.9 2.8 %collective-permute-start.20 = (bf16[192,2560]{1,0:T(8,128)(2,1)S(1)}, bf16[192,2560]{1,0:T(8,128)(2,1)}, u32[]{:S(2)}, u32[]{:S(2)}) collective-permute-start(bf16[192,2560]{1,0:T(8,128)(2,1)S(1)} %concatenate.30), channel_id=1, source_target_pairs={{0,1},{1,0},{2,3},{3,2},{4,5},{5,4},{6,7},{7,6},{8,9},{9,8},{10,11... | collective-permute-start | bytes 2949128 | tf_op jit(solution)/shard_map/ppermute | solution.py:141
  110.7 13.4 %copy-start.5 = (bf16[384,384]{1,0:T(8,128)(2,1)S(1)}, bf16[384,384]{1,0:T(8,128)(2,1)}, u32[]{:S(2)}) copy-start(bf16[384,384]{1,0:T(8,128)(2,1)} %copy-done.4) | copy-start | bytes 884740

commit v2 on v0

--- a/solution.py
+++ b/solution.py
@@ -1,6 +1,10 @@
+import functools
+
 import jax
 import jax.numpy as jnp
 from jax import lax
+from jax.experimental import pallas as pl
+from jax.experimental.pallas import tpu as pltpu
 from jax.sharding import PartitionSpec as P
 
 CAP = 6
@@ -55,7 +59,7 @@
     )
 
 
-def local(
+def slot_plan(
     tokens,
     expert_ids,
     gate_values,
@@ -130,6 +134,218 @@
     return (new_down[None], new_first[None], new_second[None])
 
 
+AXES = ("dp", "expert")
+CORE = 1
+PLANE = (2, 16, 18)
+LINE = (4, 8, 12)
+CHUNKS = 1
+LANES = 128
+MIB = 1024 * 1024
+
+
+def swap(block, mask):
+    count = lax.axis_size(AXES)
+    return lax.ppermute(block, AXES, [(i, i ^ mask) for i in range(count)])
+
+
+def spread(block):
+    block = jnp.concatenate([block] + [swap(block, mask) for mask in LINE], axis=0)
+    pieces = [block] + [swap(block, mask) for mask in PLANE]
+    return pieces + [swap(piece, CORE) for piece in pieces]
+
+
+def add_parts(own, other_parts):
+    total = own.astype(jnp.float32)
+    for part in other_parts:
+        total = total + part.astype(jnp.float32)
+    return total
+
+
+def collect(own, other):
+    total = add_parts(own, [swap(other, CORE)])
+    for masks in (PLANE, LINE):
+        parts = jnp.split(total, len(masks) + 1, axis=0)
+        sent = [swap(part.astype(jnp.bfloat16), mask) for part, mask in zip(parts[1:], masks)]
+        total = add_parts(parts[0], sent)
+    return total
+
+
+def expert_kernel(chunks, *refs):
+    pieces = refs[: 8 * chunks]
+    gate_ref, up_ref, down_ref, sel_ref = refs[8 * chunks : 8 * chunks + 4]
+    outs = refs[8 * chunks + 4 : 8 * chunks + 4 + 2 * chunks]
+    hidden_t_ref, rows, gates, gate_vm, up_vm, down_vm, sems = refs[8 * chunks + 4 + 2 * chunks :]
+    count, width = rows.shape
+    part = count // 8
+    span = width // chunks
+    copies = []
+    for c in range(chunks):
+        for p in range(8):
+            src = pieces[8 * c + p]
+            sem = sems.at[8 * c + p]
+            if c == 0:
+                copies.append(
+                    pltpu.make_async_copy(
+                        src.at[:, pl.ds(span, LANES)],
+                        gates.at[pl.ds(p * part, part)],
+                        sems.at[8 * chunks + p],
+                    )
+                )
+                src = src.at[:, pl.ds(0, span)]
+            copies.append(
+                pltpu.make_async_copy(
+                    src, rows.at[pl.ds(p * part, part), pl.ds(c * span, span)], sem
+                )
+            )
+    gate_copy = pltpu.make_async_copy(gate_ref, gate_vm, sems.at[8 * chunks + 8])
+    up_copy = pltpu.make_async_copy(up_ref, up_vm, sems.at[8 * chunks + 9])
+    down_copy = pltpu.make_async_copy(down_ref, down_vm, sems.at[8 * chunks + 10])
+    for copy in copies + [gate_copy, up_copy, down_copy]:
+        copy.start()
+    for copy in copies + [gate_copy]:
+        copy.wait()
+    contract = (((1,), (1,)), ((), ()))
+    gate = jnp.sum(gates[...].astype(jnp.float32) * sel_ref[...], axis=1, keepdims=True)
+    gate_part = lax.dot_general(
+        rows[...], gate_vm[...], contract, preferred_element_type=jnp.float32
+    )
+    up_copy.wait()
+    up_part = lax.dot_general(rows[...], up_vm[...], contract, preferred_element_type=jnp.float32)
+    hidden = gate * (jax.nn.silu(gate_part) * up_part)
+    hidden_t_ref[...] = hidden.T.astype(jnp.bfloat16)
+    hidden = hidden.astype(jnp.bfloat16)
+    down_copy.wait()
+    for c in range(chunks):
+        terms = jnp.dot(
+            hidden, down_vm[:, c * span : (c + 1) * span], preferred_element_type=jnp.float32
+        ).astype(jnp.bfloat16)
+        outs[2 * c][...] = terms[: count // 2]
+        outs[2 * c + 1][...] = terms[count // 2 :]
+
+
+def expert_terms(pieces, gate_weight, up_weight, down_weight, sel):
+    chunks = len(pieces)
+    part = pieces[0][0].shape[0]
+    units, width = gate_weight.shape
+    count = 8 * part
+    span = width // chunks
+    flat = [piece for chunk in pieces for piece in chunk]
+    half = jax.ShapeDtypeStruct((count // 2, span), jnp.bfloat16)
+    anywhere = pl.BlockSpec(memory_space=pl.ANY)
+    in_vmem = pl.BlockSpec(memory_space=pltpu.VMEM)
+    outs = pl.pallas_call(
+        functools.partial(expert_kernel, chunks),
+        out_shape=[half] * (2 * chunks) + [jax.ShapeDtypeStruct((units, count), jnp.bfloat16)],
+        in_specs=[anywhere] * (len(flat) + 3) + [in_vmem],
+        out_specs=[in_vmem] * (2 * chunks + 1),
+        scratch_shapes=[
+            pltpu.VMEM((count, width), jnp.bfloat16),
+            pltpu.VMEM((count, LANES), jnp.bfloat16),
+            pltpu.VMEM((units, width), jnp.bfloat16),
+            pltpu.VMEM((units, width), jnp.bfloat16),
+            pltpu.VMEM((units, width), jnp.bfloat16),
+            pltpu.SemaphoreType.DMA((8 * chunks + 11,)),
+        ],
+        compiler_params=pltpu.CompilerParams(vmem_limit_bytes=36 * MIB),
+        cost_estimate=pl.CostEstimate(
+            flops=6 * count * units * width,
+            bytes_accessed=10 * count * width,
+            transcendentals=count * units,
+        ),
+        name="expert_terms",
+    )(*flat, gate_weight, up_weight, down_weight, sel)
+    return outs[:-1], outs[-1]
+
+
+def update_kernel(*refs):
+    pieces = refs[:8]
+    hidden_t_ref, down_ref, first_ref, second_ref = refs[8:12]
+    new_down_ref, new_first_ref, new_second_ref = refs[-3:]
+    cotangent = jnp.concatenate([piece[...] for piece in pieces], axis=0)
+    gradient = jnp.dot(hidden_t_ref[...], cotangent, preferred_element_type=jnp.float32)
+    new_down, new_first, new_second = adam_update(
+        gradient, down_ref[...], first_ref[...], second_ref[...]
+    )
+    new_down_ref[...] = new_down
+    new_first_ref[...] = new_first
+    new_second_ref[...] = new_second
+
+
+def update(pieces, hidden_t, down_weight, first_moment, second_moment, chunk, chunks, olds):
+    units, width = down_weight.shape
+    part = pieces[0].shape[0]
+    block = 256
+    steps = width // chunks // block
+    state = pl.BlockSpec((units, block), lambda i: (0, i + chunk * steps))
+    in_specs = [pl.BlockSpec((part, block), lambda i: (0, i))] * 8
+    in_specs += [pl.BlockSpec(hidden_t.shape, lambda i: (0, 0))] + [state] * 3
+    in_specs += [pl.BlockSpec(memory_space=pl.ANY)] * len(olds)
+    return pl.pallas_call(
+        update_kernel,
+        grid=(steps,),
+        out_shape=[jax.ShapeDtypeStruct((units, width), jnp.bfloat16)] * 3,
+        in_specs=in_specs,
+        out_specs=[state] * 3,
+        input_output_aliases={12 + k: k for k in range(len(olds))},
+        compiler_params=pltpu.CompilerParams(vmem_limit_bytes=24 * MIB),
+        cost_estimate=pl.CostEstimate(
+            flops=2 * 8 * part * units * width // chunks,
+            bytes_accessed=14 * units * width // chunks,
+            transcendentals=2 * units * width // chunks,
+        ),
+        name="update",
+    )(*pieces, hidden_t, down_weight, first_moment, second_moment, *olds)
+
+
+def dense_plan(
+    tokens,
+    expert_ids,
+    gate_values,
+    gate_weight,
+    up_weight,
+    down_weight,
+    first_moment,
+    second_moment,
+):
+    experts = lax.axis_size("expert")
+    width = tokens.shape[1]
+    span = width // CHUNKS
+    hot_rows = experts * 3 // 4
+    numbers = jnp.arange(LANES, dtype=jnp.int32)
+    matches = (expert_ids[:, :, None] == numbers) & (numbers < experts)
+    gates = jnp.sum(jnp.where(matches, gate_values[:, :, None], 0), axis=1)
+    hot = jnp.any(expert_ids < experts, axis=1).astype(jnp.int32)
+    rank = jnp.cumsum(hot) - hot
+    place = jnp.arange(hot_rows, dtype=jnp.int32)
+    pick = ((rank[None, :] == place[:, None]) & (hot[None, :] == 1)).astype(jnp.bfloat16)
+    hot_tokens = jnp.dot(pick, tokens, preferred_element_type=jnp.float32).astype(jnp.bfloat16)
+    hot_gates = jnp.dot(pick, gates, preferred_element_type=jnp.float32).astype(jnp.bfloat16)
+    own = [hot_tokens[:, c * span : (c + 1) * span] for c in range(CHUNKS)]
+    sent = [jnp.concatenate([own[0], hot_gates], axis=1)] + own[1:]
+    pieces = [spread(block) for block in sent]
+    sel = (numbers == lax.axis_index("expert")).astype(jnp.float32)[None, :]
+    terms, hidden_t = expert_terms(pieces, gate_weight[0], up_weight[0], down_weight[0], sel)
+    cotangents = []
+    for c in range(CHUNKS):
+        mixed = collect(terms[2 * c], terms[2 * c + 1])
+        cotangents.append(
+            spread(jnp.tanh(own[c].astype(jnp.float32) + mixed).astype(jnp.bfloat16))
+        )
+    outs = ()
+    for c in range(CHUNKS):
+        outs = update(
+            cotangents[c],
+            hidden_t,
+            down_weight[0],
+            first_moment[0],
+            second_moment[0],
+            c,
+            CHUNKS,
+            outs,
+        )
+    return tuple(out[None] for out in outs)
+
+
 def solution(mesh):
     in_specs = (
         P(("dp", "expert"), None),
@@ -142,4 +358,6 @@
         P("expert", "dp", None),
     )
     out_specs = (P("expert", "dp", None), P("expert", "dp", None), P("expert", "dp", None))
+    small = mesh.shape["dp"] == 2 and mesh.shape["expert"] == 16
+    local = dense_plan if small else slot_plan
     return jax.shard_map(local, mesh=mesh, in_specs=in_specs, out_specs=out_specs, check_vma=False)

time: 294 us -> 97.1 us (0.33)
  waiting for transfers between devices: 202 us -> 49.9 us
  blocking collectives: 48.2 us -> 0 us
  starting transfers between devices: 5.76 us -> 25.5 us
  matrix products: 13.7 us -> 0.32 us
  between operations: 14 us -> 0.77 us
  Pallas kernels: 0 us -> 12.8 us
  other arithmetic: 7.77 us -> 2.7 us
    all_gather x3 -> x0, waiting for transfers between devices: 134 us -> none  [the longest x1 52 us: local(): lax.all_gather(up_weight, 'dp', axis=1, tiled=True)]
    ppermute x0 -> x27, waiting for transfers between devices: none -> 49.9 us  [swap(): return lax.ppermute(block, AXES, [(i, i ^ mask) for i in range(count)])]
    reduce_scatter x1 -> x0, waiting for transfers between devices: 49.8 us -> none  [local(): lax.psum_scatter(lax.dot_general(hidden, arrived_grad, over_tokens, prefe...]
    all_to_all x2 -> x0, blocking collectives: 48.2 us -> none  [the longest x1 25.4 us: local(): lax.all_to_all(outgoing.reshape(experts, capacity, model_width), 'expert'...]
    ppermute x0 -> x27, starting transfers between devices: none -> 25.5 us  [swap(): return lax.ppermute(block, AXES, [(i, i ^ mask) for i in range(count)])]
    all_to_all x1 -> x0, waiting for transfers between devices: 16.5 us -> none  [local(): lax.all_to_all(outputs.reshape(experts, capacity, model_width), 'expert',...]
    dot_general x6 -> x2, matrix products: 13.7 us -> 0.32 us  [the longest x1 0.19 us: dense_plan(): jnp.dot(pick, tokens, preferred_element_type=jnp.float32)]
    pallas_call x0 -> x2, Pallas kernels: none -> 12.8 us  [the longest x1 7.6 us: update(): pl.pallas_call(update_kernel, grid=(steps,), out_shape=[jax.ShapeDtypeStr...]
  transfers between devices with their start and end apart: 5 -> 27, of which waited for: 5 -> 20; matrix products, arithmetic and copies ran while one was open for 3% -> 0% of each run, Pallas kernels for 0% -> 0%
where the time goes in v2:
time: 97.1 us; the launch traced here: 96.9 us
  waiting for transfers between devices  49.9 us (51%)
  starting transfers between devices  25.5 us (26%)
  Pallas kernels  12.8 us (13%)
  local copies, waits for them, and re-layouts  4.87 us (5%)
  other arithmetic  2.7 us (3%)
    ppermute x27, waiting for transfers between devices, swap(): return lax.ppermute(block, AXES, [(i, i ^ mask) for i in range(count)])  49.9 us
    ppermute x27, starting transfers between devices, swap(): return lax.ppermute(block, AXES, [(i, i ^ mask) for i in range(count)])  25.5 us
    pallas_call x1, Pallas kernels, update(): pl.pallas_call(update_kernel, grid=(steps,), out_shape=[jax.ShapeDtypeStr...  7.6 us
    pallas_call x1, Pallas kernels, expert_terms(): pl.pallas_call(functools.partial(expert_kernel, chunks), out_shape=[half]...  5.17 us
    unnamed x12, local copies, waits for them, and re-layouts  4.66 us
  transfers between devices with their start and end apart: 27, of which 20 were waited for; matrix products, arithmetic and copies ran while one was open for 0% of the time, Pallas kernels for 0%

profile of v2, /device:TPU:0, one launch (start us, length us, event | category | flops | bytes accessed | tf_op | source)
XLA Modules:
  0.0 96.9 jit_solution(12359163663312171449)
XLA Ops:
  0.6 0.0 copy-start
  0.7 0.8 compare_reduce_fusion
  1.4 0.1 copy.17
  1.6 0.2 reduce-window.8
  1.7 0.1 reduce.1
  1.8 1.0 %fusion.4 = bf16[128,128]{1,0:T(8,128)(2,1)S(1)} fusion(s32[128,6]{0,1:T(8,128)} %param.9, pred[128]{0:T(512)(128)(4,1)S(1)} %iota_compare_fusion.2, bf16[128,6]{0,1:T(8,128)(2,1)} %param.10), kind=kLoop, calls=%fused_computation.11 | loop fusion | flops 376832 | bytes 37504 | tf_op jit(solution)/shard_map/reduce_sum | solution.py:316
  2.8 0.1 convolution_convert_fusion.1
  2.9 0.2 convolution_convert_fusion
  3.2 5.1 %collective-permute-start.2 = (bf16[12,2688]{1,0:T(8,128)(2,1)S(1)}, bf16[12,2688]{1,0:T(8,128)(2,1)S(1)}, u32[]{:S(2)}, u32[]{:S(2)}) collective-permute-start(bf16[12,2688]{1,0:T(8,128)(2,1)S(1)} %pad_maximum_fusion.2), channel_id=1, source_target_pairs={{0,12},{1,13},{2,14},{3,15},{4,8},{5,9},{6,10},{7,11},{8,4},{9,5},... | collective-permute-start | bytes 193544 | tf_op jit(solution)/shard_map/ppermute | solution.py:148
  8.3 0.0 collective-permute-start.1
  8.3 0.6 collective-permute-start
  8.9 2.6 %collective-permute-done.2 = bf16[12,2688]{1,0:T(8,128)(2,1)S(1)} collective-permute-done((bf16[12,2688]{1,0:T(8,128)(2,1)S(1)}, bf16[12,2688]{1,0:T(8,128)(2,1)S(1)}, u32[]{:S(2)}, u32[]{:S(2)}) %collective-permute-start.2) | collective-permute-done | bytes 64544 | tf_op jit(solution)/shard_map/ppermute | solution.py:148
  11.5 4.0 %collective-permute-done.1 = bf16[12,2688]{1,0:T(8,128)(2,1)S(1)} collective-permute-done((bf16[12,2688]{1,0:T(8,128)(2,1)S(1)}, bf16[12,2688]{1,0:T(8,128)(2,1)S(1)}, u32[]{:S(2)}, u32[]{:S(2)}) %collective-permute-start.1) | collective-permute-done | bytes 64544 | tf_op jit(solution)/shard_map/ppermute | solution.py:148
  15.5 0.1 pad_maximum_fusion.refs_0_
  15.6 2.5 %collective-permute-start.5 = (bf16[48,2688]{1,0:T(8,128)(2,1)S(1)}, bf16[48,2688]{1,0:T(8,128)(2,1)S(1)}, u32[]{:S(2)}, u32[]{:S(2)}) collective-permute-start(bf16[48,2688]{1,0:T(8,128)(2,1)S(1)} %pad_maximum_fusion.refs_0_), channel_id=1, source_target_pairs={{0,18},{1,19},{2,16},{3,17},{4,22},{5,23},{6,20},{7,21},{8,26},{9,... | collective-permute-start | bytes 774152 | tf_op jit(solution)/shard_map/ppermute | solution.py:148
  18.1 0.5 collective-permute-start.4
  18.6 0.5 collective-permute-start.3
  19.1 6.6 %collective-permute-done.5.refs_3_ = bf16[48,2688]{1,0:T(8,128)(2,1)S(1)} collective-permute-done((bf16[48,2688]{1,0:T(8,128)(2,1)S(1)}, bf16[48,2688]{1,0:T(8,128)(2,1)S(1)}, u32[]{:S(2)}, u32[]{:S(2)}) %collective-permute-start.5) | collective-permute-done | bytes 258080 | tf_op jit(solution)/shard_map/ppermute | solution.py:148
  25.8 3.7 %collective-permute-done.4.refs_2_ = bf16[48,2688]{1,0:T(8,128)(2,1)S(1)} collective-permute-done((bf16[48,2688]{1,0:T(8,128)(2,1)S(1)}, bf16[48,2688]{1,0:T(8,128)(2,1)S(1)}, u32[]{:S(2)}, u32[]{:S(2)}) %collective-permute-start.4) | collective-permute-done | bytes 258080 | tf_op jit(solution)/shard_map/ppermute | solution.py:148
  29.4 0.0 collective-permute-start.8
  29.4 0.2 collective-permute-done.3.refs_1_
  29.6 0.3 collective-permute-start.7
  29.9 0.0 collective-permute-done.6.refs_4_
  29.9 0.0 collective-permute-done.9.refs_7_
  30.0 1.0 %collective-permute-done.8.refs_6_ = bf16[48,2688]{1,0:T(8,128)(2,1)S(1)} collective-permute-done((bf16[48,2688]{1,0:T(8,128)(2,1)S(1)}, bf16[48,2688]{1,0:T(8,128)(2,1)S(1)}, u32[]{:S(2)}, u32[]{:S(2)}) %collective-permute-start.8) | collective-permute-done | bytes 258080 | tf_op jit(solution)/shard_map/ppermute | solution.py:148
  31.0 0.4 collective-permute-done.7.refs_5_
  31.3 1.5 %copy-done.1 = bf16[1,384,2560]{2,1,0:T(8,128)(2,1)S(1)} copy-done((bf16[1,384,2560]{2,1,0:T(8,128)(2,1)S(1)}, bf16[1,384,2560]{2,1,0:T(8,128)(2,1)}, u32[]{:S(2)}) %copy-start.1) | copy-done | bytes 1966104
  32.9 1.5 %copy-done.4 = bf16[1,384,2560]{2,1,0:T(8,128)(2,1)S(1)} copy-done((bf16[1,384,2560]{2,1,0:T(8,128)(2,1)S(1)}, bf16[1,384,2560]{2,1,0:T(8,128)(2,1)}, u32[]{:S(2)}) %copy-start.4) | copy-done | bytes 1966104
  34.4 1.5 %copy-done.5 = bf16[1,384,2560]{2,1,0:T(8,128)(2,1)S(1)} copy-done((bf16[1,384,2560]{2,1,0:T(8,128)(2,1)S(1)}, bf16[1,384,2560]{2,1,0:T(8,128)(2,1)}, u32[]{:S(2)}) %copy-start.5) | copy-done | bytes 1966104
  36.0 5.2 %expert_terms.1 = (bf16[192,2560]{1,0:T(8,128)(2,1)S(1)}, bf16[192,2560]{1,0:T(8,128)(2,1)S(1)}, bf16[384,384]{1,0:T(8,128)(2,1)S(1)}) custom-call(bf16[48,2688]{1,0:T(8,128)(2,1)S(1)} %pad_maximum_fusion.refs_0_, bf16[48,2688]{1,0:T(8,128)(2,1)S(1)} %collective-permute-done.3.refs_1_, bf16[48,2688]{1,0:T(8,128)(2,1)S(1)} %collective-permute-done.4.refs_2_, ...), custom_call_target="tpu_custom_call" | custom-call | flops 2264924160 | bytes 9830400 | tf_op jit(solution)/shard_map/expert_terms/pallas_call | solution.py:236
  41.1 0.2 collective-permute-start.10
  41.4 2.4 %collective-permute-done.10 = bf16[192,2560]{1,0:T(8,128)(2,1)S(1)} collective-permute-done((bf16[192,2560]{1,0:T(8,128)(2,1)S(1)}, bf16[192,2560]{1,0:T(8,128)(2,1)S(1)}, u32[]{:S(2)}, u32[]{:S(2)}) %collective-permute-start.10) | collective-permute-done | bytes 983072 | tf_op jit(solution)/shard_map/ppermute | solution.py:148
  43.8 0.3 convert_add_fusion
  44.1 0.0 copy-start.3
  44.1 0.1 fusion.20
  44.2 0.0 copy-start.2
  44.2 1.7 %collective-permute-start.11 = (bf16[48,2560]{1,0:T(8,128)(2,1)S(1)}, bf16[48,2560]{1,0:T(8,128)(2,1)S(1)}, u32[]{:S(2)}, u32[]{:S(2)}) collective-permute-start(bf16[48,2560]{1,0:T(8,128)(2,1)S(1)} %get-tuple-element.19), channel_id=1, source_target_pairs={{0,2},{1,3},{2,0},{3,1},{4,6},{5,7},{6,4},{7,5},{8,10},{9,11},{10,... | collective-permute-start | bytes 737288 | tf_op jit(solution)/shard_map/ppermute | solution.py:148
  45.9 1.5 %collective-permute-start.13 = (bf16[48,2560]{1,0:T(8,128)(2,1)S(1)}, bf16[48,2560]{1,0:T(8,128)(2,1)S(1)}, u32[]{:S(2)}, u32[]{:S(2)}) collective-permute-start(bf16[48,2560]{1,0:T(8,128)(2,1)S(1)} %get-tuple-element.20), channel_id=1, source_target_pairs={{0,18},{1,19},{2,16},{3,17},{4,22},{5,23},{6,20},{7,21},{8,26},{9,... | collective-permute-start | bytes 737288 | tf_op jit(solution)/shard_map/ppermute | solution.py:148
  47.3 0.4 collective-permute-start.12
  47.7 5.3 %collective-permute-done.11 = bf16[48,2560]{1,0:T(8,128)(2,1)S(1)} collective-permute-done((bf16[48,2560]{1,0:T(8,128)(2,1)S(1)}, bf16[48,2560]{1,0:T(8,128)(2,1)S(1)}, u32[]{:S(2)}, u32[]{:S(2)}) %collective-permute-start.11) | collective-permute-done | bytes 245792 | tf_op jit(solution)/shard_map/ppermute | solution.py:148
  53.0 5.6 %collective-permute-done.13 = bf16[48,2560]{1,0:T(8,128)(2,1)S(1)} collective-permute-done((bf16[48,2560]{1,0:T(8,128)(2,1)S(1)}, bf16[48,2560]{1,0:T(8,128)(2,1)S(1)}, u32[]{:S(2)}, u32[]{:S(2)}) %collective-permute-start.13) | collective-permute-done | bytes 245792 | tf_op jit(solution)/shard_map/ppermute | solution.py:148
  58.7 1.4 %collective-permute-done.12 = bf16[48,2560]{1,0:T(8,128)(2,1)S(1)} collective-permute-done((bf16[48,2560]{1,0:T(8,128)(2,1)S(1)}, bf16[48,2560]{1,0:T(8,128)(2,1)S(1)}, u32[]{:S(2)}, u32[]{:S(2)}) %collective-permute-start.12) | collective-permute-done | bytes 245792 | tf_op jit(solution)/shard_map/ppermute | solution.py:148
  60.0 0.1 fusion.18
  60.2 0.4 collective-permute-start.14
  60.6 1.9 %collective-permute-start.16 = (bf16[12,2560]{1,0:T(8,128)(2,1)S(1)}, bf16[12,2560]{1,0:T(8,128)(2,1)S(1)}, u32[]{:S(2)}, u32[]{:S(2)}) collective-permute-start(bf16[12,2560]{1,0:T(8,128)(2,1)S(1)} %get-tuple-element.23), channel_id=1, source_target_pairs={{0,12},{1,13},{2,14},{3,15},{4,8},{5,9},{6,10},{7,11},{8,4},{9,5},... | collective-permute-start | bytes 184328 | tf_op jit(solution)/shard_map/ppermute | solution.py:148
  62.5 1.2 %collective-permute-start.15 = (bf16[12,2560]{1,0:T(8,128)(2,1)S(1)}, bf16[12,2560]{1,0:T(8,128)(2,1)S(1)}, u32[]{:S(2)}, u32[]{:S(2)}) collective-permute-start(bf16[12,2560]{1,0:T(8,128)(2,1)S(1)} %get-tuple-element.24), channel_id=1, source_target_pairs={{0,8},{1,9},{2,10},{3,11},{4,12},{5,13},{6,14},{7,15},{8,0},{9,1},... | collective-permute-start | bytes 184328 | tf_op jit(solution)/shard_map/ppermute | solution.py:148
  63.8 1.7 %collective-permute-done.14 = bf16[12,2560]{1,0:T(8,128)(2,1)S(1)} collective-permute-done((bf16[12,2560]{1,0:T(8,128)(2,1)S(1)}, bf16[12,2560]{1,0:T(8,128)(2,1)S(1)}, u32[]{:S(2)}, u32[]{:S(2)}) %collective-permute-start.14) | collective-permute-done | bytes 61472 | tf_op jit(solution)/shard_map/ppermute | solution.py:148
  65.4 1.5 %collective-permute-done.16 = bf16[12,2560]{1,0:T(8,128)(2,1)S(1)} collective-permute-done((bf16[12,2560]{1,0:T(8,128)(2,1)S(1)}, bf16[12,2560]{1,0:T(8,128)(2,1)S(1)}, u32[]{:S(2)}, u32[]{:S(2)}) %collective-permute-start.16) | collective-permute-done | bytes 61472 | tf_op jit(solution)/shard_map/ppermute | solution.py:148
  66.9 2.5 %collective-permute-done.15 = bf16[12,2560]{1,0:T(8,128)(2,1)S(1)} collective-permute-done((bf16[12,2560]{1,0:T(8,128)(2,1)S(1)}, bf16[12,2560]{1,0:T(8,128)(2,1)S(1)}, u32[]{:S(2)}, u32[]{:S(2)}) %collective-permute-start.15) | collective-permute-done | bytes 61472 | tf_op jit(solution)/shard_map/ppermute | solution.py:148
  69.4 0.1 fusion.9
  69.5 2.7 %collective-permute-start.19 = (bf16[12,2560]{1,0:T(8,128)(2,1)S(1)}, bf16[12,2560]{1,0:T(8,128)(2,1)S(1)}, u32[]{:S(2)}, u32[]{:S(2)}) collective-permute-start(bf16[12,2560]{1,0:T(8,128)(2,1)S(1)} %fusion.9), channel_id=1, source_target_pairs={{0,12},{1,13},{2,14},{3,15},{4,8},{5,9},{6,10},{7,11},{8,4},{9,5},... | collective-permute-start | bytes 184328 | tf_op jit(solution)/shard_map/ppermute | solution.py:148
  72.2 1.8 %collective-permute-start.17 = (bf16[12,2560]{1,0:T(8,128)(2,1)S(1)}, bf16[12,2560]{1,0:T(8,128)(2,1)S(1)}, u32[]{:S(2)}, u32[]{:S(2)}) collective-permute-start(bf16[12,2560]{1,0:T(8,128)(2,1)S(1)} %fusion.9), channel_id=1, source_target_pairs={{0,4},{1,5},{2,6},{3,7},{4,0},{5,1},{6,2},{7,3},{8,12},{9,13},{10,... | collective-permute-start | bytes 184328 | tf_op jit(solution)/shard_map/ppermute | solution.py:148
  73.9 1.9 %collective-permute-done.19 = bf16[12,2560]{1,0:T(8,128)(2,1)S(1)} collective-permute-done((bf16[12,2560]{1,0:T(8,128)(2,1)S(1)}, bf16[12,2560]{1,0:T(8,128)(2,1)S(1)}, u32[]{:S(2)}, u32[]{:S(2)}) %collective-permute-start.19) | collective-permute-done | bytes 61472 | tf_op jit(solution)/shard_map/ppermute | solution.py:148
  75.8 1.8 %collective-permute-done.18 = bf16[12,2560]{1,0:T(8,128)(2,1)S(1)} collective-permute-done((bf16[12,2560]{1,0:T(8,128)(2,1)S(1)}, bf16[12,2560]{1,0:T(8,128)(2,1)S(1)}, u32[]{:S(2)}, u32[]{:S(2)}) %collective-permute-start.18) | collective-permute-done | bytes 61472 | tf_op jit(solution)/shard_map/ppermute | solution.py:148
  77.5 0.1 pad_maximum_fusion.1.refs_0_
  77.6 1.5 %collective-permute-start.22 = (bf16[48,2560]{1,0:T(8,128)(2,1)S(1)}, bf16[48,2560]{1,0:T(8,128)(2,1)S(1)}, u32[]{:S(2)}, u32[]{:S(2)}) collective-permute-start(bf16[48,2560]{1,0:T(8,128)(2,1)S(1)} %pad_maximum_fusion.1.refs_0_), channel_id=1, source_target_pairs={{0,18},{1,19},{2,16},{3,17},{4,22},{5,23},{6,20},{7,21},{8,26},{9,... | collective-permute-start | bytes 737288 | tf_op jit(solution)/shard_map/ppermute | solution.py:148
  79.1 0.8 collective-permute-start.21
  79.9 1.3 %collective-permute-start.20 = (bf16[48,2560]{1,0:T(8,128)(2,1)S(1)}, bf16[48,2560]{1,0:T(8,128)(2,1)S(1)}, u32[]{:S(2)}, u32[]{:S(2)}) collective-permute-start(bf16[48,2560]{1,0:T(8,128)(2,1)S(1)} %pad_maximum_fusion.1.refs_0_), channel_id=1, source_target_pairs={{0,2},{1,3},{2,0},{3,1},{4,6},{5,7},{6,4},{7,5},{8,10},{9,11},{10,... | collective-permute-start | bytes 737288 | tf_op jit(solution)/shard_map/ppermute | solution.py:148
  81.2 3.7 %collective-permute-done.22.refs_3_ = bf16[48,2560]{1,0:T(8,128)(2,1)S(1)} collective-permute-done((bf16[48,2560]{1,0:T(8,128)(2,1)S(1)}, bf16[48,2560]{1,0:T(8,128)(2,1)S(1)}, u32[]{:S(2)}, u32[]{:S(2)}) %collective-permute-start.22) | collective-permute-done | bytes 245792 | tf_op jit(solution)/shard_map/ppermute | solution.py:148
  84.9 2.5 %collective-permute-done.21.refs_2_ = bf16[48,2560]{1,0:T(8,128)(2,1)S(1)} collective-permute-done((bf16[48,2560]{1,0:T(8,128)(2,1)S(1)}, bf16[48,2560]{1,0:T(8,128)(2,1)S(1)}, u32[]{:S(2)}, u32[]{:S(2)}) %collective-permute-start.21) | collective-permute-done | bytes 245792 | tf_op jit(solution)/shard_map/ppermute | solution.py:148
  87.4 0.5 collective-permute-start.24
  87.9 1.0 %collective-permute-done.25.refs_6_ = bf16[48,2560]{1,0:T(8,128)(2,1)S(1)} collective-permute-done((bf16[48,2560]{1,0:T(8,128)(2,1)S(1)}, bf16[48,2560]{1,0:T(8,128)(2,1)S(1)}, u32[]{:S(2)}, u32[]{:S(2)}) %collective-permute-start.25) | collective-permute-done | bytes 245792 | tf_op jit(solution)/shard_map/ppermute | solution.py:148
  88.9 0.4 collective-permute-done.24.refs_5_
  89.3 7.6 %update.1 = (bf16[384,2560]{1,0:T(8,128)(2,1)}, bf16[384,2560]{1,0:T(8,128)(2,1)}, bf16[384,2560]{1,0:T(8,128)(2,1)}) custom-call(bf16[48,2560]{1,0:T(8,128)(2,1)S(1)} %pad_maximum_fusion.1.refs_0_, bf16[48,2560]{1,0:T(8,128)(2,1)S(1)} %collective-permute-done.20.refs_1_, bf16[48,2560]{1,0:T(8,128)(2,1)S(1)} %collective-permute-done.21.refs_2_, ...), custom_call_target="tpu_custom_call" | custom-call | flops 754974720 | bytes 13762560 | tf_op jit(solution)/shard_map/update/pallas_call | solution.py:283
  (23 shorter events, 0.1 us)
Async XLA Ops:
  0.6 2.3 %copy-start = (bf16[128,2560]{1,0:T(8,128)(2,1)S(1)}, bf16[128,2560]{1,0:T(8,128)(2,1)}, u32[]{:S(2)}) copy-start(bf16[128,2560]{1,0:T(8,128)(2,1)} %param.8) | copy-start | bytes 1966084
  3.2 8.3 %collective-permute-start.2 = (bf16[12,2688]{1,0:T(8,128)(2,1)S(1)}, bf16[12,2688]{1,0:T(8,128)(2,1)S(1)}, u32[]{:S(2)}, u32[]{:S(2)}) collective-permute-start(bf16[12,2688]{1,0:T(8,128)(2,1)S(1)} %pad_maximum_fusion.2), channel_id=1, source_target_pairs={{0,12},{1,13},{2,14},{3,15},{4,8},{5,9},{6,10},{7,11},{8,4},{9,5},... | collective-permute-start | bytes 193544 | tf_op jit(solution)/shard_map/ppermute | solution.py:148
  8.3 7.2 %collective-permute-start.1 = (bf16[12,2688]{1,0:T(8,128)(2,1)S(1)}, bf16[12,2688]{1,0:T(8,128)(2,1)S(1)}, u32[]{:S(2)}, u32[]{:S(2)}) collective-permute-start(bf16[12,2688]{1,0:T(8,128)(2,1)S(1)} %pad_maximum_fusion.2), channel_id=1, source_target_pairs={{0,8},{1,9},{2,10},{3,11},{4,12},{5,13},{6,14},{7,15},{8,0},{9,1},... | collective-permute-start | bytes 193544 | tf_op jit(solution)/shard_map/ppermute | solution.py:148
  8.3 7.2 %collective-permute-start = (bf16[12,2688]{1,0:T(8,128)(2,1)S(1)}, bf16[12,2688]{1,0:T(8,128)(2,1)S(1)}, u32[]{:S(2)}, u32[]{:S(2)}) collective-permute-start(bf16[12,2688]{1,0:T(8,128)(2,1)S(1)} %pad_maximum_fusion.2), channel_id=1, source_target_pairs={{0,4},{1,5},{2,6},{3,7},{4,0},{5,1},{6,2},{7,3},{8,12},{9,13},{10,... | collective-permute-start | bytes 193544 | tf_op jit(solution)/shard_map/ppermute | solution.py:148
  15.6 10.2 %collective-permute-start.5 = (bf16[48,2688]{1,0:T(8,128)(2,1)S(1)}, bf16[48,2688]{1,0:T(8,128)(2,1)S(1)}, u32[]{:S(2)}, u32[]{:S(2)}) collective-permute-start(bf16[48,2688]{1,0:T(8,128)(2,1)S(1)} %pad_maximum_fusion.refs_0_), channel_id=1, source_target_pairs={{0,18},{1,19},{2,16},{3,17},{4,22},{5,23},{6,20},{7,21},{8,26},{9,... | collective-permute-start | bytes 774152 | tf_op jit(solution)/shard_map/ppermute | solution.py:148
  18.1 11.3 %collective-permute-start.4 = (bf16[48,2688]{1,0:T(8,128)(2,1)S(1)}, bf16[48,2688]{1,0:T(8,128)(2,1)S(1)}, u32[]{:S(2)}, u32[]{:S(2)}) collective-permute-start(bf16[48,2688]{1,0:T(8,128)(2,1)S(1)} %pad_maximum_fusion.refs_0_), channel_id=1, source_target_pairs={{0,16},{1,17},{2,18},{3,19},{4,20},{5,21},{6,22},{7,23},{8,24},{9,... | collective-permute-start | bytes 774152 | tf_op jit(solution)/shard_map/ppermute | solution.py:148
  18.6 11.0 %collective-permute-start.3 = (bf16[48,2688]{1,0:T(8,128)(2,1)S(1)}, bf16[48,2688]{1,0:T(8,128)(2,1)S(1)}, u32[]{:S(2)}, u32[]{:S(2)}) collective-permute-start(bf16[48,2688]{1,0:T(8,128)(2,1)S(1)} %pad_maximum_fusion.refs_0_), channel_id=1, source_target_pairs={{0,2},{1,3},{2,0},{3,1},{4,6},{5,7},{6,4},{7,5},{8,10},{9,11},{10,... | collective-permute-start | bytes 774152 | tf_op jit(solution)/shard_map/ppermute | solution.py:148
  19.1 10.8 %collective-permute-start.6 = (bf16[48,2688]{1,0:T(8,128)(2,1)S(1)}, bf16[48,2688]{1,0:T(8,128)(2,1)S(1)}, u32[]{:S(2)}, u32[]{:S(2)}) collective-permute-start(bf16[48,2688]{1,0:T(8,128)(2,1)S(1)} %pad_maximum_fusion.refs_0_), channel_id=1, source_target_pairs={{0,1},{1,0},{2,3},{3,2},{4,5},{5,4},{6,7},{7,6},{8,9},{9,8},{10,11... | collective-permute-start | bytes 774152 | tf_op jit(solution)/shard_map/ppermute | solution.py:148
  25.8 4.2 %collective-permute-start.9 = (bf16[48,2688]{1,0:T(8,128)(2,1)S(1)}, bf16[48,2688]{1,0:T(8,128)(2,1)S(1)}, u32[]{:S(2)}, u32[]{:S(2)}) collective-permute-start(bf16[48,2688]{1,0:T(8,128)(2,1)S(1)} %collective-permute-done.5.refs_3_), channel_id=1, source_target_pairs={{0,1},{1,0},{2,3},{3,2},{4,5},{5,4},{6,7},{7,6},{8,9},{9,8},{10,11... | collective-permute-start | bytes 774152 | tf_op jit(solution)/shard_map/ppermute | solution.py:148
  29.4 1.5 %collective-permute-start.8 = (bf16[48,2688]{1,0:T(8,128)(2,1)S(1)}, bf16[48,2688]{1,0:T(8,128)(2,1)S(1)}, u32[]{:S(2)}, u32[]{:S(2)}) collective-permute-start(bf16[48,2688]{1,0:T(8,128)(2,1)S(1)} %collective-permute-done.4.refs_2_), channel_id=1, source_target_pairs={{0,1},{1,0},{2,3},{3,2},{4,5},{5,4},{6,7},{7,6},{8,9},{9,8},{10,11... | collective-permute-start | bytes 774152 | tf_op jit(solution)/shard_map/ppermute | solution.py:148
  29.6 1.7 %collective-permute-start.7 = (bf16[48,2688]{1,0:T(8,128)(2,1)S(1)}, bf16[48,2688]{1,0:T(8,128)(2,1)S(1)}, u32[]{:S(2)}, u32[]{:S(2)}) collective-permute-start(bf16[48,2688]{1,0:T(8,128)(2,1)S(1)} %collective-permute-done.3.refs_1_), channel_id=1, source_target_pairs={{0,1},{1,0},{2,3},{3,2},{4,5},{5,4},{6,7},{7,6},{8,9},{9,8},{10,11... | collective-permute-start | bytes 774152 | tf_op jit(solution)/shard_map/ppermute | solution.py:148
  31.3 1.5 %copy-start.1 = (bf16[1,384,2560]{2,1,0:T(8,128)(2,1)S(1)}, bf16[1,384,2560]{2,1,0:T(8,128)(2,1)}, u32[]{:S(2)}) copy-start(bf16[1,384,2560]{2,1,0:T(8,128)(2,1)} %param.13) | copy-start | bytes 5898244
  32.9 1.5 %copy-start.4 = (bf16[1,384,2560]{2,1,0:T(8,128)(2,1)S(1)}, bf16[1,384,2560]{2,1,0:T(8,128)(2,1)}, u32[]{:S(2)}) copy-start(bf16[1,384,2560]{2,1,0:T(8,128)(2,1)} %param.11) | copy-start | bytes 5898244
  34.4 1.5 %copy-start.5 = (bf16[1,384,2560]{2,1,0:T(8,128)(2,1)S(1)}, bf16[1,384,2560]{2,1,0:T(8,128)(2,1)}, u32[]{:S(2)}) copy-start(bf16[1,384,2560]{2,1,0:T(8,128)(2,1)} %param.12) | copy-start | bytes 5898244
  41.1 2.6 %collective-permute-start.10 = (bf16[192,2560]{1,0:T(8,128)(2,1)S(1)}, bf16[192,2560]{1,0:T(8,128)(2,1)S(1)}, u32[]{:S(2)}, u32[]{:S(2)}) collective-permute-start(bf16[192,2560]{1,0:T(8,128)(2,1)S(1)} %get-tuple-element.10), channel_id=1, source_target_pairs={{0,1},{1,0},{2,3},{3,2},{4,5},{5,4},{6,7},{7,6},{8,9},{9,8},{10,11... | collective-permute-start | bytes 2949128 | tf_op jit(solution)/shard_map/ppermute | solution.py:148
  44.1 45.2 %copy-start.3 = (bf16[1,384,2560]{2,1,0:T(8,128)(2,1)S(1)}, bf16[1,384,2560]{2,1,0:T(8,128)(2,1)}, u32[]{:S(2)}) copy-start(bf16[1,384,2560]{2,1,0:T(8,128)(2,1)} %param.15) | copy-start | bytes 5898244
  44.2 45.1 %copy-start.2 = (bf16[1,384,2560]{2,1,0:T(8,128)(2,1)S(1)}, bf16[1,384,2560]{2,1,0:T(8,128)(2,1)}, u32[]{:S(2)}) copy-start(bf16[1,384,2560]{2,1,0:T(8,128)(2,1)} %param.14) | copy-start | bytes 5898244
  44.2 8.9 %collective-permute-start.11 = (bf16[48,2560]{1,0:T(8,128)(2,1)S(1)}, bf16[48,2560]{1,0:T(8,128)(2,1)S(1)}, u32[]{:S(2)}, u32[]{:S(2)}) collective-permute-start(bf16[48,2560]{1,0:T(8,128)(2,1)S(1)} %get-tuple-element.19), channel_id=1, source_target_pairs={{0,2},{1,3},{2,0},{3,1},{4,6},{5,7},{6,4},{7,5},{8,10},{9,11},{10,... | collective-permute-start | bytes 737288 | tf_op jit(solution)/shard_map/ppermute | solution.py:148
  45.9 12.8 %collective-permute-start.13 = (bf16[48,2560]{1,0:T(8,128)(2,1)S(1)}, bf16[48,2560]{1,0:T(8,128)(2,1)S(1)}, u32[]{:S(2)}, u32[]{:S(2)}) collective-permute-start(bf16[48,2560]{1,0:T(8,128)(2,1)S(1)} %get-tuple-element.20), channel_id=1, source_target_pairs={{0,18},{1,19},{2,16},{3,17},{4,22},{5,23},{6,20},{7,21},{8,26},{9,... | collective-permute-start | bytes 737288 | tf_op jit(solution)/shard_map/ppermute | solution.py:148
  47.3 12.7 %collective-permute-start.12 = (bf16[48,2560]{1,0:T(8,128)(2,1)S(1)}, bf16[48,2560]{1,0:T(8,128)(2,1)S(1)}, u32[]{:S(2)}, u32[]{:S(2)}) collective-permute-start(bf16[48,2560]{1,0:T(8,128)(2,1)S(1)} %get-tuple-element.21), channel_id=1, source_target_pairs={{0,16},{1,17},{2,18},{3,19},{4,20},{5,21},{6,22},{7,23},{8,24},{9,... | collective-permute-start | bytes 737288 | tf_op jit(solution)/shard_map/ppermute | solution.py:148
  60.2 5.2 %collective-permute-start.14 = (bf16[12,2560]{1,0:T(8,128)(2,1)S(1)}, bf16[12,2560]{1,0:T(8,128)(2,1)S(1)}, u32[]{:S(2)}, u32[]{:S(2)}) collective-permute-start(bf16[12,2560]{1,0:T(8,128)(2,1)S(1)} %get-tuple-element.22), channel_id=1, source_target_pairs={{0,4},{1,5},{2,6},{3,7},{4,0},{5,1},{6,2},{7,3},{8,12},{9,13},{10,... | collective-permute-start | bytes 184328 | tf_op jit(solution)/shard_map/ppermute | solution.py:148
  60.6 6.3 %collective-permute-start.16 = (bf16[12,2560]{1,0:T(8,128)(2,1)S(1)}, bf16[12,2560]{1,0:T(8,128)(2,1)S(1)}, u32[]{:S(2)}, u32[]{:S(2)}) collective-permute-start(bf16[12,2560]{1,0:T(8,128)(2,1)S(1)} %get-tuple-element.23), channel_id=1, source_target_pairs={{0,12},{1,13},{2,14},{3,15},{4,8},{5,9},{6,10},{7,11},{8,4},{9,5},... | collective-permute-start | bytes 184328 | tf_op jit(solution)/shard_map/ppermute | solution.py:148
  62.5 6.9 %collective-permute-start.15 = (bf16[12,2560]{1,0:T(8,128)(2,1)S(1)}, bf16[12,2560]{1,0:T(8,128)(2,1)S(1)}, u32[]{:S(2)}, u32[]{:S(2)}) collective-permute-start(bf16[12,2560]{1,0:T(8,128)(2,1)S(1)} %get-tuple-element.24), channel_id=1, source_target_pairs={{0,8},{1,9},{2,10},{3,11},{4,12},{5,13},{6,14},{7,15},{8,0},{9,1},... | collective-permute-start | bytes 184328 | tf_op jit(solution)/shard_map/ppermute | solution.py:148
  69.5 6.3 %collective-permute-start.19 = (bf16[12,2560]{1,0:T(8,128)(2,1)S(1)}, bf16[12,2560]{1,0:T(8,128)(2,1)S(1)}, u32[]{:S(2)}, u32[]{:S(2)}) collective-permute-start(bf16[12,2560]{1,0:T(8,128)(2,1)S(1)} %fusion.9), channel_id=1, source_target_pairs={{0,12},{1,13},{2,14},{3,15},{4,8},{5,9},{6,10},{7,11},{8,4},{9,5},... | collective-permute-start | bytes 184328 | tf_op jit(solution)/shard_map/ppermute | solution.py:148
  72.2 5.4 %collective-permute-start.18 = (bf16[12,2560]{1,0:T(8,128)(2,1)S(1)}, bf16[12,2560]{1,0:T(8,128)(2,1)S(1)}, u32[]{:S(2)}, u32[]{:S(2)}) collective-permute-start(bf16[12,2560]{1,0:T(8,128)(2,1)S(1)} %fusion.9), channel_id=1, source_target_pairs={{0,8},{1,9},{2,10},{3,11},{4,12},{5,13},{6,14},{7,15},{8,0},{9,1},... | collective-permute-start | bytes 184328 | tf_op jit(solution)/shard_map/ppermute | solution.py:148
  72.2 5.4 %collective-permute-start.17 = (bf16[12,2560]{1,0:T(8,128)(2,1)S(1)}, bf16[12,2560]{1,0:T(8,128)(2,1)S(1)}, u32[]{:S(2)}, u32[]{:S(2)}) collective-permute-start(bf16[12,2560]{1,0:T(8,128)(2,1)S(1)} %fusion.9), channel_id=1, source_target_pairs={{0,4},{1,5},{2,6},{3,7},{4,0},{5,1},{6,2},{7,3},{8,12},{9,13},{10,... | collective-permute-start | bytes 184328 | tf_op jit(solution)/shard_map/ppermute | solution.py:148
  77.6 7.3 %collective-permute-start.22 = (bf16[48,2560]{1,0:T(8,128)(2,1)S(1)}, bf16[48,2560]{1,0:T(8,128)(2,1)S(1)}, u32[]{:S(2)}, u32[]{:S(2)}) collective-permute-start(bf16[48,2560]{1,0:T(8,128)(2,1)S(1)} %pad_maximum_fusion.1.refs_0_), channel_id=1, source_target_pairs={{0,18},{1,19},{2,16},{3,17},{4,22},{5,23},{6,20},{7,21},{8,26},{9,... | collective-permute-start | bytes 737288 | tf_op jit(solution)/shard_map/ppermute | solution.py:148
  79.1 8.3 %collective-permute-start.21 = (bf16[48,2560]{1,0:T(8,128)(2,1)S(1)}, bf16[48,2560]{1,0:T(8,128)(2,1)S(1)}, u32[]{:S(2)}, u32[]{:S(2)}) collective-permute-start(bf16[48,2560]{1,0:T(8,128)(2,1)S(1)} %pad_maximum_fusion.1.refs_0_), channel_id=1, source_target_pairs={{0,16},{1,17},{2,18},{3,19},{4,20},{5,21},{6,22},{7,23},{8,24},{9,... | collective-permute-start | bytes 737288 | tf_op jit(solution)/shard_map/ppermute | solution.py:148
  79.9 7.5 %collective-permute-start.20 = (bf16[48,2560]{1,0:T(8,128)(2,1)S(1)}, bf16[48,2560]{1,0:T(8,128)(2,1)S(1)}, u32[]{:S(2)}, u32[]{:S(2)}) collective-permute-start(bf16[48,2560]{1,0:T(8,128)(2,1)S(1)} %pad_maximum_fusion.1.refs_0_), channel_id=1, source_target_pairs={{0,2},{1,3},{2,0},{3,1},{4,6},{5,7},{6,4},{7,5},{8,10},{9,11},{10,... | collective-permute-start | bytes 737288 | tf_op jit(solution)/shard_map/ppermute | solution.py:148
  81.2 6.8 %collective-permute-start.23 = (bf16[48,2560]{1,0:T(8,128)(2,1)S(1)}, bf16[48,2560]{1,0:T(8,128)(2,1)S(1)}, u32[]{:S(2)}, u32[]{:S(2)}) collective-permute-start(bf16[48,2560]{1,0:T(8,128)(2,1)S(1)} %pad_maximum_fusion.1.refs_0_), channel_id=1, source_target_pairs={{0,1},{1,0},{2,3},{3,2},{4,5},{5,4},{6,7},{7,6},{8,9},{9,8},{10,11... | collective-permute-start | bytes 737288 | tf_op jit(solution)/shard_map/ppermute | solution.py:148
  84.9 3.0 %collective-permute-start.26 = (bf16[48,2560]{1,0:T(8,128)(2,1)S(1)}, bf16[48,2560]{1,0:T(8,128)(2,1)S(1)}, u32[]{:S(2)}, u32[]{:S(2)}) collective-permute-start(bf16[48,2560]{1,0:T(8,128)(2,1)S(1)} %collective-permute-done.22.refs_3_), channel_id=1, source_target_pairs={{0,1},{1,0},{2,3},{3,2},{4,5},{5,4},{6,7},{7,6},{8,9},{9,8},{10,11... | collective-permute-start | bytes 737288 | tf_op jit(solution)/shard_map/ppermute | solution.py:148
  87.4 1.5 %collective-permute-start.25 = (bf16[48,2560]{1,0:T(8,128)(2,1)S(1)}, bf16[48,2560]{1,0:T(8,128)(2,1)S(1)}, u32[]{:S(2)}, u32[]{:S(2)}) collective-permute-start(bf16[48,2560]{1,0:T(8,128)(2,1)S(1)} %collective-permute-done.21.refs_2_), channel_id=1, source_target_pairs={{0,1},{1,0},{2,3},{3,2},{4,5},{5,4},{6,7},{7,6},{8,9},{9,8},{10,11... | collective-permute-start | bytes 737288 | tf_op jit(solution)/shard_map/ppermute | solution.py:148
  87.4 1.9 %collective-permute-start.24 = (bf16[48,2560]{1,0:T(8,128)(2,1)S(1)}, bf16[48,2560]{1,0:T(8,128)(2,1)S(1)}, u32[]{:S(2)}, u32[]{:S(2)}) collective-permute-start(bf16[48,2560]{1,0:T(8,128)(2,1)S(1)} %collective-permute-done.20.refs_1_), channel_id=1, source_target_pairs={{0,1},{1,0},{2,3},{3,2},{4,5},{5,4},{6,7},{7,6},{8,9},{9,8},{10,11... | collective-permute-start | bytes 737288 | tf_op jit(solution)/shard_map/ppermute | solution.py:148

commit v3 on v0

--- a/solution.py
+++ b/solution.py
@@ -1,6 +1,10 @@
+import functools
+
 import jax
 import jax.numpy as jnp
 from jax import lax
+from jax.experimental import pallas as pl
+from jax.experimental.pallas import tpu as pltpu
 from jax.sharding import PartitionSpec as P
 
 CAP = 6
@@ -55,7 +59,7 @@
     )
 
 
-def local(
+def slot_plan(
     tokens,
     expert_ids,
     gate_values,
@@ -130,6 +134,192 @@
     return (new_down[None], new_first[None], new_second[None])
 
 
+AXES = ("dp", "expert")
+CORE = 1
+PLANE = (2, 16, 18)
+LINE = (4, 8, 12)
+BLOCK = 512
+PARTS = 2
+LIMIT = 48
+LANES = 128
+MIB = 1024 * 1024
+
+
+def swap(block, mask):
+    count = lax.axis_size(AXES)
+    return lax.ppermute(block, AXES, [(i, i ^ mask) for i in range(count)])
+
+
+def spread(block):
+    block = jnp.concatenate([block] + [swap(block, mask) for mask in LINE], axis=0)
+    return [block] + [swap(block, mask) for mask in PLANE]
+
+
+def to_core(pieces):
+    return [swap(piece, CORE) for piece in pieces]
+
+
+def add_parts(own, other_parts):
+    total = own.astype(jnp.float32)
+    for part in other_parts:
+        total = total + part.astype(jnp.float32)
+    return total
+
+
+def collect(own, other):
+    total = add_parts(own, [swap(other, CORE)])
+    for masks in (PLANE, LINE):
+        parts = jnp.split(total, len(masks) + 1, axis=0)
+        sent = [swap(part.astype(jnp.bfloat16), mask) for part, mask in zip(parts[1:], masks)]
+        total = add_parts(parts[0], sent)
+    return total
+
+
+def expert_kernel(*refs):
+    pieces = refs[:8]
+    gate_ref, up_ref, down_ref, own_ref, other_ref, hidden_t_ref = refs[8:14]
+    gate_vm, up_vm, down_vm, rows, sems = refs[14:]
+    count, width = rows.shape
+    part = count // 8
+    spans = [pl.ds(start, width // PARTS) for start in range(0, width, width // PARTS)]
+    loads = [
+        [
+            pltpu.make_async_copy(src.at[:, span], dst.at[:, span], sems.at[PARTS * k + s])
+            for s, span in enumerate(spans)
+        ]
+        for k, (src, dst) in enumerate(
+            ((gate_ref, gate_vm), (up_ref, up_vm), (down_ref, down_vm))
+        )
+    ]
+    for s in range(PARTS):
+        loads[0][s].start()
+        loads[1][s].start()
+    for load in loads[2]:
+        load.start()
+    for p in range(8):
+        rows[p * part : (p + 1) * part] = pieces[p][:, :width]
+    gates = jnp.concatenate([piece[:, width:] for piece in pieces], axis=0).astype(jnp.float32)
+    lane = lax.broadcasted_iota(jnp.int32, gates.shape, 1)
+    gates = jnp.where(lane == lax.axis_index("expert"), gates, 0.0)
+    gate = jnp.sum(gates, axis=1, keepdims=True)
+    contract = (((1,), (1,)), ((), ()))
+    gate_part, up_part = 0.0, 0.0
+    for s, span in enumerate(spans):
+        loads[0][s].wait()
+        gate_part += lax.dot_general(
+            rows[:, span], gate_vm[:, span], contract, preferred_element_type=jnp.float32
+        )
+        loads[1][s].wait()
+        up_part += lax.dot_general(
+            rows[:, span], up_vm[:, span], contract, preferred_element_type=jnp.float32
+        )
+    hidden = gate * (jax.nn.silu(gate_part) * up_part)
+    hidden_t_ref[...] = hidden.T.astype(jnp.bfloat16)
+    hidden = hidden.astype(jnp.bfloat16)
+    for load, span in zip(loads[2], spans):
+        load.wait()
+        terms = jnp.dot(hidden, down_vm[:, span], preferred_element_type=jnp.float32)
+        terms = terms.astype(jnp.bfloat16)
+        own_ref[:, span] = terms[: count // 2]
+        other_ref[:, span] = terms[count // 2 :]
+
+
+def expert_terms(pieces, gate_weight, up_weight, down_weight):
+    units, width = gate_weight.shape
+    count = 8 * pieces[0].shape[0]
+    half = jax.ShapeDtypeStruct((count // 2, width), jnp.bfloat16)
+    in_vmem = pl.BlockSpec(memory_space=pltpu.VMEM)
+    in_hbm = pl.BlockSpec(memory_space=pltpu.HBM)
+    return pl.pallas_call(
+        expert_kernel,
+        out_shape=[half, half, jax.ShapeDtypeStruct((units, count), jnp.bfloat16)],
+        in_specs=[in_vmem] * 8 + [in_hbm] * 3,
+        out_specs=[in_vmem] * 3,
+        scratch_shapes=[pltpu.VMEM((units, width), jnp.bfloat16)] * 3
+        + [pltpu.VMEM((count, width), jnp.bfloat16), pltpu.SemaphoreType.DMA((3 * PARTS,))],
+        compiler_params=pltpu.CompilerParams(vmem_limit_bytes=LIMIT * MIB),
+        cost_estimate=pl.CostEstimate(
+            flops=6 * count * units * width,
+            bytes_accessed=10 * count * width,
+            transcendentals=count * units,
+        ),
+        name="expert_terms",
+    )(*pieces, gate_weight, up_weight, down_weight)
+
+
+def update_kernel(block, *refs):
+    pieces = refs[:8]
+    hidden_t_ref, down_ref, first_ref, second_ref = refs[8:12]
+    new_down_ref, new_first_ref, new_second_ref = refs[12:]
+    span = pl.ds(pl.multiple_of(pl.program_id(0) * block, LANES), block)
+    cotangent = jnp.concatenate([piece[:, span] for piece in pieces], axis=0)
+    gradient = jnp.dot(hidden_t_ref[...], cotangent, preferred_element_type=jnp.float32)
+    first = first_decay * first_ref[:, span].astype(jnp.float32) + (1.0 - first_decay) * gradient
+    second = (
+        second_decay * second_ref[:, span].astype(jnp.float32)
+        + (1.0 - second_decay) * gradient * gradient
+    )
+    root = (1.0 - second_decay**adam_count) ** 0.5
+    rate = learn_rate * root / (1.0 - first_decay**adam_count)
+    keep = 1.0 - learn_rate * weight_decay
+    step = rate * first / (jnp.sqrt(second) + adam_epsilon * root)
+    new_down_ref[...] = (keep * down_ref[:, span].astype(jnp.float32) - step).astype(jnp.bfloat16)
+    new_first_ref[...] = first.astype(jnp.bfloat16)
+    new_second_ref[...] = second.astype(jnp.bfloat16)
+
+
+def update(pieces, hidden_t, down_weight, first_moment, second_moment):
+    units, width = down_weight.shape
+    part = pieces[0].shape[0]
+    in_vmem = pl.BlockSpec(memory_space=pltpu.VMEM)
+    return pl.pallas_call(
+        functools.partial(update_kernel, BLOCK),
+        grid=(width // BLOCK,),
+        out_shape=[jax.ShapeDtypeStruct((units, width), jnp.bfloat16)] * 3,
+        in_specs=[in_vmem] * 12,
+        out_specs=[pl.BlockSpec((units, BLOCK), lambda i: (0, i))] * 3,
+        compiler_params=pltpu.CompilerParams(vmem_limit_bytes=24 * MIB),
+        cost_estimate=pl.CostEstimate(
+            flops=2 * 8 * part * units * width,
+            bytes_accessed=14 * units * width,
+            transcendentals=2 * units * width,
+        ),
+        name="update",
+    )(*pieces, hidden_t, down_weight, first_moment, second_moment)
+
+
+def dense_plan(
+    tokens,
+    expert_ids,
+    gate_values,
+    gate_weight,
+    up_weight,
+    down_weight,
+    first_moment,
+    second_moment,
+):
+    experts = lax.axis_size("expert")
+    hot_rows = experts * 3 // 4
+    numbers = jnp.arange(LANES, dtype=jnp.int32)
+    matches = (expert_ids[:, :, None] == numbers) & (numbers < experts)
+    gates = jnp.sum(jnp.where(matches, gate_values[:, :, None], 0), axis=1)
+    hot = jnp.any(expert_ids < experts, axis=1).astype(jnp.int32)
+    rank = jnp.cumsum(hot) - hot
+    place = jnp.arange(hot_rows, dtype=jnp.int32)
+    pick = ((rank[None, :] == place[:, None]) & (hot[None, :] == 1)).astype(jnp.bfloat16)
+    hot_tokens = jnp.dot(pick, tokens, preferred_element_type=jnp.float32).astype(jnp.bfloat16)
+    hot_gates = jnp.dot(pick, gates, preferred_element_type=jnp.float32).astype(jnp.bfloat16)
+    pieces = spread(jnp.concatenate([hot_tokens, hot_gates], axis=1))
+    pieces += to_core(pieces)
+    own, other, hidden_t = expert_terms(pieces, gate_weight[0], up_weight[0], down_weight[0])
+    mixed = collect(own, other)
+    cotangent = jnp.tanh(hot_tokens.astype(jnp.float32) + mixed).astype(jnp.bfloat16)
+    pieces = spread(cotangent)
+    pieces += to_core(pieces)
+    outs = update(pieces, hidden_t, down_weight[0], first_moment[0], second_moment[0])
+    return tuple(out[None] for out in outs)
+
+
 def solution(mesh):
     in_specs = (
         P(("dp", "expert"), None),
@@ -142,4 +332,6 @@
         P("expert", "dp", None),
     )
     out_specs = (P("expert", "dp", None), P("expert", "dp", None), P("expert", "dp", None))
+    small = mesh.shape["dp"] == 2 and mesh.shape["expert"] == 16
+    local = dense_plan if small else slot_plan
     return jax.shard_map(local, mesh=mesh, in_specs=in_specs, out_specs=out_specs, check_vma=False)

time: 294 us -> 91.3 us (0.31)
  waiting for transfers between devices: 202 us -> 50 us
  blocking collectives: 48.2 us -> 0 us
  starting transfers between devices: 5.76 us -> 25.5 us
  matrix products: 13.7 us -> 0.32 us
  between operations: 14 us -> 0.77 us
  Pallas kernels: 0 us -> 11.6 us
  other arithmetic: 7.77 us -> 2.71 us
    all_gather x3 -> x0, waiting for transfers between devices: 134 us -> none  [the longest x1 52 us: local(): lax.all_gather(up_weight, 'dp', axis=1, tiled=True)]
    ppermute x0 -> x27, waiting for transfers between devices: none -> 50 us  [swap(): return lax.ppermute(block, AXES, [(i, i ^ mask) for i in range(count)])]
    reduce_scatter x1 -> x0, waiting for transfers between devices: 49.8 us -> none  [local(): lax.psum_scatter(lax.dot_general(hidden, arrived_grad, over_tokens, prefe...]
    all_to_all x2 -> x0, blocking collectives: 48.2 us -> none  [the longest x1 25.4 us: local(): lax.all_to_all(outgoing.reshape(experts, capacity, model_width), 'expert'...]
    ppermute x0 -> x27, starting transfers between devices: none -> 25.5 us  [swap(): return lax.ppermute(block, AXES, [(i, i ^ mask) for i in range(count)])]
    all_to_all x1 -> x0, waiting for transfers between devices: 16.5 us -> none  [local(): lax.all_to_all(outputs.reshape(experts, capacity, model_width), 'expert',...]
    dot_general x6 -> x2, matrix products: 13.7 us -> 0.32 us  [the longest x1 0.19 us: dense_plan(): jnp.dot(pick, tokens, preferred_element_type=jnp.float32)]
    pallas_call x0 -> x2, Pallas kernels: none -> 11.6 us  [the longest x1 5.98 us: expert_terms(): pl.pallas_call(expert_kernel, out_shape=[half, half, jax.ShapeDtypeStruct...]
  transfers between devices with their start and end apart: 5 -> 27, of which waited for: 5 -> 20; matrix products, arithmetic and copies ran while one was open for 3% -> 0% of each run, Pallas kernels for 0% -> 0%
where the time goes in v3:
time: 91.3 us; the launch traced here: 91.1 us
  waiting for transfers between devices  50 us (55%)
  starting transfers between devices  25.5 us (28%)
  Pallas kernels  11.6 us (13%)
  other arithmetic  2.71 us (3%)
    ppermute x27, waiting for transfers between devices, swap(): return lax.ppermute(block, AXES, [(i, i ^ mask) for i in range(count)])  50 us
    ppermute x27, starting transfers between devices, swap(): return lax.ppermute(block, AXES, [(i, i ^ mask) for i in range(count)])  25.5 us
    pallas_call x1, Pallas kernels, expert_terms(): pl.pallas_call(expert_kernel, out_shape=[half, half, jax.ShapeDtypeStruct...  5.98 us
    pallas_call x1, Pallas kernels, update(): pl.pallas_call(functools.partial(update_kernel, BLOCK), grid=(width // BL...  5.61 us
  transfers between devices with their start and end apart: 27, of which 20 were waited for; matrix products, arithmetic and copies ran while one was open for 0% of the time, Pallas kernels for 0%

profile of v3, /device:TPU:0, one launch (start us, length us, event | category | flops | bytes accessed | tf_op | source)
XLA Modules:
  0.0 91.1 jit_solution(8152126878161709654)
XLA Ops:
  0.6 0.0 copy-start
  0.7 0.8 compare_reduce_fusion
  1.4 0.1 copy.17
  1.6 0.2 reduce-window.8
  1.7 0.1 reduce.1
  1.8 1.0 %fusion.4 = bf16[128,128]{1,0:T(8,128)(2,1)S(1)} fusion(s32[128,6]{0,1:T(8,128)} %param.9, pred[128]{0:T(512)(128)(4,1)S(1)} %iota_compare_fusion.2, bf16[128,6]{0,1:T(8,128)(2,1)} %param.10), kind=kLoop, calls=%fused_computation.11 | loop fusion | flops 376832 | bytes 37504 | tf_op jit(solution)/shard_map/reduce_sum | solution.py:305
  2.8 0.1 convolution_convert_fusion.1
  2.9 0.2 convolution_convert_fusion
  3.2 5.1 %collective-permute-start.2 = (bf16[12,2688]{1,0:T(8,128)(2,1)S(1)}, bf16[12,2688]{1,0:T(8,128)(2,1)S(1)}, u32[]{:S(2)}, u32[]{:S(2)}) collective-permute-start(bf16[12,2688]{1,0:T(8,128)(2,1)S(1)} %pad_maximum_fusion.2), channel_id=1, source_target_pairs={{0,12},{1,13},{2,14},{3,15},{4,8},{5,9},{6,10},{7,11},{8,4},{9,5},... | collective-permute-start | bytes 193544 | tf_op jit(solution)/shard_map/ppermute | solution.py:150
  8.3 0.6 collective-permute-start
  8.9 2.6 %collective-permute-done.2 = bf16[12,2688]{1,0:T(8,128)(2,1)S(1)} collective-permute-done((bf16[12,2688]{1,0:T(8,128)(2,1)S(1)}, bf16[12,2688]{1,0:T(8,128)(2,1)S(1)}, u32[]{:S(2)}, u32[]{:S(2)}) %collective-permute-start.2) | collective-permute-done | bytes 64544 | tf_op jit(solution)/shard_map/ppermute | solution.py:150
  11.5 4.0 %collective-permute-done.1 = bf16[12,2688]{1,0:T(8,128)(2,1)S(1)} collective-permute-done((bf16[12,2688]{1,0:T(8,128)(2,1)S(1)}, bf16[12,2688]{1,0:T(8,128)(2,1)S(1)}, u32[]{:S(2)}, u32[]{:S(2)}) %collective-permute-start.1) | collective-permute-done | bytes 64544 | tf_op jit(solution)/shard_map/ppermute | solution.py:150
  15.5 0.0 collective-permute-done
  15.5 0.1 pad_maximum_fusion.refs_0_
  15.6 2.5 %collective-permute-start.5 = (bf16[48,2688]{1,0:T(8,128)(2,1)S(1)}, bf16[48,2688]{1,0:T(8,128)(2,1)S(1)}, u32[]{:S(2)}, u32[]{:S(2)}) collective-permute-start(bf16[48,2688]{1,0:T(8,128)(2,1)S(1)} %pad_maximum_fusion.refs_0_), channel_id=1, source_target_pairs={{0,18},{1,19},{2,16},{3,17},{4,22},{5,23},{6,20},{7,21},{8,26},{9,... | collective-permute-start | bytes 774152 | tf_op jit(solution)/shard_map/ppermute | solution.py:150
  18.1 0.5 collective-permute-start.4
  18.6 0.5 collective-permute-start.3
  19.1 0.0 collective-permute-start.6
  19.1 6.6 %collective-permute-done.5.refs_3_ = bf16[48,2688]{1,0:T(8,128)(2,1)S(1)} collective-permute-done((bf16[48,2688]{1,0:T(8,128)(2,1)S(1)}, bf16[48,2688]{1,0:T(8,128)(2,1)S(1)}, u32[]{:S(2)}, u32[]{:S(2)}) %collective-permute-start.5) | collective-permute-done | bytes 258080 | tf_op jit(solution)/shard_map/ppermute | solution.py:150
  25.8 3.7 %collective-permute-done.4.refs_2_ = bf16[48,2688]{1,0:T(8,128)(2,1)S(1)} collective-permute-done((bf16[48,2688]{1,0:T(8,128)(2,1)S(1)}, bf16[48,2688]{1,0:T(8,128)(2,1)S(1)}, u32[]{:S(2)}, u32[]{:S(2)}) %collective-permute-start.4) | collective-permute-done | bytes 258080 | tf_op jit(solution)/shard_map/ppermute | solution.py:150
  29.4 0.0 collective-permute-start.8
  29.4 0.2 collective-permute-done.3.refs_1_
  29.6 0.3 collective-permute-start.7
  29.9 0.0 collective-permute-done.9.refs_7_
  29.9 1.0 %collective-permute-done.8.refs_6_ = bf16[48,2688]{1,0:T(8,128)(2,1)S(1)} collective-permute-done((bf16[48,2688]{1,0:T(8,128)(2,1)S(1)}, bf16[48,2688]{1,0:T(8,128)(2,1)S(1)}, u32[]{:S(2)}, u32[]{:S(2)}) %collective-permute-start.8) | collective-permute-done | bytes 258080 | tf_op jit(solution)/shard_map/ppermute | solution.py:150
  31.0 0.4 collective-permute-done.7.refs_5_
  31.3 6.0 %expert_terms.1 = (bf16[192,2560]{1,0:T(8,128)(2,1)S(1)}, bf16[192,2560]{1,0:T(8,128)(2,1)S(1)}, bf16[384,384]{1,0:T(8,128)(2,1)S(1)}) custom-call(bf16[48,2688]{1,0:T(8,128)(2,1)S(1)} %pad_maximum_fusion.refs_0_, bf16[48,2688]{1,0:T(8,128)(2,1)S(1)} %collective-permute-done.3.refs_1_, bf16[48,2688]{1,0:T(8,128)(2,1)S(1)} %collective-permute-done.4.refs_2_, ...), custom_call_target="tpu_custom_call" | custom-call | flops 2264924160 | bytes 9830400 | tf_op jit(solution)/shard_map/expert_terms/pallas_call | solution.py:233
  37.3 0.2 collective-permute-start.10
  37.5 2.4 %collective-permute-done.10 = bf16[192,2560]{1,0:T(8,128)(2,1)S(1)} collective-permute-done((bf16[192,2560]{1,0:T(8,128)(2,1)S(1)}, bf16[192,2560]{1,0:T(8,128)(2,1)S(1)}, u32[]{:S(2)}, u32[]{:S(2)}) %collective-permute-start.10) | collective-permute-done | bytes 983072 | tf_op jit(solution)/shard_map/ppermute | solution.py:150
  39.9 0.3 convert_add_fusion
  40.3 0.0 copy-start.2
  40.3 0.1 fusion.20
  40.3 0.0 copy-start.1
  40.3 1.7 %collective-permute-start.11 = (bf16[48,2560]{1,0:T(8,128)(2,1)S(1)}, bf16[48,2560]{1,0:T(8,128)(2,1)S(1)}, u32[]{:S(2)}, u32[]{:S(2)}) collective-permute-start(bf16[48,2560]{1,0:T(8,128)(2,1)S(1)} %get-tuple-element.19), channel_id=1, source_target_pairs={{0,2},{1,3},{2,0},{3,1},{4,6},{5,7},{6,4},{7,5},{8,10},{9,11},{10,... | collective-permute-start | bytes 737288 | tf_op jit(solution)/shard_map/ppermute | solution.py:150
  42.0 1.5 %collective-permute-start.13 = (bf16[48,2560]{1,0:T(8,128)(2,1)S(1)}, bf16[48,2560]{1,0:T(8,128)(2,1)S(1)}, u32[]{:S(2)}, u32[]{:S(2)}) collective-permute-start(bf16[48,2560]{1,0:T(8,128)(2,1)S(1)} %get-tuple-element.20), channel_id=1, source_target_pairs={{0,18},{1,19},{2,16},{3,17},{4,22},{5,23},{6,20},{7,21},{8,26},{9,... | collective-permute-start | bytes 737288 | tf_op jit(solution)/shard_map/ppermute | solution.py:150
  43.5 0.4 collective-permute-start.12
  43.9 5.3 %collective-permute-done.11 = bf16[48,2560]{1,0:T(8,128)(2,1)S(1)} collective-permute-done((bf16[48,2560]{1,0:T(8,128)(2,1)S(1)}, bf16[48,2560]{1,0:T(8,128)(2,1)S(1)}, u32[]{:S(2)}, u32[]{:S(2)}) %collective-permute-start.11) | collective-permute-done | bytes 245792 | tf_op jit(solution)/shard_map/ppermute | solution.py:150
  49.2 5.6 %collective-permute-done.13 = bf16[48,2560]{1,0:T(8,128)(2,1)S(1)} collective-permute-done((bf16[48,2560]{1,0:T(8,128)(2,1)S(1)}, bf16[48,2560]{1,0:T(8,128)(2,1)S(1)}, u32[]{:S(2)}, u32[]{:S(2)}) %collective-permute-start.13) | collective-permute-done | bytes 245792 | tf_op jit(solution)/shard_map/ppermute | solution.py:150
  54.9 1.4 %collective-permute-done.12 = bf16[48,2560]{1,0:T(8,128)(2,1)S(1)} collective-permute-done((bf16[48,2560]{1,0:T(8,128)(2,1)S(1)}, bf16[48,2560]{1,0:T(8,128)(2,1)S(1)}, u32[]{:S(2)}, u32[]{:S(2)}) %collective-permute-start.12) | collective-permute-done | bytes 245792 | tf_op jit(solution)/shard_map/ppermute | solution.py:150
  56.2 0.1 fusion.18
  56.4 0.4 collective-permute-start.14
  56.8 2.0 %collective-permute-start.16 = (bf16[12,2560]{1,0:T(8,128)(2,1)S(1)}, bf16[12,2560]{1,0:T(8,128)(2,1)S(1)}, u32[]{:S(2)}, u32[]{:S(2)}) collective-permute-start(bf16[12,2560]{1,0:T(8,128)(2,1)S(1)} %get-tuple-element.23), channel_id=1, source_target_pairs={{0,12},{1,13},{2,14},{3,15},{4,8},{5,9},{6,10},{7,11},{8,4},{9,5},... | collective-permute-start | bytes 184328 | tf_op jit(solution)/shard_map/ppermute | solution.py:150
  58.7 1.2 %collective-permute-start.15 = (bf16[12,2560]{1,0:T(8,128)(2,1)S(1)}, bf16[12,2560]{1,0:T(8,128)(2,1)S(1)}, u32[]{:S(2)}, u32[]{:S(2)}) collective-permute-start(bf16[12,2560]{1,0:T(8,128)(2,1)S(1)} %get-tuple-element.24), channel_id=1, source_target_pairs={{0,8},{1,9},{2,10},{3,11},{4,12},{5,13},{6,14},{7,15},{8,0},{9,1},... | collective-permute-start | bytes 184328 | tf_op jit(solution)/shard_map/ppermute | solution.py:150
  60.0 1.7 %collective-permute-done.14 = bf16[12,2560]{1,0:T(8,128)(2,1)S(1)} collective-permute-done((bf16[12,2560]{1,0:T(8,128)(2,1)S(1)}, bf16[12,2560]{1,0:T(8,128)(2,1)S(1)}, u32[]{:S(2)}, u32[]{:S(2)}) %collective-permute-start.14) | collective-permute-done | bytes 61472 | tf_op jit(solution)/shard_map/ppermute | solution.py:150
  61.6 1.5 %collective-permute-done.16 = bf16[12,2560]{1,0:T(8,128)(2,1)S(1)} collective-permute-done((bf16[12,2560]{1,0:T(8,128)(2,1)S(1)}, bf16[12,2560]{1,0:T(8,128)(2,1)S(1)}, u32[]{:S(2)}, u32[]{:S(2)}) %collective-permute-start.16) | collective-permute-done | bytes 61472 | tf_op jit(solution)/shard_map/ppermute | solution.py:150
  63.1 2.5 %collective-permute-done.15 = bf16[12,2560]{1,0:T(8,128)(2,1)S(1)} collective-permute-done((bf16[12,2560]{1,0:T(8,128)(2,1)S(1)}, bf16[12,2560]{1,0:T(8,128)(2,1)S(1)}, u32[]{:S(2)}, u32[]{:S(2)}) %collective-permute-start.15) | collective-permute-done | bytes 61472 | tf_op jit(solution)/shard_map/ppermute | solution.py:150
  65.6 0.1 fusion.9
  65.7 2.7 %collective-permute-start.19 = (bf16[12,2560]{1,0:T(8,128)(2,1)S(1)}, bf16[12,2560]{1,0:T(8,128)(2,1)S(1)}, u32[]{:S(2)}, u32[]{:S(2)}) collective-permute-start(bf16[12,2560]{1,0:T(8,128)(2,1)S(1)} %fusion.9), channel_id=1, source_target_pairs={{0,12},{1,13},{2,14},{3,15},{4,8},{5,9},{6,10},{7,11},{8,4},{9,5},... | collective-permute-start | bytes 184328 | tf_op jit(solution)/shard_map/ppermute | solution.py:150
  68.4 0.0 collective-permute-start.18
  68.4 1.8 %collective-permute-start.17 = (bf16[12,2560]{1,0:T(8,128)(2,1)S(1)}, bf16[12,2560]{1,0:T(8,128)(2,1)S(1)}, u32[]{:S(2)}, u32[]{:S(2)}) collective-permute-start(bf16[12,2560]{1,0:T(8,128)(2,1)S(1)} %fusion.9), channel_id=1, source_target_pairs={{0,4},{1,5},{2,6},{3,7},{4,0},{5,1},{6,2},{7,3},{8,12},{9,13},{10,... | collective-permute-start | bytes 184328 | tf_op jit(solution)/shard_map/ppermute | solution.py:150
  70.1 1.9 %collective-permute-done.19 = bf16[12,2560]{1,0:T(8,128)(2,1)S(1)} collective-permute-done((bf16[12,2560]{1,0:T(8,128)(2,1)S(1)}, bf16[12,2560]{1,0:T(8,128)(2,1)S(1)}, u32[]{:S(2)}, u32[]{:S(2)}) %collective-permute-start.19) | collective-permute-done | bytes 61472 | tf_op jit(solution)/shard_map/ppermute | solution.py:150
  72.0 1.7 %collective-permute-done.18 = bf16[12,2560]{1,0:T(8,128)(2,1)S(1)} collective-permute-done((bf16[12,2560]{1,0:T(8,128)(2,1)S(1)}, bf16[12,2560]{1,0:T(8,128)(2,1)S(1)}, u32[]{:S(2)}, u32[]{:S(2)}) %collective-permute-start.18) | collective-permute-done | bytes 61472 | tf_op jit(solution)/shard_map/ppermute | solution.py:150
  73.7 0.0 collective-permute-done.17
  73.7 0.1 pad_maximum_fusion.1.refs_0_
  73.8 1.5 %collective-permute-start.22 = (bf16[48,2560]{1,0:T(8,128)(2,1)S(1)}, bf16[48,2560]{1,0:T(8,128)(2,1)S(1)}, u32[]{:S(2)}, u32[]{:S(2)}) collective-permute-start(bf16[48,2560]{1,0:T(8,128)(2,1)S(1)} %pad_maximum_fusion.1.refs_0_), channel_id=1, source_target_pairs={{0,18},{1,19},{2,16},{3,17},{4,22},{5,23},{6,20},{7,21},{8,26},{9,... | collective-permute-start | bytes 737288 | tf_op jit(solution)/shard_map/ppermute | solution.py:150
  75.3 0.8 collective-permute-start.21
  76.1 1.3 %collective-permute-start.20 = (bf16[48,2560]{1,0:T(8,128)(2,1)S(1)}, bf16[48,2560]{1,0:T(8,128)(2,1)S(1)}, u32[]{:S(2)}, u32[]{:S(2)}) collective-permute-start(bf16[48,2560]{1,0:T(8,128)(2,1)S(1)} %pad_maximum_fusion.1.refs_0_), channel_id=1, source_target_pairs={{0,2},{1,3},{2,0},{3,1},{4,6},{5,7},{6,4},{7,5},{8,10},{9,11},{10,... | collective-permute-start | bytes 737288 | tf_op jit(solution)/shard_map/ppermute | solution.py:150
  77.4 0.0 collective-permute-start.23
  77.4 3.7 %collective-permute-done.22.refs_3_ = bf16[48,2560]{1,0:T(8,128)(2,1)S(1)} collective-permute-done((bf16[48,2560]{1,0:T(8,128)(2,1)S(1)}, bf16[48,2560]{1,0:T(8,128)(2,1)S(1)}, u32[]{:S(2)}, u32[]{:S(2)}) %collective-permute-start.22) | collective-permute-done | bytes 245792 | tf_op jit(solution)/shard_map/ppermute | solution.py:150
  81.1 2.5 %collective-permute-done.21.refs_2_ = bf16[48,2560]{1,0:T(8,128)(2,1)S(1)} collective-permute-done((bf16[48,2560]{1,0:T(8,128)(2,1)S(1)}, bf16[48,2560]{1,0:T(8,128)(2,1)S(1)}, u32[]{:S(2)}, u32[]{:S(2)}) %collective-permute-start.21) | collective-permute-done | bytes 245792 | tf_op jit(solution)/shard_map/ppermute | solution.py:150
  83.6 0.5 collective-permute-start.24
  84.1 1.0 %collective-permute-done.25.refs_6_ = bf16[48,2560]{1,0:T(8,128)(2,1)S(1)} collective-permute-done((bf16[48,2560]{1,0:T(8,128)(2,1)S(1)}, bf16[48,2560]{1,0:T(8,128)(2,1)S(1)}, u32[]{:S(2)}, u32[]{:S(2)}) %collective-permute-start.25) | collective-permute-done | bytes 245792 | tf_op jit(solution)/shard_map/ppermute | solution.py:150
  85.1 0.4 collective-permute-done.24.refs_5_
  85.5 5.6 %update.1 = (bf16[384,2560]{1,0:T(8,128)(2,1)}, bf16[384,2560]{1,0:T(8,128)(2,1)}, bf16[384,2560]{1,0:T(8,128)(2,1)}) custom-call(bf16[48,2560]{1,0:T(8,128)(2,1)S(1)} %pad_maximum_fusion.1.refs_0_, bf16[48,2560]{1,0:T(8,128)(2,1)S(1)} %collective-permute-done.20.refs_1_, bf16[48,2560]{1,0:T(8,128)(2,1)S(1)} %collective-permute-done.21.refs_2_, ...), custom_call_target="tpu_custom_call" | custom-call | flops 754974720 | bytes 13762560 | tf_op jit(solution)/shard_map/update/pallas_call | solution.py:275
  (18 shorter events, 0.1 us)
Async XLA Ops:
  0.6 2.3 %copy-start = (bf16[128,2560]{1,0:T(8,128)(2,1)S(1)}, bf16[128,2560]{1,0:T(8,128)(2,1)}, u32[]{:S(2)}) copy-start(bf16[128,2560]{1,0:T(8,128)(2,1)} %param.8) | copy-start | bytes 1966084
  3.2 8.3 %collective-permute-start.2 = (bf16[12,2688]{1,0:T(8,128)(2,1)S(1)}, bf16[12,2688]{1,0:T(8,128)(2,1)S(1)}, u32[]{:S(2)}, u32[]{:S(2)}) collective-permute-start(bf16[12,2688]{1,0:T(8,128)(2,1)S(1)} %pad_maximum_fusion.2), channel_id=1, source_target_pairs={{0,12},{1,13},{2,14},{3,15},{4,8},{5,9},{6,10},{7,11},{8,4},{9,5},... | collective-permute-start | bytes 193544 | tf_op jit(solution)/shard_map/ppermute | solution.py:150
  8.3 7.2 %collective-permute-start.1 = (bf16[12,2688]{1,0:T(8,128)(2,1)S(1)}, bf16[12,2688]{1,0:T(8,128)(2,1)S(1)}, u32[]{:S(2)}, u32[]{:S(2)}) collective-permute-start(bf16[12,2688]{1,0:T(8,128)(2,1)S(1)} %pad_maximum_fusion.2), channel_id=1, source_target_pairs={{0,8},{1,9},{2,10},{3,11},{4,12},{5,13},{6,14},{7,15},{8,0},{9,1},... | collective-permute-start | bytes 193544 | tf_op jit(solution)/shard_map/ppermute | solution.py:150
  8.3 7.2 %collective-permute-start = (bf16[12,2688]{1,0:T(8,128)(2,1)S(1)}, bf16[12,2688]{1,0:T(8,128)(2,1)S(1)}, u32[]{:S(2)}, u32[]{:S(2)}) collective-permute-start(bf16[12,2688]{1,0:T(8,128)(2,1)S(1)} %pad_maximum_fusion.2), channel_id=1, source_target_pairs={{0,4},{1,5},{2,6},{3,7},{4,0},{5,1},{6,2},{7,3},{8,12},{9,13},{10,... | collective-permute-start | bytes 193544 | tf_op jit(solution)/shard_map/ppermute | solution.py:150
  15.6 10.2 %collective-permute-start.5 = (bf16[48,2688]{1,0:T(8,128)(2,1)S(1)}, bf16[48,2688]{1,0:T(8,128)(2,1)S(1)}, u32[]{:S(2)}, u32[]{:S(2)}) collective-permute-start(bf16[48,2688]{1,0:T(8,128)(2,1)S(1)} %pad_maximum_fusion.refs_0_), channel_id=1, source_target_pairs={{0,18},{1,19},{2,16},{3,17},{4,22},{5,23},{6,20},{7,21},{8,26},{9,... | collective-permute-start | bytes 774152 | tf_op jit(solution)/shard_map/ppermute | solution.py:150
  18.1 11.3 %collective-permute-start.4 = (bf16[48,2688]{1,0:T(8,128)(2,1)S(1)}, bf16[48,2688]{1,0:T(8,128)(2,1)S(1)}, u32[]{:S(2)}, u32[]{:S(2)}) collective-permute-start(bf16[48,2688]{1,0:T(8,128)(2,1)S(1)} %pad_maximum_fusion.refs_0_), channel_id=1, source_target_pairs={{0,16},{1,17},{2,18},{3,19},{4,20},{5,21},{6,22},{7,23},{8,24},{9,... | collective-permute-start | bytes 774152 | tf_op jit(solution)/shard_map/ppermute | solution.py:150
  18.6 11.0 %collective-permute-start.3 = (bf16[48,2688]{1,0:T(8,128)(2,1)S(1)}, bf16[48,2688]{1,0:T(8,128)(2,1)S(1)}, u32[]{:S(2)}, u32[]{:S(2)}) collective-permute-start(bf16[48,2688]{1,0:T(8,128)(2,1)S(1)} %pad_maximum_fusion.refs_0_), channel_id=1, source_target_pairs={{0,2},{1,3},{2,0},{3,1},{4,6},{5,7},{6,4},{7,5},{8,10},{9,11},{10,... | collective-permute-start | bytes 774152 | tf_op jit(solution)/shard_map/ppermute | solution.py:150
  19.1 10.8 %collective-permute-start.6 = (bf16[48,2688]{1,0:T(8,128)(2,1)S(1)}, bf16[48,2688]{1,0:T(8,128)(2,1)S(1)}, u32[]{:S(2)}, u32[]{:S(2)}) collective-permute-start(bf16[48,2688]{1,0:T(8,128)(2,1)S(1)} %pad_maximum_fusion.refs_0_), channel_id=1, source_target_pairs={{0,1},{1,0},{2,3},{3,2},{4,5},{5,4},{6,7},{7,6},{8,9},{9,8},{10,11... | collective-permute-start | bytes 774152 | tf_op jit(solution)/shard_map/ppermute | solution.py:150
  25.8 4.2 %collective-permute-start.9 = (bf16[48,2688]{1,0:T(8,128)(2,1)S(1)}, bf16[48,2688]{1,0:T(8,128)(2,1)S(1)}, u32[]{:S(2)}, u32[]{:S(2)}) collective-permute-start(bf16[48,2688]{1,0:T(8,128)(2,1)S(1)} %collective-permute-done.5.refs_3_), channel_id=1, source_target_pairs={{0,1},{1,0},{2,3},{3,2},{4,5},{5,4},{6,7},{7,6},{8,9},{9,8},{10,11... | collective-permute-start | bytes 774152 | tf_op jit(solution)/shard_map/ppermute | solution.py:150
  29.4 1.5 %collective-permute-start.8 = (bf16[48,2688]{1,0:T(8,128)(2,1)S(1)}, bf16[48,2688]{1,0:T(8,128)(2,1)S(1)}, u32[]{:S(2)}, u32[]{:S(2)}) collective-permute-start(bf16[48,2688]{1,0:T(8,128)(2,1)S(1)} %collective-permute-done.4.refs_2_), channel_id=1, source_target_pairs={{0,1},{1,0},{2,3},{3,2},{4,5},{5,4},{6,7},{7,6},{8,9},{9,8},{10,11... | collective-permute-start | bytes 774152 | tf_op jit(solution)/shard_map/ppermute | solution.py:150
  29.6 1.7 %collective-permute-start.7 = (bf16[48,2688]{1,0:T(8,128)(2,1)S(1)}, bf16[48,2688]{1,0:T(8,128)(2,1)S(1)}, u32[]{:S(2)}, u32[]{:S(2)}) collective-permute-start(bf16[48,2688]{1,0:T(8,128)(2,1)S(1)} %collective-permute-done.3.refs_1_), channel_id=1, source_target_pairs={{0,1},{1,0},{2,3},{3,2},{4,5},{5,4},{6,7},{7,6},{8,9},{9,8},{10,11... | collective-permute-start | bytes 774152 | tf_op jit(solution)/shard_map/ppermute | solution.py:150
  37.3 2.6 %collective-permute-start.10 = (bf16[192,2560]{1,0:T(8,128)(2,1)S(1)}, bf16[192,2560]{1,0:T(8,128)(2,1)S(1)}, u32[]{:S(2)}, u32[]{:S(2)}) collective-permute-start(bf16[192,2560]{1,0:T(8,128)(2,1)S(1)} %get-tuple-element.10), channel_id=1, source_target_pairs={{0,1},{1,0},{2,3},{3,2},{4,5},{5,4},{6,7},{7,6},{8,9},{9,8},{10,11... | collective-permute-start | bytes 2949128 | tf_op jit(solution)/shard_map/ppermute | solution.py:150
  39.9 45.5 %copy-start.3 = (bf16[1,384,2560]{2,1,0:T(8,128)(2,1)S(1)}, bf16[1,384,2560]{2,1,0:T(8,128)(2,1)}, u32[]{:S(2)}) copy-start(bf16[1,384,2560]{2,1,0:T(8,128)(2,1)} %param.15) | copy-start | bytes 5898244
  40.3 45.2 %copy-start.2 = (bf16[1,384,2560]{2,1,0:T(8,128)(2,1)S(1)}, bf16[1,384,2560]{2,1,0:T(8,128)(2,1)}, u32[]{:S(2)}) copy-start(bf16[1,384,2560]{2,1,0:T(8,128)(2,1)} %param.14) | copy-start | bytes 5898244
  40.3 45.2 %copy-start.1 = (bf16[1,384,2560]{2,1,0:T(8,128)(2,1)S(1)}, bf16[1,384,2560]{2,1,0:T(8,128)(2,1)}, u32[]{:S(2)}) copy-start(bf16[1,384,2560]{2,1,0:T(8,128)(2,1)} %param.13) | copy-start | bytes 5898244
  40.3 8.9 %collective-permute-start.11 = (bf16[48,2560]{1,0:T(8,128)(2,1)S(1)}, bf16[48,2560]{1,0:T(8,128)(2,1)S(1)}, u32[]{:S(2)}, u32[]{:S(2)}) collective-permute-start(bf16[48,2560]{1,0:T(8,128)(2,1)S(1)} %get-tuple-element.19), channel_id=1, source_target_pairs={{0,2},{1,3},{2,0},{3,1},{4,6},{5,7},{6,4},{7,5},{8,10},{9,11},{10,... | collective-permute-start | bytes 737288 | tf_op jit(solution)/shard_map/ppermute | solution.py:150
  42.0 12.9 %collective-permute-start.13 = (bf16[48,2560]{1,0:T(8,128)(2,1)S(1)}, bf16[48,2560]{1,0:T(8,128)(2,1)S(1)}, u32[]{:S(2)}, u32[]{:S(2)}) collective-permute-start(bf16[48,2560]{1,0:T(8,128)(2,1)S(1)} %get-tuple-element.20), channel_id=1, source_target_pairs={{0,18},{1,19},{2,16},{3,17},{4,22},{5,23},{6,20},{7,21},{8,26},{9,... | collective-permute-start | bytes 737288 | tf_op jit(solution)/shard_map/ppermute | solution.py:150
  43.5 12.7 %collective-permute-start.12 = (bf16[48,2560]{1,0:T(8,128)(2,1)S(1)}, bf16[48,2560]{1,0:T(8,128)(2,1)S(1)}, u32[]{:S(2)}, u32[]{:S(2)}) collective-permute-start(bf16[48,2560]{1,0:T(8,128)(2,1)S(1)} %get-tuple-element.21), channel_id=1, source_target_pairs={{0,16},{1,17},{2,18},{3,19},{4,20},{5,21},{6,22},{7,23},{8,24},{9,... | collective-permute-start | bytes 737288 | tf_op jit(solution)/shard_map/ppermute | solution.py:150
  56.4 5.2 %collective-permute-start.14 = (bf16[12,2560]{1,0:T(8,128)(2,1)S(1)}, bf16[12,2560]{1,0:T(8,128)(2,1)S(1)}, u32[]{:S(2)}, u32[]{:S(2)}) collective-permute-start(bf16[12,2560]{1,0:T(8,128)(2,1)S(1)} %get-tuple-element.22), channel_id=1, source_target_pairs={{0,4},{1,5},{2,6},{3,7},{4,0},{5,1},{6,2},{7,3},{8,12},{9,13},{10,... | collective-permute-start | bytes 184328 | tf_op jit(solution)/shard_map/ppermute | solution.py:150
  56.8 6.3 %collective-permute-start.16 = (bf16[12,2560]{1,0:T(8,128)(2,1)S(1)}, bf16[12,2560]{1,0:T(8,128)(2,1)S(1)}, u32[]{:S(2)}, u32[]{:S(2)}) collective-permute-start(bf16[12,2560]{1,0:T(8,128)(2,1)S(1)} %get-tuple-element.23), channel_id=1, source_target_pairs={{0,12},{1,13},{2,14},{3,15},{4,8},{5,9},{6,10},{7,11},{8,4},{9,5},... | collective-permute-start | bytes 184328 | tf_op jit(solution)/shard_map/ppermute | solution.py:150
  58.7 6.9 %collective-permute-start.15 = (bf16[12,2560]{1,0:T(8,128)(2,1)S(1)}, bf16[12,2560]{1,0:T(8,128)(2,1)S(1)}, u32[]{:S(2)}, u32[]{:S(2)}) collective-permute-start(bf16[12,2560]{1,0:T(8,128)(2,1)S(1)} %get-tuple-element.24), channel_id=1, source_target_pairs={{0,8},{1,9},{2,10},{3,11},{4,12},{5,13},{6,14},{7,15},{8,0},{9,1},... | collective-permute-start | bytes 184328 | tf_op jit(solution)/shard_map/ppermute | solution.py:150
  65.7 6.3 %collective-permute-start.19 = (bf16[12,2560]{1,0:T(8,128)(2,1)S(1)}, bf16[12,2560]{1,0:T(8,128)(2,1)S(1)}, u32[]{:S(2)}, u32[]{:S(2)}) collective-permute-start(bf16[12,2560]{1,0:T(8,128)(2,1)S(1)} %fusion.9), channel_id=1, source_target_pairs={{0,12},{1,13},{2,14},{3,15},{4,8},{5,9},{6,10},{7,11},{8,4},{9,5},... | collective-permute-start | bytes 184328 | tf_op jit(solution)/shard_map/ppermute | solution.py:150
  68.4 5.4 %collective-permute-start.18 = (bf16[12,2560]{1,0:T(8,128)(2,1)S(1)}, bf16[12,2560]{1,0:T(8,128)(2,1)S(1)}, u32[]{:S(2)}, u32[]{:S(2)}) collective-permute-start(bf16[12,2560]{1,0:T(8,128)(2,1)S(1)} %fusion.9), channel_id=1, source_target_pairs={{0,8},{1,9},{2,10},{3,11},{4,12},{5,13},{6,14},{7,15},{8,0},{9,1},... | collective-permute-start | bytes 184328 | tf_op jit(solution)/shard_map/ppermute | solution.py:150
  68.4 5.4 %collective-permute-start.17 = (bf16[12,2560]{1,0:T(8,128)(2,1)S(1)}, bf16[12,2560]{1,0:T(8,128)(2,1)S(1)}, u32[]{:S(2)}, u32[]{:S(2)}) collective-permute-start(bf16[12,2560]{1,0:T(8,128)(2,1)S(1)} %fusion.9), channel_id=1, source_target_pairs={{0,4},{1,5},{2,6},{3,7},{4,0},{5,1},{6,2},{7,3},{8,12},{9,13},{10,... | collective-permute-start | bytes 184328 | tf_op jit(solution)/shard_map/ppermute | solution.py:150
  73.8 7.3 %collective-permute-start.22 = (bf16[48,2560]{1,0:T(8,128)(2,1)S(1)}, bf16[48,2560]{1,0:T(8,128)(2,1)S(1)}, u32[]{:S(2)}, u32[]{:S(2)}) collective-permute-start(bf16[48,2560]{1,0:T(8,128)(2,1)S(1)} %pad_maximum_fusion.1.refs_0_), channel_id=1, source_target_pairs={{0,18},{1,19},{2,16},{3,17},{4,22},{5,23},{6,20},{7,21},{8,26},{9,... | collective-permute-start | bytes 737288 | tf_op jit(solution)/shard_map/ppermute | solution.py:150
  75.3 8.3 %collective-permute-start.21 = (bf16[48,2560]{1,0:T(8,128)(2,1)S(1)}, bf16[48,2560]{1,0:T(8,128)(2,1)S(1)}, u32[]{:S(2)}, u32[]{:S(2)}) collective-permute-start(bf16[48,2560]{1,0:T(8,128)(2,1)S(1)} %pad_maximum_fusion.1.refs_0_), channel_id=1, source_target_pairs={{0,16},{1,17},{2,18},{3,19},{4,20},{5,21},{6,22},{7,23},{8,24},{9,... | collective-permute-start | bytes 737288 | tf_op jit(solution)/shard_map/ppermute | solution.py:150
  76.1 7.5 %collective-permute-start.20 = (bf16[48,2560]{1,0:T(8,128)(2,1)S(1)}, bf16[48,2560]{1,0:T(8,128)(2,1)S(1)}, u32[]{:S(2)}, u32[]{:S(2)}) collective-permute-start(bf16[48,2560]{1,0:T(8,128)(2,1)S(1)} %pad_maximum_fusion.1.refs_0_), channel_id=1, source_target_pairs={{0,2},{1,3},{2,0},{3,1},{4,6},{5,7},{6,4},{7,5},{8,10},{9,11},{10,... | collective-permute-start | bytes 737288 | tf_op jit(solution)/shard_map/ppermute | solution.py:150
  77.4 6.8 %collective-permute-start.23 = (bf16[48,2560]{1,0:T(8,128)(2,1)S(1)}, bf16[48,2560]{1,0:T(8,128)(2,1)S(1)}, u32[]{:S(2)}, u32[]{:S(2)}) collective-permute-start(bf16[48,2560]{1,0:T(8,128)(2,1)S(1)} %pad_maximum_fusion.1.refs_0_), channel_id=1, source_target_pairs={{0,1},{1,0},{2,3},{3,2},{4,5},{5,4},{6,7},{7,6},{8,9},{9,8},{10,11... | collective-permute-start | bytes 737288 | tf_op jit(solution)/shard_map/ppermute | solution.py:150
  81.1 3.0 %collective-permute-start.26 = (bf16[48,2560]{1,0:T(8,128)(2,1)S(1)}, bf16[48,2560]{1,0:T(8,128)(2,1)S(1)}, u32[]{:S(2)}, u32[]{:S(2)}) collective-permute-start(bf16[48,2560]{1,0:T(8,128)(2,1)S(1)} %collective-permute-done.22.refs_3_), channel_id=1, source_target_pairs={{0,1},{1,0},{2,3},{3,2},{4,5},{5,4},{6,7},{7,6},{8,9},{9,8},{10,11... | collective-permute-start | bytes 737288 | tf_op jit(solution)/shard_map/ppermute | solution.py:150
  83.6 1.5 %collective-permute-start.25 = (bf16[48,2560]{1,0:T(8,128)(2,1)S(1)}, bf16[48,2560]{1,0:T(8,128)(2,1)S(1)}, u32[]{:S(2)}, u32[]{:S(2)}) collective-permute-start(bf16[48,2560]{1,0:T(8,128)(2,1)S(1)} %collective-permute-done.21.refs_2_), channel_id=1, source_target_pairs={{0,1},{1,0},{2,3},{3,2},{4,5},{5,4},{6,7},{7,6},{8,9},{9,8},{10,11... | collective-permute-start | bytes 737288 | tf_op jit(solution)/shard_map/ppermute | solution.py:150
  83.6 1.9 %collective-permute-start.24 = (bf16[48,2560]{1,0:T(8,128)(2,1)S(1)}, bf16[48,2560]{1,0:T(8,128)(2,1)S(1)}, u32[]{:S(2)}, u32[]{:S(2)}) collective-permute-start(bf16[48,2560]{1,0:T(8,128)(2,1)S(1)} %collective-permute-done.20.refs_1_), channel_id=1, source_target_pairs={{0,1},{1,0},{2,3},{3,2},{4,5},{5,4},{6,7},{7,6},{8,9},{9,8},{10,11... | collective-permute-start | bytes 737288 | tf_op jit(solution)/shard_map/ppermute | solution.py:150

commit v4 on v3

--- a/solution.py
+++ b/solution.py
@@ -137,10 +137,13 @@
 AXES = ("dp", "expert")
 CORE = 1
 PLANE = (2, 16, 18)
-LINE = (4, 8, 12)
+LINE = (8, 4, 12)
 BLOCK = 512
-PARTS = 2
+UPDATE_BLOCK = 256
+PARTS = 4
 LIMIT = 48
+PACK_PARTS = 4
+PACK_LIMIT = 60
 LANES = 128
 MIB = 1024 * 1024
 
@@ -152,6 +155,10 @@
 
 def spread(block):
     block = jnp.concatenate([block] + [swap(block, mask) for mask in LINE], axis=0)
+    return across(block)
+
+
+def across(block):
     return [block] + [swap(block, mask) for mask in PLANE]
 
 
@@ -168,11 +175,75 @@
 
 def collect(own, other):
     total = add_parts(own, [swap(other, CORE)])
-    for masks in (PLANE, LINE):
-        parts = jnp.split(total, len(masks) + 1, axis=0)
-        sent = [swap(part.astype(jnp.bfloat16), mask) for part, mask in zip(parts[1:], masks)]
-        total = add_parts(parts[0], sent)
-    return total
+    parts = jnp.split(total, len(PLANE) + 1, axis=0)
+    sent = [swap(part.astype(jnp.bfloat16), mask) for part, mask in zip(parts[1:], PLANE)]
+    kept, sent = jnp.split(add_parts(parts[0], sent), 2, axis=0)
+    pair = add_parts(kept, [swap(sent.astype(jnp.bfloat16), LINE[1])]).astype(jnp.bfloat16)
+    mine, its = jnp.split(pair, 2, axis=0)
+    return add_parts(pair, [swap(jnp.concatenate([its, mine], axis=0), LINE[0])])
+
+
+def pack_kernel(experts, tokens_ref, ids_ref, gates_ref, out_ref, *scratch):
+    tokens_vm, ids_vm, gates_vm, sems = scratch
+    count, width = tokens_vm.shape
+    part = count // PACK_PARTS
+    loads = [
+        pltpu.make_async_copy(
+            tokens_ref.at[pl.ds(k * part, part)], tokens_vm.at[pl.ds(k * part, part)], sems.at[k]
+        )
+        for k in range(PACK_PARTS)
+    ]
+    ids_load = pltpu.make_async_copy(ids_ref, ids_vm, sems.at[PACK_PARTS])
+    gates_load = pltpu.make_async_copy(gates_ref, gates_vm, sems.at[PACK_PARTS + 1])
+    for load in [ids_load, gates_load] + loads:
+        load.start()
+    ids_load.wait()
+    gates_load.wait()
+    ids, values = ids_vm[...], gates_vm[...].astype(jnp.float32)
+    row = lax.broadcasted_iota(jnp.int32, (LANES, count), 0)
+    gates = jnp.zeros((LANES, count), jnp.float32)
+    hot = jnp.zeros((LANES, count), jnp.bool_)
+    for k in range(ids.shape[0]):
+        named = jnp.broadcast_to(ids[k : k + 1], row.shape)
+        gates += jnp.where((named == row) & (row < experts), values[k : k + 1], 0.0)
+        hot |= named < experts
+    source = lax.broadcasted_iota(jnp.int32, (count, count), 0)
+    target = lax.broadcasted_iota(jnp.int32, (count, count), 1)
+    before = jnp.where(source < target, 1.0, 0.0).astype(jnp.bfloat16)
+    marks = jnp.where(hot, 1.0, 0.0).astype(jnp.bfloat16)
+    rank = jnp.dot(marks, before, preferred_element_type=jnp.float32)
+    pick = jnp.where(hot & (rank.astype(jnp.int32) == row), 1.0, 0.0).astype(jnp.bfloat16)
+    rows = out_ref.shape[0]
+    pick = pick[: 16 * pl.cdiv(rows, 16)]
+    hot_gates = lax.dot_general(
+        pick,
+        gates.astype(jnp.bfloat16),
+        (((1,), (1,)), ((), ())),
+        preferred_element_type=jnp.float32,
+    )
+    out_ref[:, width:] = hot_gates[:rows].astype(jnp.bfloat16)
+    for load in loads:
+        load.wait()
+    hot_tokens = jnp.dot(pick, tokens_vm[...], preferred_element_type=jnp.float32)
+    out_ref[:, :width] = hot_tokens[:rows].astype(jnp.bfloat16)
+
+
+def pack(tokens, expert_ids, gate_values, experts):
+    in_vmem = pl.BlockSpec(memory_space=pltpu.VMEM)
+    return pl.pallas_call(
+        functools.partial(pack_kernel, experts),
+        out_shape=jax.ShapeDtypeStruct((experts * 3 // 4, tokens.shape[1] + LANES), jnp.bfloat16),
+        in_specs=[pl.BlockSpec(memory_space=pltpu.HBM)] * 3,
+        out_specs=in_vmem,
+        scratch_shapes=[
+            pltpu.VMEM(tokens.shape, tokens.dtype),
+            pltpu.VMEM(expert_ids.shape[::-1], expert_ids.dtype),
+            pltpu.VMEM(gate_values.shape[::-1], gate_values.dtype),
+            pltpu.SemaphoreType.DMA((PACK_PARTS + 2,)),
+        ],
+        compiler_params=pltpu.CompilerParams(vmem_limit_bytes=PACK_LIMIT * MIB),
+        name="pack",
+    )(tokens, expert_ids.T, gate_values.T)
 
 
 def expert_kernel(*refs):
@@ -181,21 +252,23 @@
     gate_vm, up_vm, down_vm, rows, sems = refs[14:]
     count, width = rows.shape
     part = count // 8
-    spans = [pl.ds(start, width // PARTS) for start in range(0, width, width // PARTS)]
+    units = gate_vm.shape[0]
     loads = [
         [
-            pltpu.make_async_copy(src.at[:, span], dst.at[:, span], sems.at[PARTS * k + s])
-            for s, span in enumerate(spans)
+            pltpu.make_async_copy(
+                src.at[pl.ds(s * units // PARTS, units // PARTS)],
+                dst.at[pl.ds(s * units // PARTS, units // PARTS)],
+                sems.at[PARTS * k + s],
+            )
+            for s in range(PARTS)
         ]
         for k, (src, dst) in enumerate(
             ((gate_ref, gate_vm), (up_ref, up_vm), (down_ref, down_vm))
         )
     ]
-    for s in range(PARTS):
-        loads[0][s].start()
-        loads[1][s].start()
-    for load in loads[2]:
-        load.start()
+    for weight in loads:
+        for load in weight:
+            load.start()
     for p in range(8):
         rows[p * part : (p + 1) * part] = pieces[p][:, :width]
     gates = jnp.concatenate([piece[:, width:] for piece in pieces], axis=0).astype(jnp.float32)
@@ -203,21 +276,21 @@
     gates = jnp.where(lane == lax.axis_index("expert"), gates, 0.0)
     gate = jnp.sum(gates, axis=1, keepdims=True)
     contract = (((1,), (1,)), ((), ()))
-    gate_part, up_part = 0.0, 0.0
-    for s, span in enumerate(spans):
-        loads[0][s].wait()
-        gate_part += lax.dot_general(
-            rows[:, span], gate_vm[:, span], contract, preferred_element_type=jnp.float32
-        )
-        loads[1][s].wait()
-        up_part += lax.dot_general(
-            rows[:, span], up_vm[:, span], contract, preferred_element_type=jnp.float32
-        )
+    for load in loads[0]:
+        load.wait()
+    gate_part = lax.dot_general(
+        rows[...], gate_vm[...], contract, preferred_element_type=jnp.float32
+    )
+    for load in loads[1]:
+        load.wait()
+    up_part = lax.dot_general(rows[...], up_vm[...], contract, preferred_element_type=jnp.float32)
     hidden = gate * (jax.nn.silu(gate_part) * up_part)
     hidden_t_ref[...] = hidden.T.astype(jnp.bfloat16)
     hidden = hidden.astype(jnp.bfloat16)
-    for load, span in zip(loads[2], spans):
+    for load in loads[2]:
         load.wait()
+    for start in range(0, width, BLOCK):
+        span = slice(start, start + BLOCK)
         terms = jnp.dot(hidden, down_vm[:, span], preferred_element_type=jnp.float32)
         terms = terms.astype(jnp.bfloat16)
         own_ref[:, span] = terms[: count // 2]
@@ -247,37 +320,46 @@
     )(*pieces, gate_weight, up_weight, down_weight)
 
 
-def update_kernel(block, *refs):
+def update_kernel(*refs):
     pieces = refs[:8]
     hidden_t_ref, down_ref, first_ref, second_ref = refs[8:12]
-    new_down_ref, new_first_ref, new_second_ref = refs[12:]
-    span = pl.ds(pl.multiple_of(pl.program_id(0) * block, LANES), block)
-    cotangent = jnp.concatenate([piece[:, span] for piece in pieces], axis=0)
-    gradient = jnp.dot(hidden_t_ref[...], cotangent, preferred_element_type=jnp.float32)
-    first = first_decay * first_ref[:, span].astype(jnp.float32) + (1.0 - first_decay) * gradient
-    second = (
-        second_decay * second_ref[:, span].astype(jnp.float32)
-        + (1.0 - second_decay) * gradient * gradient
-    )
+    outs, held, sems = refs[12:15], refs[15:18], refs[18]
     root = (1.0 - second_decay**adam_count) ** 0.5
     rate = learn_rate * root / (1.0 - first_decay**adam_count)
     keep = 1.0 - learn_rate * weight_decay
-    step = rate * first / (jnp.sqrt(second) + adam_epsilon * root)
-    new_down_ref[...] = (keep * down_ref[:, span].astype(jnp.float32) - step).astype(jnp.bfloat16)
-    new_first_ref[...] = first.astype(jnp.bfloat16)
-    new_second_ref[...] = second.astype(jnp.bfloat16)
+    stores = []
+    for start in range(0, down_ref.shape[1], UPDATE_BLOCK):
+        span = pl.ds(start, UPDATE_BLOCK)
+        cotangent = jnp.concatenate([piece[:, span] for piece in pieces], axis=0)
+        gradient = jnp.dot(hidden_t_ref[...], cotangent, preferred_element_type=jnp.float32)
+        first = first_decay * first_ref[:, span].astype(jnp.float32)
+        first += (1.0 - first_decay) * gradient
+        second = second_decay * second_ref[:, span].astype(jnp.float32)
+        second += (1.0 - second_decay) * gradient * gradient
+        step = rate * first / (jnp.sqrt(second) + adam_epsilon * root)
+        down = keep * down_ref[:, span].astype(jnp.float32) - step
+        for k, value in enumerate((down, first, second)):
+            held[k][:, span] = value.astype(jnp.bfloat16)
+            stores.append(
+                pltpu.make_async_copy(
+                    held[k].at[:, span], outs[k].at[:, span], sems.at[len(stores)]
+                )
+            )
+            stores[-1].start()
+    for store in stores:
+        store.wait()
 
 
 def update(pieces, hidden_t, down_weight, first_moment, second_moment):
     units, width = down_weight.shape
     part = pieces[0].shape[0]
-    in_vmem = pl.BlockSpec(memory_space=pltpu.VMEM)
     return pl.pallas_call(
-        functools.partial(update_kernel, BLOCK),
-        grid=(width // BLOCK,),
+        update_kernel,
         out_shape=[jax.ShapeDtypeStruct((units, width), jnp.bfloat16)] * 3,
-        in_specs=[in_vmem] * 12,
-        out_specs=[pl.BlockSpec((units, BLOCK), lambda i: (0, i))] * 3,
+        in_specs=[pl.BlockSpec(memory_space=pltpu.VMEM)] * 12,
+        out_specs=[pl.BlockSpec(memory_space=pltpu.HBM)] * 3,
+        scratch_shapes=[pltpu.VMEM((units, width), jnp.bfloat16)] * 3
+        + [pltpu.SemaphoreType.DMA((3 * width // UPDATE_BLOCK,))],
         compiler_params=pltpu.CompilerParams(vmem_limit_bytes=24 * MIB),
         cost_estimate=pl.CostEstimate(
             flops=2 * 8 * part * units * width,
@@ -299,22 +381,14 @@
     second_moment,
 ):
     experts = lax.axis_size("expert")
-    hot_rows = experts * 3 // 4
-    numbers = jnp.arange(LANES, dtype=jnp.int32)
-    matches = (expert_ids[:, :, None] == numbers) & (numbers < experts)
-    gates = jnp.sum(jnp.where(matches, gate_values[:, :, None], 0), axis=1)
-    hot = jnp.any(expert_ids < experts, axis=1).astype(jnp.int32)
-    rank = jnp.cumsum(hot) - hot
-    place = jnp.arange(hot_rows, dtype=jnp.int32)
-    pick = ((rank[None, :] == place[:, None]) & (hot[None, :] == 1)).astype(jnp.bfloat16)
-    hot_tokens = jnp.dot(pick, tokens, preferred_element_type=jnp.float32).astype(jnp.bfloat16)
-    hot_gates = jnp.dot(pick, gates, preferred_element_type=jnp.float32).astype(jnp.bfloat16)
-    pieces = spread(jnp.concatenate([hot_tokens, hot_gates], axis=1))
+    width = tokens.shape[1]
+    pieces = spread(pack(tokens, expert_ids, gate_values, experts))
+    pair_tokens = pieces[0][: 2 * (experts * 3 // 4), :width].astype(jnp.float32)
     pieces += to_core(pieces)
     own, other, hidden_t = expert_terms(pieces, gate_weight[0], up_weight[0], down_weight[0])
-    mixed = collect(own, other)
-    cotangent = jnp.tanh(hot_tokens.astype(jnp.float32) + mixed).astype(jnp.bfloat16)
-    pieces = spread(cotangent)
+    cotangent = jnp.tanh(pair_tokens + collect(own, other)).astype(jnp.bfloat16)
+    cotangent = jnp.concatenate([cotangent, swap(cotangent, LINE[1])], axis=0)
+    pieces = across(cotangent)
     pieces += to_core(pieces)
     outs = update(pieces, hidden_t, down_weight[0], first_moment[0], second_moment[0])
     return tuple(out[None] for out in outs)

time: 91.3 us -> 89.1 us (0.976)
  starting transfers between devices: 25.5 us -> 21.4 us
  waiting for transfers between devices: 50 us -> 52.8 us
  other arithmetic: 2.71 us -> 1.57 us
    ppermute x27 -> x24, starting transfers between devices: 25.5 us -> 21.4 us  [swap(): return lax.ppermute(block, AXES, [(i, i ^ mask) for i in range(count)])]
    ppermute x27 -> x24, waiting for transfers between devices: 50 us -> 52.8 us  [swap(): return lax.ppermute(block, AXES, [(i, i ^ mask) for i in range(count)])]
    pallas_call x1 -> x2, Pallas kernels: 5.61 us -> 7 us  [the longest x1 4.93 us: update(): pl.pallas_call(update_kernel, out_shape=[jax.ShapeDtypeStruct((units, wid...]
    reduce_sum x1 -> x0, other arithmetic: 0.97 us -> none  [dense_plan(): gates = jnp.sum(jnp.where(matches, gate_values[:, :, None], 0), axis=1)]
  transfers between devices with their start and end apart: 27 -> 24, of which waited for: 20 -> 19; matrix products, arithmetic and copies ran while one was open for 0% -> 0% of each run, Pallas kernels for 0% -> 0%
where the time goes in v4:
time: 89.1 us; the launch traced here: 88.9 us
  waiting for transfers between devices  52.8 us (59%)
  starting transfers between devices  21.4 us (24%)
  Pallas kernels  12.3 us (14%)
  other arithmetic  1.57 us (2%)
    ppermute x24, waiting for transfers between devices, swap(): return lax.ppermute(block, AXES, [(i, i ^ mask) for i in range(count)])  52.8 us
    ppermute x24, starting transfers between devices, swap(): return lax.ppermute(block, AXES, [(i, i ^ mask) for i in range(count)])  21.4 us
    pallas_call x1, Pallas kernels, expert_terms(): pl.pallas_call(expert_kernel, out_shape=[half, half, jax.ShapeDtypeStruct...  5.3 us
    pallas_call x1, Pallas kernels, update(): pl.pallas_call(update_kernel, out_shape=[jax.ShapeDtypeStruct((units, wid...  4.93 us
    pallas_call x1, Pallas kernels, pack(): pl.pallas_call(functools.partial(pack_kernel, experts), out_shape=jax.Sha...  2.07 us
  transfers between devices with their start and end apart: 24, of which 19 were waited for; matrix products, arithmetic and copies ran while one was open for 0% of the time, Pallas kernels for 0%

profile of v4, /device:TPU:0, one launch (start us, length us, event | category | flops | bytes accessed | tf_op | source)
XLA Modules:
  0.0 88.9 jit_solution(11434423355988412746)
XLA Ops:
  0.6 2.1 %pack.1 = bf16[12,2688]{1,0:T(8,128)(2,1)} custom-call(bf16[128,2560]{1,0:T(8,128)(2,1)} %tokens_ref.1, s32[6,128]{1,0:T(8,128)} %bitcast.14, bf16[6,128]{1,0:T(8,128)(2,1)} %bitcast.15), custom_call_target="tpu_custom_call" | custom-call | tf_op jit(solution)/shard_map/pack/pallas_call | solution.py:233
  2.7 5.1 %collective-permute-start.2 = (bf16[12,2688]{1,0:T(8,128)(2,1)}, bf16[12,2688]{1,0:T(8,128)(2,1)S(1)}, u32[]{:S(2)}, u32[]{:S(2)}) collective-permute-start(bf16[12,2688]{1,0:T(8,128)(2,1)} %pack.1), channel_id=1, source_target_pairs={{0,12},{1,13},{2,14},{3,15},{4,8},{5,9},{6,10},{7,11},{8,4},{9,5},... | collective-permute-start | bytes 193544 | tf_op jit(solution)/shard_map/ppermute | solution.py:153
  7.8 0.0 collective-permute-start.1
  7.8 0.6 collective-permute-start
  8.5 3.0 %collective-permute-done.2 = bf16[12,2688]{1,0:T(8,128)(2,1)S(1)} collective-permute-done((bf16[12,2688]{1,0:T(8,128)(2,1)}, bf16[12,2688]{1,0:T(8,128)(2,1)S(1)}, u32[]{:S(2)}, u32[]{:S(2)}) %collective-permute-start.2) | collective-permute-done | bytes 64544 | tf_op jit(solution)/shard_map/ppermute | solution.py:153
  11.5 2.7 %collective-permute-done.1 = bf16[12,2688]{1,0:T(8,128)(2,1)S(1)} collective-permute-done((bf16[12,2688]{1,0:T(8,128)(2,1)}, bf16[12,2688]{1,0:T(8,128)(2,1)S(1)}, u32[]{:S(2)}, u32[]{:S(2)}) %collective-permute-start.1) | collective-permute-done | bytes 64544 | tf_op jit(solution)/shard_map/ppermute | solution.py:153
  14.2 1.0 %collective-permute-done = bf16[12,2688]{1,0:T(8,128)(2,1)S(1)} collective-permute-done((bf16[12,2688]{1,0:T(8,128)(2,1)}, bf16[12,2688]{1,0:T(8,128)(2,1)S(1)}, u32[]{:S(2)}, u32[]{:S(2)}) %collective-permute-start) | collective-permute-done | bytes 64544 | tf_op jit(solution)/shard_map/ppermute | solution.py:153
  15.2 1.0 %pad_maximum_fusion.refs_0_ = bf16[48,2688]{1,0:T(8,128)(2,1)S(1)} fusion(bf16[12,2688]{1,0:T(8,128)(2,1)S(1)} %collective-permute-done.2, bf16[12,2688]{1,0:T(8,128)(2,1)S(1)} %collective-permute-done.1, bf16[12,2688]{1,0:T(8,128)(2,1)S(1)} %collective-permute-done, bf16[12,2688]{1,0:T(8,128)(2,1)} %pack.1), kind=kLoop, calls=%fused_computation.4 | loop fusion | flops 1032192 | bytes 516096 | tf_op jit(solution)/shard_map/concatenate | solution.py:157
  16.2 2.5 %collective-permute-start.5 = (bf16[48,2688]{1,0:T(8,128)(2,1)S(1)}, bf16[48,2688]{1,0:T(8,128)(2,1)S(1)}, u32[]{:S(2)}, u32[]{:S(2)}) collective-permute-start(bf16[48,2688]{1,0:T(8,128)(2,1)S(1)} %pad_maximum_fusion.refs_0_), channel_id=1, source_target_pairs={{0,18},{1,19},{2,16},{3,17},{4,22},{5,23},{6,20},{7,21},{8,26},{9,... | collective-permute-start | bytes 774152 | tf_op jit(solution)/shard_map/ppermute | solution.py:153
  18.7 0.5 collective-permute-start.4
  19.2 0.5 collective-permute-start.3
  19.8 0.0 collective-permute-start.6
  19.8 6.1 %collective-permute-done.5.refs_3_ = bf16[48,2688]{1,0:T(8,128)(2,1)S(1)} collective-permute-done((bf16[48,2688]{1,0:T(8,128)(2,1)S(1)}, bf16[48,2688]{1,0:T(8,128)(2,1)S(1)}, u32[]{:S(2)}, u32[]{:S(2)}) %collective-permute-start.5) | collective-permute-done | bytes 258080 | tf_op jit(solution)/shard_map/ppermute | solution.py:153
  25.9 0.0 collective-permute-start.9
  25.9 2.7 %collective-permute-done.4.refs_2_ = bf16[48,2688]{1,0:T(8,128)(2,1)S(1)} collective-permute-done((bf16[48,2688]{1,0:T(8,128)(2,1)S(1)}, bf16[48,2688]{1,0:T(8,128)(2,1)S(1)}, u32[]{:S(2)}, u32[]{:S(2)}) %collective-permute-start.4) | collective-permute-done | bytes 258080 | tf_op jit(solution)/shard_map/ppermute | solution.py:153
  28.6 0.0 collective-permute-start.8
  28.6 0.2 collective-permute-done.3.refs_1_
  28.8 0.3 collective-permute-start.7
  29.1 0.0 collective-permute-done.6.refs_4_
  29.1 0.0 collective-permute-done.9.refs_7_
  29.1 1.0 %collective-permute-done.8.refs_6_ = bf16[48,2688]{1,0:T(8,128)(2,1)S(1)} collective-permute-done((bf16[48,2688]{1,0:T(8,128)(2,1)S(1)}, bf16[48,2688]{1,0:T(8,128)(2,1)S(1)}, u32[]{:S(2)}, u32[]{:S(2)}) %collective-permute-start.8) | collective-permute-done | bytes 258080 | tf_op jit(solution)/shard_map/ppermute | solution.py:153
  30.1 0.4 collective-permute-done.7.refs_5_
  30.5 5.3 %expert_terms.1 = (bf16[192,2560]{1,0:T(8,128)(2,1)S(1)}, bf16[192,2560]{1,0:T(8,128)(2,1)S(1)}, bf16[384,384]{1,0:T(8,128)(2,1)S(1)}) custom-call(bf16[48,2688]{1,0:T(8,128)(2,1)S(1)} %pad_maximum_fusion.refs_0_, bf16[48,2688]{1,0:T(8,128)(2,1)S(1)} %collective-permute-done.3.refs_1_, bf16[48,2688]{1,0:T(8,128)(2,1)S(1)} %collective-permute-done.4.refs_2_, ...), custom_call_target="tpu_custom_call" | custom-call | flops 2264924160 | bytes 9830400 | tf_op jit(solution)/shard_map/expert_terms/pallas_call | solution.py:306
  35.8 0.2 collective-permute-start.10
  36.0 2.4 %collective-permute-done.10 = bf16[192,2560]{1,0:T(8,128)(2,1)S(1)} collective-permute-done((bf16[192,2560]{1,0:T(8,128)(2,1)S(1)}, bf16[192,2560]{1,0:T(8,128)(2,1)S(1)}, u32[]{:S(2)}, u32[]{:S(2)}) %collective-permute-start.10) | collective-permute-done | bytes 983072 | tf_op jit(solution)/shard_map/ppermute | solution.py:153
  38.4 0.0 copy-start.2
  38.4 0.3 fusion.3
  38.8 0.0 copy-start.3
  38.8 0.1 fusion.4
  38.8 1.7 %collective-permute-start.11 = (bf16[48,2560]{1,0:T(8,128)(2,1)S(1)}, bf16[48,2560]{1,0:T(8,128)(2,1)S(1)}, u32[]{:S(2)}, u32[]{:S(2)}) collective-permute-start(bf16[48,2560]{1,0:T(8,128)(2,1)S(1)} %get-tuple-element.17), channel_id=1, source_target_pairs={{0,2},{1,3},{2,0},{3,1},{4,6},{5,7},{6,4},{7,5},{8,10},{9,11},{10,... | collective-permute-start | bytes 737288 | tf_op jit(solution)/shard_map/ppermute | solution.py:153
  40.5 1.5 %collective-permute-start.13 = (bf16[48,2560]{1,0:T(8,128)(2,1)S(1)}, bf16[48,2560]{1,0:T(8,128)(2,1)S(1)}, u32[]{:S(2)}, u32[]{:S(2)}) collective-permute-start(bf16[48,2560]{1,0:T(8,128)(2,1)S(1)} %get-tuple-element.18), channel_id=1, source_target_pairs={{0,18},{1,19},{2,16},{3,17},{4,22},{5,23},{6,20},{7,21},{8,26},{9,... | collective-permute-start | bytes 737288 | tf_op jit(solution)/shard_map/ppermute | solution.py:153
  42.0 0.4 collective-permute-start.12
  42.4 5.3 %collective-permute-done.11 = bf16[48,2560]{1,0:T(8,128)(2,1)S(1)} collective-permute-done((bf16[48,2560]{1,0:T(8,128)(2,1)S(1)}, bf16[48,2560]{1,0:T(8,128)(2,1)S(1)}, u32[]{:S(2)}, u32[]{:S(2)}) %collective-permute-start.11) | collective-permute-done | bytes 245792 | tf_op jit(solution)/shard_map/ppermute | solution.py:153
  47.7 5.7 %collective-permute-done.13 = bf16[48,2560]{1,0:T(8,128)(2,1)S(1)} collective-permute-done((bf16[48,2560]{1,0:T(8,128)(2,1)S(1)}, bf16[48,2560]{1,0:T(8,128)(2,1)S(1)}, u32[]{:S(2)}, u32[]{:S(2)}) %collective-permute-start.13) | collective-permute-done | bytes 245792 | tf_op jit(solution)/shard_map/ppermute | solution.py:153
  53.4 1.4 %collective-permute-done.12 = bf16[48,2560]{1,0:T(8,128)(2,1)S(1)} collective-permute-done((bf16[48,2560]{1,0:T(8,128)(2,1)S(1)}, bf16[48,2560]{1,0:T(8,128)(2,1)S(1)}, u32[]{:S(2)}, u32[]{:S(2)}) %collective-permute-start.12) | collective-permute-done | bytes 245792 | tf_op jit(solution)/shard_map/ppermute | solution.py:153
  54.7 0.0 copy-start
  54.7 0.0 copy-start.1
  54.7 0.1 fusion.1
  54.9 0.7 collective-permute-start.14
  55.6 4.2 %collective-permute-done.14 = bf16[24,2560]{1,0:T(8,128)(2,1)S(1)} collective-permute-done((bf16[24,2560]{1,0:T(8,128)(2,1)S(1)}, bf16[24,2560]{1,0:T(8,128)(2,1)S(1)}, u32[]{:S(2)}, u32[]{:S(2)}) %collective-permute-start.14) | collective-permute-done | bytes 122912 | tf_op jit(solution)/shard_map/ppermute | solution.py:153
  59.9 3.1 %collective-permute-start.15 = (bf16[24,2560]{1,0:T(8,128)(2,1)S(1)}, bf16[24,2560]{1,0:T(8,128)(2,1)S(1)}, u32[]{:S(2)}, u32[]{:S(2)}) collective-permute-start(bf16[24,2560]{1,0:T(8,128)(2,1)S(1)} %pad_maximum_fusion.3), channel_id=1, source_target_pairs={{0,8},{1,9},{2,10},{3,11},{4,12},{5,13},{6,14},{7,15},{8,0},{9,1},... | collective-permute-start | bytes 368648 | tf_op jit(solution)/shard_map/ppermute | solution.py:153
  63.1 4.2 %collective-permute-done.15 = bf16[24,2560]{1,0:T(8,128)(2,1)S(1)} collective-permute-done((bf16[24,2560]{1,0:T(8,128)(2,1)S(1)}, bf16[24,2560]{1,0:T(8,128)(2,1)S(1)}, u32[]{:S(2)}, u32[]{:S(2)}) %collective-permute-start.15) | collective-permute-done | bytes 122912 | tf_op jit(solution)/shard_map/ppermute | solution.py:153
  67.2 0.0 copy-done.3
  67.2 0.1 tanh_convert_fusion
  67.3 0.1 collective-permute-start.16
  67.4 4.9 %collective-permute-done.16 = bf16[24,2560]{1,0:T(8,128)(2,1)S(1)} collective-permute-done((bf16[24,2560]{1,0:T(8,128)(2,1)S(1)}, bf16[24,2560]{1,0:T(8,128)(2,1)S(1)}, u32[]{:S(2)}, u32[]{:S(2)}) %collective-permute-start.16) | collective-permute-done | bytes 122912 | tf_op jit(solution)/shard_map/ppermute | solution.py:153
  72.3 1.5 %collective-permute-start.19 = (bf16[48,2560]{1,0:T(8,128)(2,1)S(1)}, bf16[48,2560]{1,0:T(8,128)(2,1)S(1)}, u32[]{:S(2)}, u32[]{:S(2)}) collective-permute-start(bf16[48,2560]{1,0:T(8,128)(2,1)S(1)} %pad_maximum_fusion.1.refs_0_), channel_id=1, source_target_pairs={{0,18},{1,19},{2,16},{3,17},{4,22},{5,23},{6,20},{7,21},{8,26},{9,... | collective-permute-start | bytes 737288 | tf_op jit(solution)/shard_map/ppermute | solution.py:153
  73.8 0.8 collective-permute-start.18
  74.6 1.2 %collective-permute-start.17 = (bf16[48,2560]{1,0:T(8,128)(2,1)S(1)}, bf16[48,2560]{1,0:T(8,128)(2,1)S(1)}, u32[]{:S(2)}, u32[]{:S(2)}) collective-permute-start(bf16[48,2560]{1,0:T(8,128)(2,1)S(1)} %pad_maximum_fusion.1.refs_0_), channel_id=1, source_target_pairs={{0,2},{1,3},{2,0},{3,1},{4,6},{5,7},{6,4},{7,5},{8,10},{9,11},{10,... | collective-permute-start | bytes 737288 | tf_op jit(solution)/shard_map/ppermute | solution.py:153
  75.9 0.0 collective-permute-start.20
  75.9 3.7 %collective-permute-done.19.refs_3_ = bf16[48,2560]{1,0:T(8,128)(2,1)S(1)} collective-permute-done((bf16[48,2560]{1,0:T(8,128)(2,1)S(1)}, bf16[48,2560]{1,0:T(8,128)(2,1)S(1)}, u32[]{:S(2)}, u32[]{:S(2)}) %collective-permute-start.19) | collective-permute-done | bytes 245792 | tf_op jit(solution)/shard_map/ppermute | solution.py:153
  79.6 0.0 collective-permute-start.23
  79.6 2.5 %collective-permute-done.18.refs_2_ = bf16[48,2560]{1,0:T(8,128)(2,1)S(1)} collective-permute-done((bf16[48,2560]{1,0:T(8,128)(2,1)S(1)}, bf16[48,2560]{1,0:T(8,128)(2,1)S(1)}, u32[]{:S(2)}, u32[]{:S(2)}) %collective-permute-start.18) | collective-permute-done | bytes 245792 | tf_op jit(solution)/shard_map/ppermute | solution.py:153
  82.1 0.0 collective-permute-start.22
  82.1 0.0 collective-permute-done.17.refs_1_
  82.1 0.5 collective-permute-start.21
  82.6 0.0 collective-permute-done.20.refs_4_
  82.6 0.0 collective-permute-done.23.refs_7_
  82.6 1.0 %collective-permute-done.22.refs_6_ = bf16[48,2560]{1,0:T(8,128)(2,1)S(1)} collective-permute-done((bf16[48,2560]{1,0:T(8,128)(2,1)S(1)}, bf16[48,2560]{1,0:T(8,128)(2,1)S(1)}, u32[]{:S(2)}, u32[]{:S(2)}) %collective-permute-start.22) | collective-permute-done | bytes 245792 | tf_op jit(solution)/shard_map/ppermute | solution.py:153
  83.6 0.4 collective-permute-done.21.refs_5_
  84.0 0.0 copy-done.2
  84.0 0.0 copy-done
  84.0 0.0 copy-done.1
  84.0 4.9 %update.1 = (bf16[384,2560]{1,0:T(8,128)(2,1)}, bf16[384,2560]{1,0:T(8,128)(2,1)}, bf16[384,2560]{1,0:T(8,128)(2,1)}) custom-call(bf16[48,2560]{1,0:T(8,128)(2,1)S(1)} %pad_maximum_fusion.1.refs_0_, bf16[48,2560]{1,0:T(8,128)(2,1)S(1)} %collective-permute-done.17.refs_1_, bf16[48,2560]{1,0:T(8,128)(2,1)S(1)} %collective-permute-done.18.refs_2_, ...), custom_call_target="tpu_custom_call" | custom-call | flops 754974720 | bytes 13762560 | tf_op jit(solution)/shard_map/update/pallas_call | solution.py:356
  (5 shorter events, 0.1 us)
Async XLA Ops:
  2.7 8.8 %collective-permute-start.2 = (bf16[12,2688]{1,0:T(8,128)(2,1)}, bf16[12,2688]{1,0:T(8,128)(2,1)S(1)}, u32[]{:S(2)}, u32[]{:S(2)}) collective-permute-start(bf16[12,2688]{1,0:T(8,128)(2,1)} %pack.1), channel_id=1, source_target_pairs={{0,12},{1,13},{2,14},{3,15},{4,8},{5,9},{6,10},{7,11},{8,4},{9,5},... | collective-permute-start | bytes 193544 | tf_op jit(solution)/shard_map/ppermute | solution.py:153
  7.8 6.4 %collective-permute-start.1 = (bf16[12,2688]{1,0:T(8,128)(2,1)}, bf16[12,2688]{1,0:T(8,128)(2,1)S(1)}, u32[]{:S(2)}, u32[]{:S(2)}) collective-permute-start(bf16[12,2688]{1,0:T(8,128)(2,1)} %pack.1), channel_id=1, source_target_pairs={{0,4},{1,5},{2,6},{3,7},{4,0},{5,1},{6,2},{7,3},{8,12},{9,13},{10,... | collective-permute-start | bytes 193544 | tf_op jit(solution)/shard_map/ppermute | solution.py:153
  7.8 7.4 %collective-permute-start = (bf16[12,2688]{1,0:T(8,128)(2,1)}, bf16[12,2688]{1,0:T(8,128)(2,1)S(1)}, u32[]{:S(2)}, u32[]{:S(2)}) collective-permute-start(bf16[12,2688]{1,0:T(8,128)(2,1)} %pack.1), channel_id=1, source_target_pairs={{0,8},{1,9},{2,10},{3,11},{4,12},{5,13},{6,14},{7,15},{8,0},{9,1},... | collective-permute-start | bytes 193544 | tf_op jit(solution)/shard_map/ppermute | solution.py:153
  16.2 9.7 %collective-permute-start.5 = (bf16[48,2688]{1,0:T(8,128)(2,1)S(1)}, bf16[48,2688]{1,0:T(8,128)(2,1)S(1)}, u32[]{:S(2)}, u32[]{:S(2)}) collective-permute-start(bf16[48,2688]{1,0:T(8,128)(2,1)S(1)} %pad_maximum_fusion.refs_0_), channel_id=1, source_target_pairs={{0,18},{1,19},{2,16},{3,17},{4,22},{5,23},{6,20},{7,21},{8,26},{9,... | collective-permute-start | bytes 774152 | tf_op jit(solution)/shard_map/ppermute | solution.py:153
  18.7 9.9 %collective-permute-start.4 = (bf16[48,2688]{1,0:T(8,128)(2,1)S(1)}, bf16[48,2688]{1,0:T(8,128)(2,1)S(1)}, u32[]{:S(2)}, u32[]{:S(2)}) collective-permute-start(bf16[48,2688]{1,0:T(8,128)(2,1)S(1)} %pad_maximum_fusion.refs_0_), channel_id=1, source_target_pairs={{0,16},{1,17},{2,18},{3,19},{4,20},{5,21},{6,22},{7,23},{8,24},{9,... | collective-permute-start | bytes 774152 | tf_op jit(solution)/shard_map/ppermute | solution.py:153
  19.2 9.6 %collective-permute-start.3 = (bf16[48,2688]{1,0:T(8,128)(2,1)S(1)}, bf16[48,2688]{1,0:T(8,128)(2,1)S(1)}, u32[]{:S(2)}, u32[]{:S(2)}) collective-permute-start(bf16[48,2688]{1,0:T(8,128)(2,1)S(1)} %pad_maximum_fusion.refs_0_), channel_id=1, source_target_pairs={{0,2},{1,3},{2,0},{3,1},{4,6},{5,7},{6,4},{7,5},{8,10},{9,11},{10,... | collective-permute-start | bytes 774152 | tf_op jit(solution)/shard_map/ppermute | solution.py:153
  19.8 9.3 %collective-permute-start.6 = (bf16[48,2688]{1,0:T(8,128)(2,1)S(1)}, bf16[48,2688]{1,0:T(8,128)(2,1)S(1)}, u32[]{:S(2)}, u32[]{:S(2)}) collective-permute-start(bf16[48,2688]{1,0:T(8,128)(2,1)S(1)} %pad_maximum_fusion.refs_0_), channel_id=1, source_target_pairs={{0,1},{1,0},{2,3},{3,2},{4,5},{5,4},{6,7},{7,6},{8,9},{9,8},{10,11... | collective-permute-start | bytes 774152 | tf_op jit(solution)/shard_map/ppermute | solution.py:153
  25.9 3.2 %collective-permute-start.9 = (bf16[48,2688]{1,0:T(8,128)(2,1)S(1)}, bf16[48,2688]{1,0:T(8,128)(2,1)S(1)}, u32[]{:S(2)}, u32[]{:S(2)}) collective-permute-start(bf16[48,2688]{1,0:T(8,128)(2,1)S(1)} %collective-permute-done.5.refs_3_), channel_id=1, source_target_pairs={{0,1},{1,0},{2,3},{3,2},{4,5},{5,4},{6,7},{7,6},{8,9},{9,8},{10,11... | collective-permute-start | bytes 774152 | tf_op jit(solution)/shard_map/ppermute | solution.py:153
  28.6 1.5 %collective-permute-start.8 = (bf16[48,2688]{1,0:T(8,128)(2,1)S(1)}, bf16[48,2688]{1,0:T(8,128)(2,1)S(1)}, u32[]{:S(2)}, u32[]{:S(2)}) collective-permute-start(bf16[48,2688]{1,0:T(8,128)(2,1)S(1)} %collective-permute-done.4.refs_2_), channel_id=1, source_target_pairs={{0,1},{1,0},{2,3},{3,2},{4,5},{5,4},{6,7},{7,6},{8,9},{9,8},{10,11... | collective-permute-start | bytes 774152 | tf_op jit(solution)/shard_map/ppermute | solution.py:153
  28.8 1.7 %collective-permute-start.7 = (bf16[48,2688]{1,0:T(8,128)(2,1)S(1)}, bf16[48,2688]{1,0:T(8,128)(2,1)S(1)}, u32[]{:S(2)}, u32[]{:S(2)}) collective-permute-start(bf16[48,2688]{1,0:T(8,128)(2,1)S(1)} %collective-permute-done.3.refs_1_), channel_id=1, source_target_pairs={{0,1},{1,0},{2,3},{3,2},{4,5},{5,4},{6,7},{7,6},{8,9},{9,8},{10,11... | collective-permute-start | bytes 774152 | tf_op jit(solution)/shard_map/ppermute | solution.py:153
  35.8 2.6 %collective-permute-start.10 = (bf16[192,2560]{1,0:T(8,128)(2,1)S(1)}, bf16[192,2560]{1,0:T(8,128)(2,1)S(1)}, u32[]{:S(2)}, u32[]{:S(2)}) collective-permute-start(bf16[192,2560]{1,0:T(8,128)(2,1)S(1)} %get-tuple-element.10), channel_id=1, source_target_pairs={{0,1},{1,0},{2,3},{3,2},{4,5},{5,4},{6,7},{7,6},{8,9},{9,8},{10,11... | collective-permute-start | bytes 2949128 | tf_op jit(solution)/shard_map/ppermute | solution.py:153
  38.4 45.5 %copy-start.2 = (bf16[1,384,2560]{2,1,0:T(8,128)(2,1)S(1)}, bf16[1,384,2560]{2,1,0:T(8,128)(2,1)}, u32[]{:S(2)}) copy-start(bf16[1,384,2560]{2,1,0:T(8,128)(2,1)} %param.15) | copy-start | bytes 5898244
  38.8 28.5 %copy-start.3 = (bf16[12,2688]{1,0:T(8,128)(2,1)S(1)}, bf16[12,2688]{1,0:T(8,128)(2,1)}, u32[]{:S(2)}) copy-start(bf16[12,2688]{1,0:T(8,128)(2,1)} %pack.1) | copy-start | bytes 193540
  38.8 8.9 %collective-permute-start.11 = (bf16[48,2560]{1,0:T(8,128)(2,1)S(1)}, bf16[48,2560]{1,0:T(8,128)(2,1)S(1)}, u32[]{:S(2)}, u32[]{:S(2)}) collective-permute-start(bf16[48,2560]{1,0:T(8,128)(2,1)S(1)} %get-tuple-element.17), channel_id=1, source_target_pairs={{0,2},{1,3},{2,0},{3,1},{4,6},{5,7},{6,4},{7,5},{8,10},{9,11},{10,... | collective-permute-start | bytes 737288 | tf_op jit(solution)/shard_map/ppermute | solution.py:153
  40.5 12.8 %collective-permute-start.13 = (bf16[48,2560]{1,0:T(8,128)(2,1)S(1)}, bf16[48,2560]{1,0:T(8,128)(2,1)S(1)}, u32[]{:S(2)}, u32[]{:S(2)}) collective-permute-start(bf16[48,2560]{1,0:T(8,128)(2,1)S(1)} %get-tuple-element.18), channel_id=1, source_target_pairs={{0,18},{1,19},{2,16},{3,17},{4,22},{5,23},{6,20},{7,21},{8,26},{9,... | collective-permute-start | bytes 737288 | tf_op jit(solution)/shard_map/ppermute | solution.py:153
  42.0 12.7 %collective-permute-start.12 = (bf16[48,2560]{1,0:T(8,128)(2,1)S(1)}, bf16[48,2560]{1,0:T(8,128)(2,1)S(1)}, u32[]{:S(2)}, u32[]{:S(2)}) collective-permute-start(bf16[48,2560]{1,0:T(8,128)(2,1)S(1)} %get-tuple-element.19), channel_id=1, source_target_pairs={{0,16},{1,17},{2,18},{3,19},{4,20},{5,21},{6,22},{7,23},{8,24},{9,... | collective-permute-start | bytes 737288 | tf_op jit(solution)/shard_map/ppermute | solution.py:153
  54.7 29.2 %copy-start = (bf16[1,384,2560]{2,1,0:T(8,128)(2,1)S(1)}, bf16[1,384,2560]{2,1,0:T(8,128)(2,1)}, u32[]{:S(2)}) copy-start(bf16[1,384,2560]{2,1,0:T(8,128)(2,1)} %param.13) | copy-start | bytes 5898244
  54.7 29.2 %copy-start.1 = (bf16[1,384,2560]{2,1,0:T(8,128)(2,1)S(1)}, bf16[1,384,2560]{2,1,0:T(8,128)(2,1)}, u32[]{:S(2)}) copy-start(bf16[1,384,2560]{2,1,0:T(8,128)(2,1)} %param.14) | copy-start | bytes 5898244
  54.9 4.9 %collective-permute-start.14 = (bf16[24,2560]{1,0:T(8,128)(2,1)S(1)}, bf16[24,2560]{1,0:T(8,128)(2,1)S(1)}, u32[]{:S(2)}, u32[]{:S(2)}) collective-permute-start(bf16[24,2560]{1,0:T(8,128)(2,1)S(1)} %split.53), channel_id=1, source_target_pairs={{0,4},{1,5},{2,6},{3,7},{4,0},{5,1},{6,2},{7,3},{8,12},{9,13},{10,... | collective-permute-start | bytes 368648 | tf_op jit(solution)/shard_map/ppermute | solution.py:153
  59.9 7.3 %collective-permute-start.15 = (bf16[24,2560]{1,0:T(8,128)(2,1)S(1)}, bf16[24,2560]{1,0:T(8,128)(2,1)S(1)}, u32[]{:S(2)}, u32[]{:S(2)}) collective-permute-start(bf16[24,2560]{1,0:T(8,128)(2,1)S(1)} %pad_maximum_fusion.3), channel_id=1, source_target_pairs={{0,8},{1,9},{2,10},{3,11},{4,12},{5,13},{6,14},{7,15},{8,0},{9,1},... | collective-permute-start | bytes 368648 | tf_op jit(solution)/shard_map/ppermute | solution.py:153
  67.3 4.9 %collective-permute-start.16 = (bf16[24,2560]{1,0:T(8,128)(2,1)S(1)}, bf16[24,2560]{1,0:T(8,128)(2,1)S(1)}, u32[]{:S(2)}, u32[]{:S(2)}) collective-permute-start(bf16[24,2560]{1,0:T(8,128)(2,1)S(1)} %tanh_convert_fusion), channel_id=1, source_target_pairs={{0,4},{1,5},{2,6},{3,7},{4,0},{5,1},{6,2},{7,3},{8,12},{9,13},{10,... | collective-permute-start | bytes 368648 | tf_op jit(solution)/shard_map/ppermute | solution.py:153
  72.3 7.3 %collective-permute-start.19 = (bf16[48,2560]{1,0:T(8,128)(2,1)S(1)}, bf16[48,2560]{1,0:T(8,128)(2,1)S(1)}, u32[]{:S(2)}, u32[]{:S(2)}) collective-permute-start(bf16[48,2560]{1,0:T(8,128)(2,1)S(1)} %pad_maximum_fusion.1.refs_0_), channel_id=1, source_target_pairs={{0,18},{1,19},{2,16},{3,17},{4,22},{5,23},{6,20},{7,21},{8,26},{9,... | collective-permute-start | bytes 737288 | tf_op jit(solution)/shard_map/ppermute | solution.py:153
  73.8 8.3 %collective-permute-start.18 = (bf16[48,2560]{1,0:T(8,128)(2,1)S(1)}, bf16[48,2560]{1,0:T(8,128)(2,1)S(1)}, u32[]{:S(2)}, u32[]{:S(2)}) collective-permute-start(bf16[48,2560]{1,0:T(8,128)(2,1)S(1)} %pad_maximum_fusion.1.refs_0_), channel_id=1, source_target_pairs={{0,16},{1,17},{2,18},{3,19},{4,20},{5,21},{6,22},{7,23},{8,24},{9,... | collective-permute-start | bytes 737288 | tf_op jit(solution)/shard_map/ppermute | solution.py:153
  74.6 7.5 %collective-permute-start.17 = (bf16[48,2560]{1,0:T(8,128)(2,1)S(1)}, bf16[48,2560]{1,0:T(8,128)(2,1)S(1)}, u32[]{:S(2)}, u32[]{:S(2)}) collective-permute-start(bf16[48,2560]{1,0:T(8,128)(2,1)S(1)} %pad_maximum_fusion.1.refs_0_), channel_id=1, source_target_pairs={{0,2},{1,3},{2,0},{3,1},{4,6},{5,7},{6,4},{7,5},{8,10},{9,11},{10,... | collective-permute-start | bytes 737288 | tf_op jit(solution)/shard_map/ppermute | solution.py:153
  75.9 6.8 %collective-permute-start.20 = (bf16[48,2560]{1,0:T(8,128)(2,1)S(1)}, bf16[48,2560]{1,0:T(8,128)(2,1)S(1)}, u32[]{:S(2)}, u32[]{:S(2)}) collective-permute-start(bf16[48,2560]{1,0:T(8,128)(2,1)S(1)} %pad_maximum_fusion.1.refs_0_), channel_id=1, source_target_pairs={{0,1},{1,0},{2,3},{3,2},{4,5},{5,4},{6,7},{7,6},{8,9},{9,8},{10,11... | collective-permute-start | bytes 737288 | tf_op jit(solution)/shard_map/ppermute | solution.py:153
  79.6 3.0 %collective-permute-start.23 = (bf16[48,2560]{1,0:T(8,128)(2,1)S(1)}, bf16[48,2560]{1,0:T(8,128)(2,1)S(1)}, u32[]{:S(2)}, u32[]{:S(2)}) collective-permute-start(bf16[48,2560]{1,0:T(8,128)(2,1)S(1)} %collective-permute-done.19.refs_3_), channel_id=1, source_target_pairs={{0,1},{1,0},{2,3},{3,2},{4,5},{5,4},{6,7},{7,6},{8,9},{9,8},{10,11... | collective-permute-start | bytes 737288 | tf_op jit(solution)/shard_map/ppermute | solution.py:153
  82.1 1.5 %collective-permute-start.22 = (bf16[48,2560]{1,0:T(8,128)(2,1)S(1)}, bf16[48,2560]{1,0:T(8,128)(2,1)S(1)}, u32[]{:S(2)}, u32[]{:S(2)}) collective-permute-start(bf16[48,2560]{1,0:T(8,128)(2,1)S(1)} %collective-permute-done.18.refs_2_), channel_id=1, source_target_pairs={{0,1},{1,0},{2,3},{3,2},{4,5},{5,4},{6,7},{7,6},{8,9},{9,8},{10,11... | collective-permute-start | bytes 737288 | tf_op jit(solution)/shard_map/ppermute | solution.py:153
  82.1 1.9 %collective-permute-start.21 = (bf16[48,2560]{1,0:T(8,128)(2,1)S(1)}, bf16[48,2560]{1,0:T(8,128)(2,1)S(1)}, u32[]{:S(2)}, u32[]{:S(2)}) collective-permute-start(bf16[48,2560]{1,0:T(8,128)(2,1)S(1)} %collective-permute-done.17.refs_1_), channel_id=1, source_target_pairs={{0,1},{1,0},{2,3},{3,2},{4,5},{5,4},{6,7},{7,6},{8,9},{9,8},{10,11... | collective-permute-start | bytes 737288 | tf_op jit(solution)/shard_map/ppermute | solution.py:153

commit v5 on v4

--- a/solution.py
+++ b/solution.py
@@ -141,7 +141,7 @@
 BLOCK = 512
 UPDATE_BLOCK = 256
 PARTS = 4
-LIMIT = 48
+LIMIT = 46
 PACK_PARTS = 4
 PACK_LIMIT = 60
 LANES = 128
@@ -175,9 +175,14 @@
 
 def collect(own, other):
     total = add_parts(own, [swap(other, CORE)])
-    parts = jnp.split(total, len(PLANE) + 1, axis=0)
-    sent = [swap(part.astype(jnp.bfloat16), mask) for part, mask in zip(parts[1:], PLANE)]
-    kept, sent = jnp.split(add_parts(parts[0], sent), 2, axis=0)
+    own, first, second, both = jnp.split(total, len(PLANE) + 1, axis=0)
+    half = total.shape[1] // 2
+    low = swap(both[:, :half].astype(jnp.bfloat16), PLANE[0])
+    high = swap(both[:, half:].astype(jnp.bfloat16), PLANE[1])
+    first = jnp.concatenate([first[:, :half], add_parts(first[:, half:], [high])], axis=1)
+    second = jnp.concatenate([add_parts(second[:, :half], [low]), second[:, half:]], axis=1)
+    sent = [swap(first.astype(jnp.bfloat16), PLANE[0]), swap(second.astype(jnp.bfloat16), PLANE[1])]
+    kept, sent = jnp.split(add_parts(own, sent), 2, axis=0)
     pair = add_parts(kept, [swap(sent.astype(jnp.bfloat16), LINE[1])]).astype(jnp.bfloat16)
     mine, its = jnp.split(pair, 2, axis=0)
     return add_parts(pair, [swap(jnp.concatenate([its, mine], axis=0), LINE[0])])
@@ -246,78 +251,102 @@
     )(tokens, expert_ids.T, gate_values.T)
 
 
-def expert_kernel(*refs):
-    pieces = refs[:8]
-    gate_ref, up_ref, down_ref, own_ref, other_ref, hidden_t_ref = refs[8:14]
-    gate_vm, up_vm, down_vm, rows, sems = refs[14:]
+def expert_kernel(held, *refs):
+    pieces, weights, refs = refs[:4], refs[4:7], refs[7:]
+    terms_ref, hidden_ref, refs = refs[0], refs[1], refs[2:]
+    rows = refs[0] if held else refs[3]
     count, width = rows.shape
-    part = count // 8
-    units = gate_vm.shape[0]
-    loads = [
-        [
-            pltpu.make_async_copy(
-                src.at[pl.ds(s * units // PARTS, units // PARTS)],
-                dst.at[pl.ds(s * units // PARTS, units // PARTS)],
-                sems.at[PARTS * k + s],
-            )
-            for s in range(PARTS)
+    part = count // 4
+    loads = [(), (), ()]
+    if not held:
+        units, sems = weights[0].shape[0], refs[4]
+        loads = [
+            [
+                pltpu.make_async_copy(
+                    src.at[pl.ds(s * units // PARTS, units // PARTS)],
+                    dst.at[pl.ds(s * units // PARTS, units // PARTS)],
+                    sems.at[PARTS * k + s],
+                )
+                for s in range(PARTS)
+            ]
+            for k, (src, dst) in enumerate(zip(weights, refs[:3]))
         ]
-        for k, (src, dst) in enumerate(
-            ((gate_ref, gate_vm), (up_ref, up_vm), (down_ref, down_vm))
-        )
-    ]
+        weights = refs[:3]
     for weight in loads:
         for load in weight:
             load.start()
-    for p in range(8):
+    for p in range(4):
         rows[p * part : (p + 1) * part] = pieces[p][:, :width]
     gates = jnp.concatenate([piece[:, width:] for piece in pieces], axis=0).astype(jnp.float32)
     lane = lax.broadcasted_iota(jnp.int32, gates.shape, 1)
     gates = jnp.where(lane == lax.axis_index("expert"), gates, 0.0)
     gate = jnp.sum(gates, axis=1, keepdims=True)
     contract = (((1,), (1,)), ((), ()))
-    for load in loads[0]:
-        load.wait()
-    gate_part = lax.dot_general(
-        rows[...], gate_vm[...], contract, preferred_element_type=jnp.float32
-    )
-    for load in loads[1]:
-        load.wait()
-    up_part = lax.dot_general(rows[...], up_vm[...], contract, preferred_element_type=jnp.float32)
-    hidden = gate * (jax.nn.silu(gate_part) * up_part)
-    hidden_t_ref[...] = hidden.T.astype(jnp.bfloat16)
-    hidden = hidden.astype(jnp.bfloat16)
+    products = []
+    for k in range(2):
+        for load in loads[k]:
+            load.wait()
+        products.append(
+            lax.dot_general(
+                rows[...], weights[k][...], contract, preferred_element_type=jnp.float32
+            )
+        )
+    hidden = (gate * (jax.nn.silu(products[0]) * products[1])).astype(jnp.bfloat16)
+    hidden_ref[...] = hidden
     for load in loads[2]:
         load.wait()
     for start in range(0, width, BLOCK):
         span = slice(start, start + BLOCK)
-        terms = jnp.dot(hidden, down_vm[:, span], preferred_element_type=jnp.float32)
-        terms = terms.astype(jnp.bfloat16)
-        own_ref[:, span] = terms[: count // 2]
-        other_ref[:, span] = terms[count // 2 :]
-
-
-def expert_terms(pieces, gate_weight, up_weight, down_weight):
-    units, width = gate_weight.shape
-    count = 8 * pieces[0].shape[0]
-    half = jax.ShapeDtypeStruct((count // 2, width), jnp.bfloat16)
+        terms = jnp.dot(hidden, weights[2][:, span], preferred_element_type=jnp.float32)
+        terms_ref[:, span] = terms.astype(jnp.bfloat16)
+
+
+def expert_terms(pieces, weights, held):
+    units, width = weights[0].shape
+    count = 4 * pieces[0].shape[0]
     in_vmem = pl.BlockSpec(memory_space=pltpu.VMEM)
     in_hbm = pl.BlockSpec(memory_space=pltpu.HBM)
+    out_shape = [
+        jax.ShapeDtypeStruct((count, width), jnp.bfloat16),
+        jax.ShapeDtypeStruct((count, units), jnp.bfloat16),
+    ]
+    scratch = [pltpu.VMEM((count, width), jnp.bfloat16)]
+    if not held:
+        out_shape += [jax.ShapeDtypeStruct((units, width), jnp.bfloat16)] * 3
+        scratch += [pltpu.SemaphoreType.DMA((3 * PARTS,))]
     return pl.pallas_call(
-        expert_kernel,
-        out_shape=[half, half, jax.ShapeDtypeStruct((units, count), jnp.bfloat16)],
-        in_specs=[in_vmem] * 8 + [in_hbm] * 3,
-        out_specs=[in_vmem] * 3,
-        scratch_shapes=[pltpu.VMEM((units, width), jnp.bfloat16)] * 3
-        + [pltpu.VMEM((count, width), jnp.bfloat16), pltpu.SemaphoreType.DMA((3 * PARTS,))],
-        compiler_params=pltpu.CompilerParams(vmem_limit_bytes=LIMIT * MIB),
+        functools.partial(expert_kernel, held),
+        out_shape=out_shape,
+        in_specs=[in_vmem] * 4 + [in_vmem if held else in_hbm] * 3,
+        out_specs=[in_vmem] * len(out_shape),
+        scratch_shapes=scratch,
+        compiler_params=pltpu.CompilerParams(vmem_limit_bytes=(16 if held else LIMIT) * MIB),
         cost_estimate=pl.CostEstimate(
             flops=6 * count * units * width,
-            bytes_accessed=10 * count * width,
+            bytes_accessed=8 * units * width,
             transcendentals=count * units,
         ),
         name="expert_terms",
-    )(*pieces, gate_weight, up_weight, down_weight)
+    )(*pieces, *weights)
+
+
+def turn_kernel(first_ref, second_ref, out_ref):
+    hidden = jnp.concatenate([first_ref[...], second_ref[...]], axis=0)
+    out_ref[...] = hidden.astype(jnp.float32).T.astype(jnp.bfloat16)
+
+
+def turn(first, second):
+    return pl.pallas_call(
+        turn_kernel,
+        out_shape=jax.ShapeDtypeStruct((first.shape[1], 2 * first.shape[0]), jnp.bfloat16),
+        in_specs=[pl.BlockSpec(memory_space=pltpu.VMEM)] * 2,
+        out_specs=pl.BlockSpec(memory_space=pltpu.VMEM),
+        compiler_params=pltpu.CompilerParams(vmem_limit_bytes=8 * MIB),
+        cost_estimate=pl.CostEstimate(
+            flops=0, bytes_accessed=8 * first.size, transcendentals=0
+        ),
+        name="turn",
+    )(first, second)
 
 
 def update_kernel(*refs):
@@ -385,7 +414,10 @@
     pieces = spread(pack(tokens, expert_ids, gate_values, experts))
     pair_tokens = pieces[0][: 2 * (experts * 3 // 4), :width].astype(jnp.float32)
     pieces += to_core(pieces)
-    own, other, hidden_t = expert_terms(pieces, gate_weight[0], up_weight[0], down_weight[0])
+    weights = (gate_weight[0], up_weight[0], down_weight[0])
+    own, own_hidden, *held = expert_terms(pieces[:4], weights, False)
+    other, other_hidden = expert_terms(pieces[4:], held, True)
+    hidden_t = turn(own_hidden, other_hidden)
     cotangent = jnp.tanh(pair_tokens + collect(own, other)).astype(jnp.bfloat16)
     cotangent = jnp.concatenate([cotangent, swap(cotangent, LINE[1])], axis=0)
     pieces = across(cotangent)

time: 89.1 us -> 87 us (0.976)
  waiting for transfers between devices: 52.8 us -> 48.3 us
  starting transfers between devices: 21.4 us -> 22.8 us
  Pallas kernels: 12.3 us -> 13.2 us
    ppermute x24 -> x25, waiting for transfers between devices: 52.8 us -> 48.3 us  [swap(): return lax.ppermute(block, AXES, [(i, i ^ mask) for i in range(count)])]
    ppermute x24 -> x25, starting transfers between devices: 21.4 us -> 22.8 us  [swap(): return lax.ppermute(block, AXES, [(i, i ^ mask) for i in range(count)])]
    pallas_call x1 -> x3, Pallas kernels: 5.3 us -> 6.2 us  [the longest x2 6.04 us: expert_terms(): pl.pallas_call(functools.partial(expert_kernel, held), out_shape=out_shap...]
  transfers between devices with their start and end apart: 24 -> 25, of which waited for: 19 -> 18; matrix products, arithmetic and copies ran while one was open for 0% -> 0% of each run, Pallas kernels for 0% -> 5%
where the time goes in v5:
time: 87 us; the launch traced here: 86.9 us
  waiting for transfers between devices  48.3 us (56%)
  starting transfers between devices  22.8 us (26%)
  Pallas kernels  13.2 us (15%)
  other arithmetic  1.62 us (2%)
    ppermute x25, waiting for transfers between devices, swap(): return lax.ppermute(block, AXES, [(i, i ^ mask) for i in range(count)])  48.3 us
    ppermute x25, starting transfers between devices, swap(): return lax.ppermute(block, AXES, [(i, i ^ mask) for i in range(count)])  22.8 us
    pallas_call x2, Pallas kernels, expert_terms(): pl.pallas_call(functools.partial(expert_kernel, held), out_shape=out_shap...  6.04 us
    pallas_call x1, Pallas kernels, update(): pl.pallas_call(update_kernel, out_shape=[jax.ShapeDtypeStruct((units, wid...  4.91 us
    pallas_call x1, Pallas kernels, pack(): pl.pallas_call(functools.partial(pack_kernel, experts), out_shape=jax.Sha...  2.07 us
  transfers between devices with their start and end apart: 25, of which 18 were waited for; matrix products, arithmetic and copies ran while one was open for 0% of the time, Pallas kernels for 5%

profile of v5, /device:TPU:0, one launch (start us, length us, event | category | flops | bytes accessed | tf_op | source)
XLA Modules:
  0.0 86.9 jit_solution(7067109348920394398)
XLA Ops:
  0.6 2.1 %pack.1 = bf16[12,2688]{1,0:T(8,128)(2,1)} custom-call(bf16[128,2560]{1,0:T(8,128)(2,1)} %tokens_ref.1, s32[6,128]{1,0:T(8,128)} %bitcast.16, bf16[6,128]{1,0:T(8,128)(2,1)} %bitcast.17), custom_call_target="tpu_custom_call" | custom-call | tf_op jit(solution)/shard_map/pack/pallas_call | solution.py:238
  2.7 5.1 %collective-permute-start.2 = (bf16[12,2688]{1,0:T(8,128)(2,1)}, bf16[12,2688]{1,0:T(8,128)(2,1)S(1)}, u32[]{:S(2)}, u32[]{:S(2)}) collective-permute-start(bf16[12,2688]{1,0:T(8,128)(2,1)} %pack.1), channel_id=1, source_target_pairs={{0,12},{1,13},{2,14},{3,15},{4,8},{5,9},{6,10},{7,11},{8,4},{9,5},... | collective-permute-start | bytes 193544 | tf_op jit(solution)/shard_map/ppermute | solution.py:153
  7.8 0.0 collective-permute-start.1
  7.8 0.6 collective-permute-start
  8.5 3.0 %collective-permute-done.2 = bf16[12,2688]{1,0:T(8,128)(2,1)S(1)} collective-permute-done((bf16[12,2688]{1,0:T(8,128)(2,1)}, bf16[12,2688]{1,0:T(8,128)(2,1)S(1)}, u32[]{:S(2)}, u32[]{:S(2)}) %collective-permute-start.2) | collective-permute-done | bytes 64544 | tf_op jit(solution)/shard_map/ppermute | solution.py:153
  11.5 2.7 %collective-permute-done.1 = bf16[12,2688]{1,0:T(8,128)(2,1)S(1)} collective-permute-done((bf16[12,2688]{1,0:T(8,128)(2,1)}, bf16[12,2688]{1,0:T(8,128)(2,1)S(1)}, u32[]{:S(2)}, u32[]{:S(2)}) %collective-permute-start.1) | collective-permute-done | bytes 64544 | tf_op jit(solution)/shard_map/ppermute | solution.py:153
  14.2 1.0 %collective-permute-done = bf16[12,2688]{1,0:T(8,128)(2,1)S(1)} collective-permute-done((bf16[12,2688]{1,0:T(8,128)(2,1)}, bf16[12,2688]{1,0:T(8,128)(2,1)S(1)}, u32[]{:S(2)}, u32[]{:S(2)}) %collective-permute-start) | collective-permute-done | bytes 64544 | tf_op jit(solution)/shard_map/ppermute | solution.py:153
  15.2 1.0 %pad_maximum_fusion.refs_0_ = bf16[48,2688]{1,0:T(8,128)(2,1)S(1)} fusion(bf16[12,2688]{1,0:T(8,128)(2,1)S(1)} %collective-permute-done.2, bf16[12,2688]{1,0:T(8,128)(2,1)S(1)} %collective-permute-done.1, bf16[12,2688]{1,0:T(8,128)(2,1)S(1)} %collective-permute-done, bf16[12,2688]{1,0:T(8,128)(2,1)} %pack.1), kind=kLoop, calls=%fused_computation.3 | loop fusion | flops 1032192 | bytes 516096 | tf_op jit(solution)/shard_map/concatenate | solution.py:157
  16.2 2.5 %collective-permute-start.5 = (bf16[48,2688]{1,0:T(8,128)(2,1)S(1)}, bf16[48,2688]{1,0:T(8,128)(2,1)S(1)}, u32[]{:S(2)}, u32[]{:S(2)}) collective-permute-start(bf16[48,2688]{1,0:T(8,128)(2,1)S(1)} %pad_maximum_fusion.refs_0_), channel_id=1, source_target_pairs={{0,18},{1,19},{2,16},{3,17},{4,22},{5,23},{6,20},{7,21},{8,26},{9,... | collective-permute-start | bytes 774152 | tf_op jit(solution)/shard_map/ppermute | solution.py:153
  18.7 0.5 collective-permute-start.4
  19.2 0.5 collective-permute-start.3
  19.8 0.0 collective-permute-start.6
  19.8 6.1 %collective-permute-done.5.refs_3_ = bf16[48,2688]{1,0:T(8,128)(2,1)S(1)} collective-permute-done((bf16[48,2688]{1,0:T(8,128)(2,1)S(1)}, bf16[48,2688]{1,0:T(8,128)(2,1)S(1)}, u32[]{:S(2)}, u32[]{:S(2)}) %collective-permute-start.5) | collective-permute-done | bytes 258080 | tf_op jit(solution)/shard_map/ppermute | solution.py:153
  25.9 0.0 collective-permute-start.9
  25.9 2.7 %collective-permute-done.4.refs_2_ = bf16[48,2688]{1,0:T(8,128)(2,1)S(1)} collective-permute-done((bf16[48,2688]{1,0:T(8,128)(2,1)S(1)}, bf16[48,2688]{1,0:T(8,128)(2,1)S(1)}, u32[]{:S(2)}, u32[]{:S(2)}) %collective-permute-start.4) | collective-permute-done | bytes 258080 | tf_op jit(solution)/shard_map/ppermute | solution.py:153
  28.6 0.0 collective-permute-start.8
  28.6 0.2 collective-permute-done.3.refs_1_
  28.8 0.3 collective-permute-start.7
  29.1 4.0 %expert_terms.2 = (bf16[192,2560]{1,0:T(8,128)(2,1)S(1)}, bf16[192,384]{1,0:T(8,128)(2,1)S(1)}, bf16[384,2560]{1,0:T(8,128)(2,1)S(1)}, bf16[384,2560]{1,0:T(8,128)(2,1)S(1)}, bf16[384,2560]{1,0:T(8,128)(2,1)S(1)}) custom-call(bf16[48,2688]{1,0:T(8,128)(2,1)S(1)} %pad_maximum_fusion.refs_0_, bf16[48,2688]{1,0:T(8,128)(2,1)S(1)} %collective-permute-done.3.refs_1_, ...), custom_call_target="tpu_custom_call" | custom-call | flops 1132462080 | bytes 7864320 | tf_op jit(solution)/shard_map/expert_terms/pallas_call | solution.py:317
  33.2 0.0 collective-permute-done.6.refs_0_
  33.2 0.0 collective-permute-done.9.refs_3_
  33.2 0.0 collective-permute-done.8.refs_2_
  33.2 0.0 collective-permute-done.7.refs_1_
  33.2 2.0 %expert_terms.3 = (bf16[192,2560]{1,0:T(8,128)(2,1)S(1)}, bf16[192,384]{1,0:T(8,128)(2,1)S(1)}) custom-call(bf16[48,2688]{1,0:T(8,128)(2,1)S(1)} %collective-permute-done.6.refs_0_, bf16[48,2688]{1,0:T(8,128)(2,1)S(1)} %collective-permute-done.7.refs_1_, bf16[48,2688]{1,0:T(8,128)(2,1)S(1)} %collective-permute-done.8.refs_2_, ...), custom_call_target="tpu_custom_call" | custom-call | flops 1132462080 | bytes 7864320 | tf_op jit(solution)/shard_map/expert_terms/pallas_call | solution.py:317
  35.2 0.3 collective-permute-start.10
  35.5 2.3 %collective-permute-done.10 = bf16[192,2560]{1,0:T(8,128)(2,1)S(1)} collective-permute-done((bf16[192,2560]{1,0:T(8,128)(2,1)S(1)}, bf16[192,2560]{1,0:T(8,128)(2,1)S(1)}, u32[]{:S(2)}, u32[]{:S(2)}) %collective-permute-start.10) | collective-permute-done | bytes 983072 | tf_op jit(solution)/shard_map/ppermute | solution.py:153
  37.8 0.3 fusion.4
  38.2 1.7 %collective-permute-start.13 = (bf16[48,1280]{1,0:T(8,128)(2,1)S(1)}, bf16[48,1280]{1,0:T(8,128)(2,1)S(1)}, u32[]{:S(2)}, u32[]{:S(2)}) collective-permute-start(bf16[48,1280]{1,0:T(8,128)(2,1)S(1)} %get-tuple-element.29), channel_id=1, source_target_pairs={{0,2},{1,3},{2,0},{3,1},{4,6},{5,7},{6,4},{7,5},{8,10},{9,11},{10,... | collective-permute-start | bytes 368648 | tf_op jit(solution)/shard_map/ppermute | solution.py:153
  39.9 0.7 collective-permute-start.11
  40.6 3.1 %collective-permute-done.13 = bf16[48,1280]{1,0:T(8,128)(2,1)S(1)} collective-permute-done((bf16[48,1280]{1,0:T(8,128)(2,1)S(1)}, bf16[48,1280]{1,0:T(8,128)(2,1)S(1)}, u32[]{:S(2)}, u32[]{:S(2)}) %collective-permute-start.13) | collective-permute-done | bytes 122912 | tf_op jit(solution)/shard_map/ppermute | solution.py:153
  43.7 1.3 %collective-permute-done.11 = bf16[48,1280]{1,0:T(8,128)(2,1)S(1)} collective-permute-done((bf16[48,1280]{1,0:T(8,128)(2,1)S(1)}, bf16[48,1280]{1,0:T(8,128)(2,1)S(1)}, u32[]{:S(2)}, u32[]{:S(2)}) %collective-permute-start.11) | collective-permute-done | bytes 122912 | tf_op jit(solution)/shard_map/ppermute | solution.py:153
  45.0 0.0 copy-start.3
  45.1 0.8 collective-permute-start.14
  45.9 0.0 copy-start
  45.9 0.0 copy-start.1
  45.9 1.4 %collective-permute-start.12 = (bf16[48,2560]{1,0:T(8,128)(2,1)S(1)}, bf16[48,2560]{1,0:T(8,128)(2,1)S(1)}, u32[]{:S(2)}, u32[]{:S(2)}) collective-permute-start(bf16[48,2560]{1,0:T(8,128)(2,1)S(1)} %pad_maximum_fusion.1), channel_id=1, source_target_pairs={{0,2},{1,3},{2,0},{3,1},{4,6},{5,7},{6,4},{7,5},{8,10},{9,11},{10,... | collective-permute-start | bytes 737288 | tf_op jit(solution)/shard_map/ppermute | solution.py:153
  47.3 4.7 %collective-permute-done.14 = bf16[48,2560]{1,0:T(8,128)(2,1)S(1)} collective-permute-done((bf16[48,2560]{1,0:T(8,128)(2,1)S(1)}, bf16[48,2560]{1,0:T(8,128)(2,1)S(1)}, u32[]{:S(2)}, u32[]{:S(2)}) %collective-permute-start.14) | collective-permute-done | bytes 245792 | tf_op jit(solution)/shard_map/ppermute | solution.py:153
  52.0 0.5 collective-permute-done.12
  52.5 0.1 fusion
  52.6 0.9 %collective-permute-start.15 = (bf16[24,2560]{1,0:T(8,128)(2,1)S(1)}, bf16[24,2560]{1,0:T(8,128)(2,1)S(1)}, u32[]{:S(2)}, u32[]{:S(2)}) collective-permute-start(bf16[24,2560]{1,0:T(8,128)(2,1)S(1)} %split.36), channel_id=1, source_target_pairs={{0,4},{1,5},{2,6},{3,7},{4,0},{5,1},{6,2},{7,3},{8,12},{9,13},{10,... | collective-permute-start | bytes 368648 | tf_op jit(solution)/shard_map/ppermute | solution.py:153
  53.5 4.1 %collective-permute-done.15 = bf16[24,2560]{1,0:T(8,128)(2,1)S(1)} collective-permute-done((bf16[24,2560]{1,0:T(8,128)(2,1)S(1)}, bf16[24,2560]{1,0:T(8,128)(2,1)S(1)}, u32[]{:S(2)}, u32[]{:S(2)}) %collective-permute-start.15) | collective-permute-done | bytes 122912 | tf_op jit(solution)/shard_map/ppermute | solution.py:153
  57.7 3.4 %collective-permute-start.16 = (bf16[24,2560]{1,0:T(8,128)(2,1)S(1)}, bf16[24,2560]{1,0:T(8,128)(2,1)S(1)}, u32[]{:S(2)}, u32[]{:S(2)}) collective-permute-start(bf16[24,2560]{1,0:T(8,128)(2,1)S(1)} %pad_maximum_fusion.5), channel_id=1, source_target_pairs={{0,8},{1,9},{2,10},{3,11},{4,12},{5,13},{6,14},{7,15},{8,0},{9,1},... | collective-permute-start | bytes 368648 | tf_op jit(solution)/shard_map/ppermute | solution.py:153
  61.0 4.2 %collective-permute-done.16 = bf16[24,2560]{1,0:T(8,128)(2,1)S(1)} collective-permute-done((bf16[24,2560]{1,0:T(8,128)(2,1)S(1)}, bf16[24,2560]{1,0:T(8,128)(2,1)S(1)}, u32[]{:S(2)}, u32[]{:S(2)}) %collective-permute-start.16) | collective-permute-done | bytes 122912 | tf_op jit(solution)/shard_map/ppermute | solution.py:153
  65.2 0.0 copy-done.3
  65.2 0.1 tanh_convert_fusion
  65.3 0.1 collective-permute-start.17
  65.4 4.9 %collective-permute-done.17 = bf16[24,2560]{1,0:T(8,128)(2,1)S(1)} collective-permute-done((bf16[24,2560]{1,0:T(8,128)(2,1)S(1)}, bf16[24,2560]{1,0:T(8,128)(2,1)S(1)}, u32[]{:S(2)}, u32[]{:S(2)}) %collective-permute-start.17) | collective-permute-done | bytes 122912 | tf_op jit(solution)/shard_map/ppermute | solution.py:153
  70.3 1.2 %collective-permute-start.20 = (bf16[48,2560]{1,0:T(8,128)(2,1)S(1)}, bf16[48,2560]{1,0:T(8,128)(2,1)S(1)}, u32[]{:S(2)}, u32[]{:S(2)}) collective-permute-start(bf16[48,2560]{1,0:T(8,128)(2,1)S(1)} %pad_maximum_fusion.3.refs_0_), channel_id=1, source_target_pairs={{0,18},{1,19},{2,16},{3,17},{4,22},{5,23},{6,20},{7,21},{8,26},{9,... | collective-permute-start | bytes 737288 | tf_op jit(solution)/shard_map/ppermute | solution.py:153
  71.5 1.5 %collective-permute-start.19 = (bf16[48,2560]{1,0:T(8,128)(2,1)S(1)}, bf16[48,2560]{1,0:T(8,128)(2,1)S(1)}, u32[]{:S(2)}, u32[]{:S(2)}) collective-permute-start(bf16[48,2560]{1,0:T(8,128)(2,1)S(1)} %pad_maximum_fusion.3.refs_0_), channel_id=1, source_target_pairs={{0,16},{1,17},{2,18},{3,19},{4,20},{5,21},{6,22},{7,23},{8,24},{9,... | collective-permute-start | bytes 737288 | tf_op jit(solution)/shard_map/ppermute | solution.py:153
  73.0 0.8 collective-permute-start.18
  73.8 0.0 collective-permute-start.21
  73.8 3.7 %collective-permute-done.20.refs_3_ = bf16[48,2560]{1,0:T(8,128)(2,1)S(1)} collective-permute-done((bf16[48,2560]{1,0:T(8,128)(2,1)S(1)}, bf16[48,2560]{1,0:T(8,128)(2,1)S(1)}, u32[]{:S(2)}, u32[]{:S(2)}) %collective-permute-start.20) | collective-permute-done | bytes 245792 | tf_op jit(solution)/shard_map/ppermute | solution.py:153
  77.5 0.0 collective-permute-start.24
  77.5 2.5 %collective-permute-done.19.refs_2_ = bf16[48,2560]{1,0:T(8,128)(2,1)S(1)} collective-permute-done((bf16[48,2560]{1,0:T(8,128)(2,1)S(1)}, bf16[48,2560]{1,0:T(8,128)(2,1)S(1)}, u32[]{:S(2)}, u32[]{:S(2)}) %collective-permute-start.19) | collective-permute-done | bytes 245792 | tf_op jit(solution)/shard_map/ppermute | solution.py:153
  80.1 0.0 collective-permute-start.23
  80.1 0.0 collective-permute-done.18.refs_1_
  80.1 0.5 collective-permute-start.22
  80.6 0.2 turn.1.refs_8_
  80.8 0.0 collective-permute-done.21.refs_4_
  80.8 0.0 collective-permute-done.24.refs_7_
  80.8 0.8 collective-permute-done.23.refs_6_
  81.6 0.4 collective-permute-done.22.refs_5_
  81.9 0.0 copy-done.2
  81.9 4.9 %update.1 = (bf16[384,2560]{1,0:T(8,128)(2,1)}, bf16[384,2560]{1,0:T(8,128)(2,1)}, bf16[384,2560]{1,0:T(8,128)(2,1)}) custom-call(bf16[48,2560]{1,0:T(8,128)(2,1)S(1)} %pad_maximum_fusion.3.refs_0_, bf16[48,2560]{1,0:T(8,128)(2,1)S(1)} %collective-permute-done.18.refs_1_, bf16[48,2560]{1,0:T(8,128)(2,1)S(1)} %collective-permute-done.19.refs_2_, ...), custom_call_target="tpu_custom_call" | custom-call | flops 754974720 | bytes 13762560 | tf_op jit(solution)/shard_map/update/pallas_call | solution.py:385
  (12 shorter events, 0.2 us)
Async XLA Ops:
  2.7 8.8 %collective-permute-start.2 = (bf16[12,2688]{1,0:T(8,128)(2,1)}, bf16[12,2688]{1,0:T(8,128)(2,1)S(1)}, u32[]{:S(2)}, u32[]{:S(2)}) collective-permute-start(bf16[12,2688]{1,0:T(8,128)(2,1)} %pack.1), channel_id=1, source_target_pairs={{0,12},{1,13},{2,14},{3,15},{4,8},{5,9},{6,10},{7,11},{8,4},{9,5},... | collective-permute-start | bytes 193544 | tf_op jit(solution)/shard_map/ppermute | solution.py:153
  7.8 6.4 %collective-permute-start.1 = (bf16[12,2688]{1,0:T(8,128)(2,1)}, bf16[12,2688]{1,0:T(8,128)(2,1)S(1)}, u32[]{:S(2)}, u32[]{:S(2)}) collective-permute-start(bf16[12,2688]{1,0:T(8,128)(2,1)} %pack.1), channel_id=1, source_target_pairs={{0,4},{1,5},{2,6},{3,7},{4,0},{5,1},{6,2},{7,3},{8,12},{9,13},{10,... | collective-permute-start | bytes 193544 | tf_op jit(solution)/shard_map/ppermute | solution.py:153
  7.8 7.4 %collective-permute-start = (bf16[12,2688]{1,0:T(8,128)(2,1)}, bf16[12,2688]{1,0:T(8,128)(2,1)S(1)}, u32[]{:S(2)}, u32[]{:S(2)}) collective-permute-start(bf16[12,2688]{1,0:T(8,128)(2,1)} %pack.1), channel_id=1, source_target_pairs={{0,8},{1,9},{2,10},{3,11},{4,12},{5,13},{6,14},{7,15},{8,0},{9,1},... | collective-permute-start | bytes 193544 | tf_op jit(solution)/shard_map/ppermute | solution.py:153
  16.2 9.7 %collective-permute-start.5 = (bf16[48,2688]{1,0:T(8,128)(2,1)S(1)}, bf16[48,2688]{1,0:T(8,128)(2,1)S(1)}, u32[]{:S(2)}, u32[]{:S(2)}) collective-permute-start(bf16[48,2688]{1,0:T(8,128)(2,1)S(1)} %pad_maximum_fusion.refs_0_), channel_id=1, source_target_pairs={{0,18},{1,19},{2,16},{3,17},{4,22},{5,23},{6,20},{7,21},{8,26},{9,... | collective-permute-start | bytes 774152 | tf_op jit(solution)/shard_map/ppermute | solution.py:153
  18.7 9.9 %collective-permute-start.4 = (bf16[48,2688]{1,0:T(8,128)(2,1)S(1)}, bf16[48,2688]{1,0:T(8,128)(2,1)S(1)}, u32[]{:S(2)}, u32[]{:S(2)}) collective-permute-start(bf16[48,2688]{1,0:T(8,128)(2,1)S(1)} %pad_maximum_fusion.refs_0_), channel_id=1, source_target_pairs={{0,16},{1,17},{2,18},{3,19},{4,20},{5,21},{6,22},{7,23},{8,24},{9,... | collective-permute-start | bytes 774152 | tf_op jit(solution)/shard_map/ppermute | solution.py:153
  19.2 9.6 %collective-permute-start.3 = (bf16[48,2688]{1,0:T(8,128)(2,1)S(1)}, bf16[48,2688]{1,0:T(8,128)(2,1)S(1)}, u32[]{:S(2)}, u32[]{:S(2)}) collective-permute-start(bf16[48,2688]{1,0:T(8,128)(2,1)S(1)} %pad_maximum_fusion.refs_0_), channel_id=1, source_target_pairs={{0,2},{1,3},{2,0},{3,1},{4,6},{5,7},{6,4},{7,5},{8,10},{9,11},{10,... | collective-permute-start | bytes 774152 | tf_op jit(solution)/shard_map/ppermute | solution.py:153
  19.8 13.4 %collective-permute-start.6 = (bf16[48,2688]{1,0:T(8,128)(2,1)S(1)}, bf16[48,2688]{1,0:T(8,128)(2,1)S(1)}, u32[]{:S(2)}, u32[]{:S(2)}) collective-permute-start(bf16[48,2688]{1,0:T(8,128)(2,1)S(1)} %pad_maximum_fusion.refs_0_), channel_id=1, source_target_pairs={{0,1},{1,0},{2,3},{3,2},{4,5},{5,4},{6,7},{7,6},{8,9},{9,8},{10,11... | collective-permute-start | bytes 774152 | tf_op jit(solution)/shard_map/ppermute | solution.py:153
  25.9 7.3 %collective-permute-start.9 = (bf16[48,2688]{1,0:T(8,128)(2,1)S(1)}, bf16[48,2688]{1,0:T(8,128)(2,1)S(1)}, u32[]{:S(2)}, u32[]{:S(2)}) collective-permute-start(bf16[48,2688]{1,0:T(8,128)(2,1)S(1)} %collective-permute-done.5.refs_3_), channel_id=1, source_target_pairs={{0,1},{1,0},{2,3},{3,2},{4,5},{5,4},{6,7},{7,6},{8,9},{9,8},{10,11... | collective-permute-start | bytes 774152 | tf_op jit(solution)/shard_map/ppermute | solution.py:153
  28.6 4.6 %collective-permute-start.8 = (bf16[48,2688]{1,0:T(8,128)(2,1)S(1)}, bf16[48,2688]{1,0:T(8,128)(2,1)S(1)}, u32[]{:S(2)}, u32[]{:S(2)}) collective-permute-start(bf16[48,2688]{1,0:T(8,128)(2,1)S(1)} %collective-permute-done.4.refs_2_), channel_id=1, source_target_pairs={{0,1},{1,0},{2,3},{3,2},{4,5},{5,4},{6,7},{7,6},{8,9},{9,8},{10,11... | collective-permute-start | bytes 774152 | tf_op jit(solution)/shard_map/ppermute | solution.py:153
  28.8 4.4 %collective-permute-start.7 = (bf16[48,2688]{1,0:T(8,128)(2,1)S(1)}, bf16[48,2688]{1,0:T(8,128)(2,1)S(1)}, u32[]{:S(2)}, u32[]{:S(2)}) collective-permute-start(bf16[48,2688]{1,0:T(8,128)(2,1)S(1)} %collective-permute-done.3.refs_1_), channel_id=1, source_target_pairs={{0,1},{1,0},{2,3},{3,2},{4,5},{5,4},{6,7},{7,6},{8,9},{9,8},{10,11... | collective-permute-start | bytes 774152 | tf_op jit(solution)/shard_map/ppermute | solution.py:153
  35.2 2.6 %collective-permute-start.10 = (bf16[192,2560]{1,0:T(8,128)(2,1)S(1)}, bf16[192,2560]{1,0:T(8,128)(2,1)S(1)}, u32[]{:S(2)}, u32[]{:S(2)}) collective-permute-start(bf16[192,2560]{1,0:T(8,128)(2,1)S(1)} %get-tuple-element.17), channel_id=1, source_target_pairs={{0,1},{1,0},{2,3},{3,2},{4,5},{5,4},{6,7},{7,6},{8,9},{9,8},{10,11... | collective-permute-start | bytes 2949128 | tf_op jit(solution)/shard_map/ppermute | solution.py:153
  38.2 5.5 %collective-permute-start.13 = (bf16[48,1280]{1,0:T(8,128)(2,1)S(1)}, bf16[48,1280]{1,0:T(8,128)(2,1)S(1)}, u32[]{:S(2)}, u32[]{:S(2)}) collective-permute-start(bf16[48,1280]{1,0:T(8,128)(2,1)S(1)} %get-tuple-element.29), channel_id=1, source_target_pairs={{0,2},{1,3},{2,0},{3,1},{4,6},{5,7},{6,4},{7,5},{8,10},{9,11},{10,... | collective-permute-start | bytes 368648 | tf_op jit(solution)/shard_map/ppermute | solution.py:153
  39.9 5.1 %collective-permute-start.11 = (bf16[48,1280]{1,0:T(8,128)(2,1)S(1)}, bf16[48,1280]{1,0:T(8,128)(2,1)S(1)}, u32[]{:S(2)}, u32[]{:S(2)}) collective-permute-start(bf16[48,1280]{1,0:T(8,128)(2,1)S(1)} %get-tuple-element.30), channel_id=1, source_target_pairs={{0,16},{1,17},{2,18},{3,19},{4,20},{5,21},{6,22},{7,23},{8,24},{9,... | collective-permute-start | bytes 368648 | tf_op jit(solution)/shard_map/ppermute | solution.py:153
  45.0 37.0 %copy-start.2 = (bf16[1,384,2560]{2,1,0:T(8,128)(2,1)S(1)}, bf16[1,384,2560]{2,1,0:T(8,128)(2,1)}, u32[]{:S(2)}) copy-start(bf16[1,384,2560]{2,1,0:T(8,128)(2,1)} %param.15) | copy-start | bytes 5898244
  45.0 20.2 %copy-start.3 = (bf16[12,2688]{1,0:T(8,128)(2,1)S(1)}, bf16[12,2688]{1,0:T(8,128)(2,1)}, u32[]{:S(2)}) copy-start(bf16[12,2688]{1,0:T(8,128)(2,1)} %pack.1) | copy-start | bytes 193540
  45.1 6.9 %collective-permute-start.14 = (bf16[48,2560]{1,0:T(8,128)(2,1)S(1)}, bf16[48,2560]{1,0:T(8,128)(2,1)S(1)}, u32[]{:S(2)}, u32[]{:S(2)}) collective-permute-start(bf16[48,2560]{1,0:T(8,128)(2,1)S(1)} %pad_maximum_fusion.2), channel_id=1, source_target_pairs={{0,16},{1,17},{2,18},{3,19},{4,20},{5,21},{6,22},{7,23},{8,24},{9,... | collective-permute-start | bytes 737288 | tf_op jit(solution)/shard_map/ppermute | solution.py:153
  45.9 36.1 %copy-start = (bf16[1,384,2560]{2,1,0:T(8,128)(2,1)S(1)}, bf16[1,384,2560]{2,1,0:T(8,128)(2,1)}, u32[]{:S(2)}) copy-start(bf16[1,384,2560]{2,1,0:T(8,128)(2,1)} %param.13) | copy-start | bytes 5898244
  45.9 36.1 %copy-start.1 = (bf16[1,384,2560]{2,1,0:T(8,128)(2,1)S(1)}, bf16[1,384,2560]{2,1,0:T(8,128)(2,1)}, u32[]{:S(2)}) copy-start(bf16[1,384,2560]{2,1,0:T(8,128)(2,1)} %param.14) | copy-start | bytes 5898244
  45.9 6.6 %collective-permute-start.12 = (bf16[48,2560]{1,0:T(8,128)(2,1)S(1)}, bf16[48,2560]{1,0:T(8,128)(2,1)S(1)}, u32[]{:S(2)}, u32[]{:S(2)}) collective-permute-start(bf16[48,2560]{1,0:T(8,128)(2,1)S(1)} %pad_maximum_fusion.1), channel_id=1, source_target_pairs={{0,2},{1,3},{2,0},{3,1},{4,6},{5,7},{6,4},{7,5},{8,10},{9,11},{10,... | collective-permute-start | bytes 737288 | tf_op jit(solution)/shard_map/ppermute | solution.py:153
  52.6 4.9 %collective-permute-start.15 = (bf16[24,2560]{1,0:T(8,128)(2,1)S(1)}, bf16[24,2560]{1,0:T(8,128)(2,1)S(1)}, u32[]{:S(2)}, u32[]{:S(2)}) collective-permute-start(bf16[24,2560]{1,0:T(8,128)(2,1)S(1)} %split.36), channel_id=1, source_target_pairs={{0,4},{1,5},{2,6},{3,7},{4,0},{5,1},{6,2},{7,3},{8,12},{9,13},{10,... | collective-permute-start | bytes 368648 | tf_op jit(solution)/shard_map/ppermute | solution.py:153
  57.7 7.6 %collective-permute-start.16 = (bf16[24,2560]{1,0:T(8,128)(2,1)S(1)}, bf16[24,2560]{1,0:T(8,128)(2,1)S(1)}, u32[]{:S(2)}, u32[]{:S(2)}) collective-permute-start(bf16[24,2560]{1,0:T(8,128)(2,1)S(1)} %pad_maximum_fusion.5), channel_id=1, source_target_pairs={{0,8},{1,9},{2,10},{3,11},{4,12},{5,13},{6,14},{7,15},{8,0},{9,1},... | collective-permute-start | bytes 368648 | tf_op jit(solution)/shard_map/ppermute | solution.py:153
  65.3 4.9 %collective-permute-start.17 = (bf16[24,2560]{1,0:T(8,128)(2,1)S(1)}, bf16[24,2560]{1,0:T(8,128)(2,1)S(1)}, u32[]{:S(2)}, u32[]{:S(2)}) collective-permute-start(bf16[24,2560]{1,0:T(8,128)(2,1)S(1)} %tanh_convert_fusion), channel_id=1, source_target_pairs={{0,4},{1,5},{2,6},{3,7},{4,0},{5,1},{6,2},{7,3},{8,12},{9,13},{10,... | collective-permute-start | bytes 368648 | tf_op jit(solution)/shard_map/ppermute | solution.py:153
  70.3 7.3 %collective-permute-start.20 = (bf16[48,2560]{1,0:T(8,128)(2,1)S(1)}, bf16[48,2560]{1,0:T(8,128)(2,1)S(1)}, u32[]{:S(2)}, u32[]{:S(2)}) collective-permute-start(bf16[48,2560]{1,0:T(8,128)(2,1)S(1)} %pad_maximum_fusion.3.refs_0_), channel_id=1, source_target_pairs={{0,18},{1,19},{2,16},{3,17},{4,22},{5,23},{6,20},{7,21},{8,26},{9,... | collective-permute-start | bytes 737288 | tf_op jit(solution)/shard_map/ppermute | solution.py:153
  71.5 8.6 %collective-permute-start.19 = (bf16[48,2560]{1,0:T(8,128)(2,1)S(1)}, bf16[48,2560]{1,0:T(8,128)(2,1)S(1)}, u32[]{:S(2)}, u32[]{:S(2)}) collective-permute-start(bf16[48,2560]{1,0:T(8,128)(2,1)S(1)} %pad_maximum_fusion.3.refs_0_), channel_id=1, source_target_pairs={{0,16},{1,17},{2,18},{3,19},{4,20},{5,21},{6,22},{7,23},{8,24},{9,... | collective-permute-start | bytes 737288 | tf_op jit(solution)/shard_map/ppermute | solution.py:153
  73.0 7.0 %collective-permute-start.18 = (bf16[48,2560]{1,0:T(8,128)(2,1)S(1)}, bf16[48,2560]{1,0:T(8,128)(2,1)S(1)}, u32[]{:S(2)}, u32[]{:S(2)}) collective-permute-start(bf16[48,2560]{1,0:T(8,128)(2,1)S(1)} %pad_maximum_fusion.3.refs_0_), channel_id=1, source_target_pairs={{0,2},{1,3},{2,0},{3,1},{4,6},{5,7},{6,4},{7,5},{8,10},{9,11},{10,... | collective-permute-start | bytes 737288 | tf_op jit(solution)/shard_map/ppermute | solution.py:153
  73.8 6.9 %collective-permute-start.21 = (bf16[48,2560]{1,0:T(8,128)(2,1)S(1)}, bf16[48,2560]{1,0:T(8,128)(2,1)S(1)}, u32[]{:S(2)}, u32[]{:S(2)}) collective-permute-start(bf16[48,2560]{1,0:T(8,128)(2,1)S(1)} %pad_maximum_fusion.3.refs_0_), channel_id=1, source_target_pairs={{0,1},{1,0},{2,3},{3,2},{4,5},{5,4},{6,7},{7,6},{8,9},{9,8},{10,11... | collective-permute-start | bytes 737288 | tf_op jit(solution)/shard_map/ppermute | solution.py:153
  77.5 3.2 %collective-permute-start.24 = (bf16[48,2560]{1,0:T(8,128)(2,1)S(1)}, bf16[48,2560]{1,0:T(8,128)(2,1)S(1)}, u32[]{:S(2)}, u32[]{:S(2)}) collective-permute-start(bf16[48,2560]{1,0:T(8,128)(2,1)S(1)} %collective-permute-done.20.refs_3_), channel_id=1, source_target_pairs={{0,1},{1,0},{2,3},{3,2},{4,5},{5,4},{6,7},{7,6},{8,9},{9,8},{10,11... | collective-permute-start | bytes 737288 | tf_op jit(solution)/shard_map/ppermute | solution.py:153
  80.1 1.5 %collective-permute-start.23 = (bf16[48,2560]{1,0:T(8,128)(2,1)S(1)}, bf16[48,2560]{1,0:T(8,128)(2,1)S(1)}, u32[]{:S(2)}, u32[]{:S(2)}) collective-permute-start(bf16[48,2560]{1,0:T(8,128)(2,1)S(1)} %collective-permute-done.19.refs_2_), channel_id=1, source_target_pairs={{0,1},{1,0},{2,3},{3,2},{4,5},{5,4},{6,7},{7,6},{8,9},{9,8},{10,11... | collective-permute-start | bytes 737288 | tf_op jit(solution)/shard_map/ppermute | solution.py:153
  80.1 1.9 %collective-permute-start.22 = (bf16[48,2560]{1,0:T(8,128)(2,1)S(1)}, bf16[48,2560]{1,0:T(8,128)(2,1)S(1)}, u32[]{:S(2)}, u32[]{:S(2)}) collective-permute-start(bf16[48,2560]{1,0:T(8,128)(2,1)S(1)} %collective-permute-done.18.refs_1_), channel_id=1, source_target_pairs={{0,1},{1,0},{2,3},{3,2},{4,5},{5,4},{6,7},{7,6},{8,9},{9,8},{10,11... | collective-permute-start | bytes 737288 | tf_op jit(solution)/shard_map/ppermute | solution.py:153

commit v6 on v5

--- a/solution.py
+++ b/solution.py
@@ -174,9 +174,10 @@
 
 
 def collect(own, other):
-    total = add_parts(own, [swap(other, CORE)])
-    own, first, second, both = jnp.split(total, len(PLANE) + 1, axis=0)
-    half = total.shape[1] // 2
+    rows = own.shape[0] // (len(PLANE) + 1)
+    half = own.shape[1] // 2
+    both = add_parts(own[3 * rows :], [swap(other[1], CORE)])
+    own, first, second = jnp.split(add_parts(own[: 3 * rows], [swap(other[0], CORE)]), 3, axis=0)
     low = swap(both[:, :half].astype(jnp.bfloat16), PLANE[0])
     high = swap(both[:, half:].astype(jnp.bfloat16), PLANE[1])
     first = jnp.concatenate([first[:, :half], add_parts(first[:, half:], [high])], axis=1)
@@ -253,7 +254,8 @@
 
 def expert_kernel(held, *refs):
     pieces, weights, refs = refs[:4], refs[4:7], refs[7:]
-    terms_ref, hidden_ref, refs = refs[0], refs[1], refs[2:]
+    groups = 2 if held else 1
+    terms_refs, hidden_ref, refs = refs[:groups], refs[groups], refs[groups + 1 :]
     rows = refs[0] if held else refs[3]
     count, width = rows.shape
     part = count // 4
@@ -298,7 +300,11 @@
     for start in range(0, width, BLOCK):
         span = slice(start, start + BLOCK)
         terms = jnp.dot(hidden, weights[2][:, span], preferred_element_type=jnp.float32)
-        terms_ref[:, span] = terms.astype(jnp.bfloat16)
+        terms, done = terms.astype(jnp.bfloat16), 0
+        for terms_ref in terms_refs:
+            size = terms_ref.shape[0]
+            terms_ref[:, span] = terms[done : done + size]
+            done += size
 
 
 def expert_terms(pieces, weights, held):
@@ -306,10 +312,9 @@
     count = 4 * pieces[0].shape[0]
     in_vmem = pl.BlockSpec(memory_space=pltpu.VMEM)
     in_hbm = pl.BlockSpec(memory_space=pltpu.HBM)
-    out_shape = [
-        jax.ShapeDtypeStruct((count, width), jnp.bfloat16),
-        jax.ShapeDtypeStruct((count, units), jnp.bfloat16),
-    ]
+    groups = [count * 3 // 4, count // 4] if held else [count]
+    out_shape = [jax.ShapeDtypeStruct((size, width), jnp.bfloat16) for size in groups]
+    out_shape += [jax.ShapeDtypeStruct((count, units), jnp.bfloat16)]
     scratch = [pltpu.VMEM((count, width), jnp.bfloat16)]
     if not held:
         out_shape += [jax.ShapeDtypeStruct((units, width), jnp.bfloat16)] * 3
@@ -416,7 +421,7 @@
     pieces += to_core(pieces)
     weights = (gate_weight[0], up_weight[0], down_weight[0])
     own, own_hidden, *held = expert_terms(pieces[:4], weights, False)
-    other, other_hidden = expert_terms(pieces[4:], held, True)
+    *other, other_hidden = expert_terms(pieces[4:], held, True)
     hidden_t = turn(own_hidden, other_hidden)
     cotangent = jnp.tanh(pair_tokens + collect(own, other)).astype(jnp.bfloat16)
     cotangent = jnp.concatenate([cotangent, swap(cotangent, LINE[1])], axis=0)

time: 87 us -> 85.4 us (0.982)
  waiting for transfers between devices: 48.3 us -> 46.9 us
    ppermute x25 -> x26, waiting for transfers between devices: 48.3 us -> 46.9 us  [swap(): return lax.ppermute(block, AXES, [(i, i ^ mask) for i in range(count)])]
    ppermute x25 -> x26, starting transfers between devices: 22.8 us -> 22.6 us  [swap(): return lax.ppermute(block, AXES, [(i, i ^ mask) for i in range(count)])]
  transfers between devices with their start and end apart: 25 -> 26, of which waited for: 18 -> 19; matrix products, arithmetic and copies ran while one was open for 0% -> 0% of each run, Pallas kernels for 5% -> 5%
where the time goes in v6:
time: 85.4 us; the launch traced here: 85.3 us
  waiting for transfers between devices  46.9 us (55%)
  starting transfers between devices  22.6 us (26%)
  Pallas kernels  13.2 us (15%)
  other arithmetic  1.58 us (2%)
    ppermute x26, waiting for transfers between devices, swap(): return lax.ppermute(block, AXES, [(i, i ^ mask) for i in range(count)])  46.9 us
    ppermute x26, starting transfers between devices, swap(): return lax.ppermute(block, AXES, [(i, i ^ mask) for i in range(count)])  22.6 us
    pallas_call x2, Pallas kernels, expert_terms(): pl.pallas_call(functools.partial(expert_kernel, held), out_shape=out_shap...  6.03 us
    pallas_call x1, Pallas kernels, update(): pl.pallas_call(update_kernel, out_shape=[jax.ShapeDtypeStruct((units, wid...  4.93 us
    pallas_call x1, Pallas kernels, pack(): pl.pallas_call(functools.partial(pack_kernel, experts), out_shape=jax.Sha...  2.07 us
  transfers between devices with their start and end apart: 26, of which 19 were waited for; matrix products, arithmetic and copies ran while one was open for 0% of the time, Pallas kernels for 5%

profile of v6, /device:TPU:0, one launch (start us, length us, event | category | flops | bytes accessed | tf_op | source)
XLA Modules:
  0.0 85.3 jit_solution(14236214394886919838)
XLA Ops:
  0.6 2.1 %pack.1 = bf16[12,2688]{1,0:T(8,128)(2,1)} custom-call(bf16[128,2560]{1,0:T(8,128)(2,1)} %tokens_ref.1, s32[6,128]{1,0:T(8,128)} %bitcast.16, bf16[6,128]{1,0:T(8,128)(2,1)} %bitcast.17), custom_call_target="tpu_custom_call" | custom-call | tf_op jit(solution)/shard_map/pack/pallas_call | solution.py:239
  2.7 5.1 %collective-permute-start.2 = (bf16[12,2688]{1,0:T(8,128)(2,1)}, bf16[12,2688]{1,0:T(8,128)(2,1)S(1)}, u32[]{:S(2)}, u32[]{:S(2)}) collective-permute-start(bf16[12,2688]{1,0:T(8,128)(2,1)} %pack.1), channel_id=1, source_target_pairs={{0,12},{1,13},{2,14},{3,15},{4,8},{5,9},{6,10},{7,11},{8,4},{9,5},... | collective-permute-start | bytes 193544 | tf_op jit(solution)/shard_map/ppermute | solution.py:153
  7.8 0.0 collective-permute-start.1
  7.8 0.6 collective-permute-start
  8.5 3.0 %collective-permute-done.2 = bf16[12,2688]{1,0:T(8,128)(2,1)S(1)} collective-permute-done((bf16[12,2688]{1,0:T(8,128)(2,1)}, bf16[12,2688]{1,0:T(8,128)(2,1)S(1)}, u32[]{:S(2)}, u32[]{:S(2)}) %collective-permute-start.2) | collective-permute-done | bytes 64544 | tf_op jit(solution)/shard_map/ppermute | solution.py:153
  11.5 2.7 %collective-permute-done.1 = bf16[12,2688]{1,0:T(8,128)(2,1)S(1)} collective-permute-done((bf16[12,2688]{1,0:T(8,128)(2,1)}, bf16[12,2688]{1,0:T(8,128)(2,1)S(1)}, u32[]{:S(2)}, u32[]{:S(2)}) %collective-permute-start.1) | collective-permute-done | bytes 64544 | tf_op jit(solution)/shard_map/ppermute | solution.py:153
  14.2 1.0 %collective-permute-done = bf16[12,2688]{1,0:T(8,128)(2,1)S(1)} collective-permute-done((bf16[12,2688]{1,0:T(8,128)(2,1)}, bf16[12,2688]{1,0:T(8,128)(2,1)S(1)}, u32[]{:S(2)}, u32[]{:S(2)}) %collective-permute-start) | collective-permute-done | bytes 64544 | tf_op jit(solution)/shard_map/ppermute | solution.py:153
  15.2 1.0 %pad_maximum_fusion.refs_0_ = bf16[48,2688]{1,0:T(8,128)(2,1)S(1)} fusion(bf16[12,2688]{1,0:T(8,128)(2,1)S(1)} %collective-permute-done.2, bf16[12,2688]{1,0:T(8,128)(2,1)S(1)} %collective-permute-done.1, bf16[12,2688]{1,0:T(8,128)(2,1)S(1)} %collective-permute-done, bf16[12,2688]{1,0:T(8,128)(2,1)} %pack.1), kind=kLoop, calls=%fused_computation.4 | loop fusion | flops 1032192 | bytes 516096 | tf_op jit(solution)/shard_map/concatenate | solution.py:157
  16.2 2.5 %collective-permute-start.5 = (bf16[48,2688]{1,0:T(8,128)(2,1)S(1)}, bf16[48,2688]{1,0:T(8,128)(2,1)S(1)}, u32[]{:S(2)}, u32[]{:S(2)}) collective-permute-start(bf16[48,2688]{1,0:T(8,128)(2,1)S(1)} %pad_maximum_fusion.refs_0_), channel_id=1, source_target_pairs={{0,18},{1,19},{2,16},{3,17},{4,22},{5,23},{6,20},{7,21},{8,26},{9,... | collective-permute-start | bytes 774152 | tf_op jit(solution)/shard_map/ppermute | solution.py:153
  18.7 0.5 collective-permute-start.4
  19.2 0.5 collective-permute-start.3
  19.8 0.0 collective-permute-start.6
  19.8 6.1 %collective-permute-done.5.refs_3_ = bf16[48,2688]{1,0:T(8,128)(2,1)S(1)} collective-permute-done((bf16[48,2688]{1,0:T(8,128)(2,1)S(1)}, bf16[48,2688]{1,0:T(8,128)(2,1)S(1)}, u32[]{:S(2)}, u32[]{:S(2)}) %collective-permute-start.5) | collective-permute-done | bytes 258080 | tf_op jit(solution)/shard_map/ppermute | solution.py:153
  25.9 0.0 collective-permute-start.9
  25.9 2.7 %collective-permute-done.4.refs_2_ = bf16[48,2688]{1,0:T(8,128)(2,1)S(1)} collective-permute-done((bf16[48,2688]{1,0:T(8,128)(2,1)S(1)}, bf16[48,2688]{1,0:T(8,128)(2,1)S(1)}, u32[]{:S(2)}, u32[]{:S(2)}) %collective-permute-start.4) | collective-permute-done | bytes 258080 | tf_op jit(solution)/shard_map/ppermute | solution.py:153
  28.6 0.0 collective-permute-start.8
  28.6 0.2 collective-permute-done.3.refs_1_
  28.8 0.3 collective-permute-start.7
  29.1 4.0 %expert_terms.2 = (bf16[192,2560]{1,0:T(8,128)(2,1)S(1)}, bf16[192,384]{1,0:T(8,128)(2,1)S(1)}, bf16[384,2560]{1,0:T(8,128)(2,1)S(1)}, bf16[384,2560]{1,0:T(8,128)(2,1)S(1)}, bf16[384,2560]{1,0:T(8,128)(2,1)S(1)}) custom-call(bf16[48,2688]{1,0:T(8,128)(2,1)S(1)} %pad_maximum_fusion.refs_0_, bf16[48,2688]{1,0:T(8,128)(2,1)S(1)} %collective-permute-done.3.refs_1_, ...), custom_call_target="tpu_custom_call" | custom-call | flops 1132462080 | bytes 7864320 | tf_op jit(solution)/shard_map/expert_terms/pallas_call | solution.py:322
  33.2 0.0 collective-permute-done.6.refs_0_
  33.2 0.0 collective-permute-done.9.refs_3_
  33.2 0.0 collective-permute-done.8.refs_2_
  33.2 0.0 collective-permute-done.7.refs_1_
  33.2 2.0 %expert_terms.3 = (bf16[144,2560]{1,0:T(8,128)(2,1)S(1)}, bf16[48,2560]{1,0:T(8,128)(2,1)S(1)}, bf16[192,384]{1,0:T(8,128)(2,1)S(1)}) custom-call(bf16[48,2688]{1,0:T(8,128)(2,1)S(1)} %collective-permute-done.6.refs_0_, bf16[48,2688]{1,0:T(8,128)(2,1)S(1)} %collective-permute-done.7.refs_1_, bf16[48,2688]{1,0:T(8,128)(2,1)S(1)} %collective-permute-done.8.refs_2_, ...), custom_call_target="tpu_custom_call" | custom-call | flops 1132462080 | bytes 7864320 | tf_op jit(solution)/shard_map/expert_terms/pallas_call | solution.py:322
  35.2 0.3 collective-permute-start.11
  35.5 0.3 collective-permute-start.10
  35.8 1.0 %collective-permute-done.11 = bf16[48,2560]{1,0:T(8,128)(2,1)S(1)} collective-permute-done((bf16[48,2560]{1,0:T(8,128)(2,1)S(1)}, bf16[48,2560]{1,0:T(8,128)(2,1)S(1)}, u32[]{:S(2)}, u32[]{:S(2)}) %collective-permute-start.11) | collective-permute-done | bytes 245792 | tf_op jit(solution)/shard_map/ppermute | solution.py:153
  36.8 0.1 add_convert_fusion
  36.9 1.7 %collective-permute-start.12 = (bf16[48,1280]{1,0:T(8,128)(2,1)S(1)}, bf16[48,1280]{1,0:T(8,128)(2,1)S(1)}, u32[]{:S(2)}, u32[]{:S(2)}) collective-permute-start(bf16[48,1280]{1,0:T(8,128)(2,1)S(1)} %get-tuple-element.31), channel_id=1, source_target_pairs={{0,16},{1,17},{2,18},{3,19},{4,20},{5,21},{6,22},{7,23},{8,24},{9,... | collective-permute-start | bytes 368648 | tf_op jit(solution)/shard_map/ppermute | solution.py:153
  38.6 0.7 collective-permute-start.14
  39.3 0.0 collective-permute-done.10
  39.3 0.2 fusion.4
  39.5 2.9 %collective-permute-done.12 = bf16[48,1280]{1,0:T(8,128)(2,1)S(1)} collective-permute-done((bf16[48,1280]{1,0:T(8,128)(2,1)S(1)}, bf16[48,1280]{1,0:T(8,128)(2,1)S(1)}, u32[]{:S(2)}, u32[]{:S(2)}) %collective-permute-start.12) | collective-permute-done | bytes 122912 | tf_op jit(solution)/shard_map/ppermute | solution.py:153
  42.4 1.3 %collective-permute-done.14 = bf16[48,1280]{1,0:T(8,128)(2,1)S(1)} collective-permute-done((bf16[48,1280]{1,0:T(8,128)(2,1)S(1)}, bf16[48,1280]{1,0:T(8,128)(2,1)S(1)}, u32[]{:S(2)}, u32[]{:S(2)}) %collective-permute-start.14) | collective-permute-done | bytes 122912 | tf_op jit(solution)/shard_map/ppermute | solution.py:153
  43.7 0.1 fusion.3
  43.7 0.0 copy-start.3
  43.8 0.5 collective-permute-start.15
  44.3 0.0 copy-start
  44.3 0.0 copy-start.1
  44.3 1.6 %collective-permute-start.13 = (bf16[48,2560]{1,0:T(8,128)(2,1)S(1)}, bf16[48,2560]{1,0:T(8,128)(2,1)S(1)}, u32[]{:S(2)}, u32[]{:S(2)}) collective-permute-start(bf16[48,2560]{1,0:T(8,128)(2,1)S(1)} %pad_maximum_fusion.1), channel_id=1, source_target_pairs={{0,2},{1,3},{2,0},{3,1},{4,6},{5,7},{6,4},{7,5},{8,10},{9,11},{10,... | collective-permute-start | bytes 737288 | tf_op jit(solution)/shard_map/ppermute | solution.py:153
  45.9 4.7 %collective-permute-done.15 = bf16[48,2560]{1,0:T(8,128)(2,1)S(1)} collective-permute-done((bf16[48,2560]{1,0:T(8,128)(2,1)S(1)}, bf16[48,2560]{1,0:T(8,128)(2,1)S(1)}, u32[]{:S(2)}, u32[]{:S(2)}) %collective-permute-start.15) | collective-permute-done | bytes 245792 | tf_op jit(solution)/shard_map/ppermute | solution.py:153
  50.7 0.4 collective-permute-done.13
  51.1 0.1 fusion
  51.2 0.7 collective-permute-start.16
  52.0 4.2 %collective-permute-done.16 = bf16[24,2560]{1,0:T(8,128)(2,1)S(1)} collective-permute-done((bf16[24,2560]{1,0:T(8,128)(2,1)S(1)}, bf16[24,2560]{1,0:T(8,128)(2,1)S(1)}, u32[]{:S(2)}, u32[]{:S(2)}) %collective-permute-start.16) | collective-permute-done | bytes 122912 | tf_op jit(solution)/shard_map/ppermute | solution.py:153
  56.3 3.1 %collective-permute-start.17 = (bf16[24,2560]{1,0:T(8,128)(2,1)S(1)}, bf16[24,2560]{1,0:T(8,128)(2,1)S(1)}, u32[]{:S(2)}, u32[]{:S(2)}) collective-permute-start(bf16[24,2560]{1,0:T(8,128)(2,1)S(1)} %pad_maximum_fusion.5), channel_id=1, source_target_pairs={{0,8},{1,9},{2,10},{3,11},{4,12},{5,13},{6,14},{7,15},{8,0},{9,1},... | collective-permute-start | bytes 368648 | tf_op jit(solution)/shard_map/ppermute | solution.py:153
  59.4 4.2 %collective-permute-done.17 = bf16[24,2560]{1,0:T(8,128)(2,1)S(1)} collective-permute-done((bf16[24,2560]{1,0:T(8,128)(2,1)S(1)}, bf16[24,2560]{1,0:T(8,128)(2,1)S(1)}, u32[]{:S(2)}, u32[]{:S(2)}) %collective-permute-start.17) | collective-permute-done | bytes 122912 | tf_op jit(solution)/shard_map/ppermute | solution.py:153
  63.6 0.1 tanh_convert_fusion
  63.7 0.1 collective-permute-start.18
  63.8 4.9 %collective-permute-done.18 = bf16[24,2560]{1,0:T(8,128)(2,1)S(1)} collective-permute-done((bf16[24,2560]{1,0:T(8,128)(2,1)S(1)}, bf16[24,2560]{1,0:T(8,128)(2,1)S(1)}, u32[]{:S(2)}, u32[]{:S(2)}) %collective-permute-start.18) | collective-permute-done | bytes 122912 | tf_op jit(solution)/shard_map/ppermute | solution.py:153
  68.7 1.8 %collective-permute-start.21 = (bf16[48,2560]{1,0:T(8,128)(2,1)S(1)}, bf16[48,2560]{1,0:T(8,128)(2,1)S(1)}, u32[]{:S(2)}, u32[]{:S(2)}) collective-permute-start(bf16[48,2560]{1,0:T(8,128)(2,1)S(1)} %pad_maximum_fusion.3.refs_0_), channel_id=1, source_target_pairs={{0,18},{1,19},{2,16},{3,17},{4,22},{5,23},{6,20},{7,21},{8,26},{9,... | collective-permute-start | bytes 737288 | tf_op jit(solution)/shard_map/ppermute | solution.py:153
  70.5 1.2 %collective-permute-start.20 = (bf16[48,2560]{1,0:T(8,128)(2,1)S(1)}, bf16[48,2560]{1,0:T(8,128)(2,1)S(1)}, u32[]{:S(2)}, u32[]{:S(2)}) collective-permute-start(bf16[48,2560]{1,0:T(8,128)(2,1)S(1)} %pad_maximum_fusion.3.refs_0_), channel_id=1, source_target_pairs={{0,16},{1,17},{2,18},{3,19},{4,20},{5,21},{6,22},{7,23},{8,24},{9,... | collective-permute-start | bytes 737288 | tf_op jit(solution)/shard_map/ppermute | solution.py:153
  71.7 0.5 collective-permute-start.19
  72.2 0.0 collective-permute-start.22
  72.2 3.7 %collective-permute-done.21.refs_3_ = bf16[48,2560]{1,0:T(8,128)(2,1)S(1)} collective-permute-done((bf16[48,2560]{1,0:T(8,128)(2,1)S(1)}, bf16[48,2560]{1,0:T(8,128)(2,1)S(1)}, u32[]{:S(2)}, u32[]{:S(2)}) %collective-permute-start.21) | collective-permute-done | bytes 245792 | tf_op jit(solution)/shard_map/ppermute | solution.py:153
  75.9 0.0 collective-permute-start.25
  75.9 2.5 %collective-permute-done.20.refs_2_ = bf16[48,2560]{1,0:T(8,128)(2,1)S(1)} collective-permute-done((bf16[48,2560]{1,0:T(8,128)(2,1)S(1)}, bf16[48,2560]{1,0:T(8,128)(2,1)S(1)}, u32[]{:S(2)}, u32[]{:S(2)}) %collective-permute-start.20) | collective-permute-done | bytes 245792 | tf_op jit(solution)/shard_map/ppermute | solution.py:153
  78.4 0.0 collective-permute-start.24
  78.5 0.1 collective-permute-done.19.refs_1_
  78.6 0.4 collective-permute-start.23
  79.0 0.2 turn.1.refs_8_
  79.2 0.8 collective-permute-done.24.refs_6_
  80.0 0.4 collective-permute-done.23.refs_5_
  80.3 4.9 %update.1 = (bf16[384,2560]{1,0:T(8,128)(2,1)}, bf16[384,2560]{1,0:T(8,128)(2,1)}, bf16[384,2560]{1,0:T(8,128)(2,1)}) custom-call(bf16[48,2560]{1,0:T(8,128)(2,1)S(1)} %pad_maximum_fusion.3.refs_0_, bf16[48,2560]{1,0:T(8,128)(2,1)S(1)} %collective-permute-done.19.refs_1_, bf16[48,2560]{1,0:T(8,128)(2,1)S(1)} %collective-permute-done.20.refs_2_, ...), custom_call_target="tpu_custom_call" | custom-call | flops 754974720 | bytes 13762560 | tf_op jit(solution)/shard_map/update/pallas_call | solution.py:390
  (16 shorter events, 0.2 us)
Async XLA Ops:
  2.7 8.8 %collective-permute-start.2 = (bf16[12,2688]{1,0:T(8,128)(2,1)}, bf16[12,2688]{1,0:T(8,128)(2,1)S(1)}, u32[]{:S(2)}, u32[]{:S(2)}) collective-permute-start(bf16[12,2688]{1,0:T(8,128)(2,1)} %pack.1), channel_id=1, source_target_pairs={{0,12},{1,13},{2,14},{3,15},{4,8},{5,9},{6,10},{7,11},{8,4},{9,5},... | collective-permute-start | bytes 193544 | tf_op jit(solution)/shard_map/ppermute | solution.py:153
  7.8 6.4 %collective-permute-start.1 = (bf16[12,2688]{1,0:T(8,128)(2,1)}, bf16[12,2688]{1,0:T(8,128)(2,1)S(1)}, u32[]{:S(2)}, u32[]{:S(2)}) collective-permute-start(bf16[12,2688]{1,0:T(8,128)(2,1)} %pack.1), channel_id=1, source_target_pairs={{0,4},{1,5},{2,6},{3,7},{4,0},{5,1},{6,2},{7,3},{8,12},{9,13},{10,... | collective-permute-start | bytes 193544 | tf_op jit(solution)/shard_map/ppermute | solution.py:153
  7.8 7.4 %collective-permute-start = (bf16[12,2688]{1,0:T(8,128)(2,1)}, bf16[12,2688]{1,0:T(8,128)(2,1)S(1)}, u32[]{:S(2)}, u32[]{:S(2)}) collective-permute-start(bf16[12,2688]{1,0:T(8,128)(2,1)} %pack.1), channel_id=1, source_target_pairs={{0,8},{1,9},{2,10},{3,11},{4,12},{5,13},{6,14},{7,15},{8,0},{9,1},... | collective-permute-start | bytes 193544 | tf_op jit(solution)/shard_map/ppermute | solution.py:153
  16.2 9.7 %collective-permute-start.5 = (bf16[48,2688]{1,0:T(8,128)(2,1)S(1)}, bf16[48,2688]{1,0:T(8,128)(2,1)S(1)}, u32[]{:S(2)}, u32[]{:S(2)}) collective-permute-start(bf16[48,2688]{1,0:T(8,128)(2,1)S(1)} %pad_maximum_fusion.refs_0_), channel_id=1, source_target_pairs={{0,18},{1,19},{2,16},{3,17},{4,22},{5,23},{6,20},{7,21},{8,26},{9,... | collective-permute-start | bytes 774152 | tf_op jit(solution)/shard_map/ppermute | solution.py:153
  18.7 9.9 %collective-permute-start.4 = (bf16[48,2688]{1,0:T(8,128)(2,1)S(1)}, bf16[48,2688]{1,0:T(8,128)(2,1)S(1)}, u32[]{:S(2)}, u32[]{:S(2)}) collective-permute-start(bf16[48,2688]{1,0:T(8,128)(2,1)S(1)} %pad_maximum_fusion.refs_0_), channel_id=1, source_target_pairs={{0,16},{1,17},{2,18},{3,19},{4,20},{5,21},{6,22},{7,23},{8,24},{9,... | collective-permute-start | bytes 774152 | tf_op jit(solution)/shard_map/ppermute | solution.py:153
  19.2 9.6 %collective-permute-start.3 = (bf16[48,2688]{1,0:T(8,128)(2,1)S(1)}, bf16[48,2688]{1,0:T(8,128)(2,1)S(1)}, u32[]{:S(2)}, u32[]{:S(2)}) collective-permute-start(bf16[48,2688]{1,0:T(8,128)(2,1)S(1)} %pad_maximum_fusion.refs_0_), channel_id=1, source_target_pairs={{0,2},{1,3},{2,0},{3,1},{4,6},{5,7},{6,4},{7,5},{8,10},{9,11},{10,... | collective-permute-start | bytes 774152 | tf_op jit(solution)/shard_map/ppermute | solution.py:153
  19.8 13.4 %collective-permute-start.6 = (bf16[48,2688]{1,0:T(8,128)(2,1)S(1)}, bf16[48,2688]{1,0:T(8,128)(2,1)S(1)}, u32[]{:S(2)}, u32[]{:S(2)}) collective-permute-start(bf16[48,2688]{1,0:T(8,128)(2,1)S(1)} %pad_maximum_fusion.refs_0_), channel_id=1, source_target_pairs={{0,1},{1,0},{2,3},{3,2},{4,5},{5,4},{6,7},{7,6},{8,9},{9,8},{10,11... | collective-permute-start | bytes 774152 | tf_op jit(solution)/shard_map/ppermute | solution.py:153
  25.9 7.3 %collective-permute-start.9 = (bf16[48,2688]{1,0:T(8,128)(2,1)S(1)}, bf16[48,2688]{1,0:T(8,128)(2,1)S(1)}, u32[]{:S(2)}, u32[]{:S(2)}) collective-permute-start(bf16[48,2688]{1,0:T(8,128)(2,1)S(1)} %collective-permute-done.5.refs_3_), channel_id=1, source_target_pairs={{0,1},{1,0},{2,3},{3,2},{4,5},{5,4},{6,7},{7,6},{8,9},{9,8},{10,11... | collective-permute-start | bytes 774152 | tf_op jit(solution)/shard_map/ppermute | solution.py:153
  28.6 4.6 %collective-permute-start.8 = (bf16[48,2688]{1,0:T(8,128)(2,1)S(1)}, bf16[48,2688]{1,0:T(8,128)(2,1)S(1)}, u32[]{:S(2)}, u32[]{:S(2)}) collective-permute-start(bf16[48,2688]{1,0:T(8,128)(2,1)S(1)} %collective-permute-done.4.refs_2_), channel_id=1, source_target_pairs={{0,1},{1,0},{2,3},{3,2},{4,5},{5,4},{6,7},{7,6},{8,9},{9,8},{10,11... | collective-permute-start | bytes 774152 | tf_op jit(solution)/shard_map/ppermute | solution.py:153
  28.8 4.4 %collective-permute-start.7 = (bf16[48,2688]{1,0:T(8,128)(2,1)S(1)}, bf16[48,2688]{1,0:T(8,128)(2,1)S(1)}, u32[]{:S(2)}, u32[]{:S(2)}) collective-permute-start(bf16[48,2688]{1,0:T(8,128)(2,1)S(1)} %collective-permute-done.3.refs_1_), channel_id=1, source_target_pairs={{0,1},{1,0},{2,3},{3,2},{4,5},{5,4},{6,7},{7,6},{8,9},{9,8},{10,11... | collective-permute-start | bytes 774152 | tf_op jit(solution)/shard_map/ppermute | solution.py:153
  35.2 1.6 %collective-permute-start.11 = (bf16[48,2560]{1,0:T(8,128)(2,1)S(1)}, bf16[48,2560]{1,0:T(8,128)(2,1)S(1)}, u32[]{:S(2)}, u32[]{:S(2)}) collective-permute-start(bf16[48,2560]{1,0:T(8,128)(2,1)S(1)} %get-tuple-element.19), channel_id=1, source_target_pairs={{0,1},{1,0},{2,3},{3,2},{4,5},{5,4},{6,7},{7,6},{8,9},{9,8},{10,11... | collective-permute-start | bytes 737288 | tf_op jit(solution)/shard_map/ppermute | solution.py:153
  35.5 3.8 %collective-permute-start.10 = (bf16[144,2560]{1,0:T(8,128)(2,1)S(1)}, bf16[144,2560]{1,0:T(8,128)(2,1)S(1)}, u32[]{:S(2)}, u32[]{:S(2)}) collective-permute-start(bf16[144,2560]{1,0:T(8,128)(2,1)S(1)} %get-tuple-element.18), channel_id=1, source_target_pairs={{0,1},{1,0},{2,3},{3,2},{4,5},{5,4},{6,7},{7,6},{8,9},{9,8},{10,11... | collective-permute-start | bytes 2211848 | tf_op jit(solution)/shard_map/ppermute | solution.py:153
  36.9 5.5 %collective-permute-start.12 = (bf16[48,1280]{1,0:T(8,128)(2,1)S(1)}, bf16[48,1280]{1,0:T(8,128)(2,1)S(1)}, u32[]{:S(2)}, u32[]{:S(2)}) collective-permute-start(bf16[48,1280]{1,0:T(8,128)(2,1)S(1)} %get-tuple-element.31), channel_id=1, source_target_pairs={{0,16},{1,17},{2,18},{3,19},{4,20},{5,21},{6,22},{7,23},{8,24},{9,... | collective-permute-start | bytes 368648 | tf_op jit(solution)/shard_map/ppermute | solution.py:153
  38.6 5.1 %collective-permute-start.14 = (bf16[48,1280]{1,0:T(8,128)(2,1)S(1)}, bf16[48,1280]{1,0:T(8,128)(2,1)S(1)}, u32[]{:S(2)}, u32[]{:S(2)}) collective-permute-start(bf16[48,1280]{1,0:T(8,128)(2,1)S(1)} %get-tuple-element.32), channel_id=1, source_target_pairs={{0,2},{1,3},{2,0},{3,1},{4,6},{5,7},{6,4},{7,5},{8,10},{9,11},{10,... | collective-permute-start | bytes 368648 | tf_op jit(solution)/shard_map/ppermute | solution.py:153
  43.7 36.6 %copy-start.2 = (bf16[1,384,2560]{2,1,0:T(8,128)(2,1)S(1)}, bf16[1,384,2560]{2,1,0:T(8,128)(2,1)}, u32[]{:S(2)}) copy-start(bf16[1,384,2560]{2,1,0:T(8,128)(2,1)} %param.15) | copy-start | bytes 5898244
  43.7 19.9 %copy-start.3 = (bf16[12,2688]{1,0:T(8,128)(2,1)S(1)}, bf16[12,2688]{1,0:T(8,128)(2,1)}, u32[]{:S(2)}) copy-start(bf16[12,2688]{1,0:T(8,128)(2,1)} %pack.1) | copy-start | bytes 193540
  43.8 6.9 %collective-permute-start.15 = (bf16[48,2560]{1,0:T(8,128)(2,1)S(1)}, bf16[48,2560]{1,0:T(8,128)(2,1)S(1)}, u32[]{:S(2)}, u32[]{:S(2)}) collective-permute-start(bf16[48,2560]{1,0:T(8,128)(2,1)S(1)} %pad_maximum_fusion.2), channel_id=1, source_target_pairs={{0,16},{1,17},{2,18},{3,19},{4,20},{5,21},{6,22},{7,23},{8,24},{9,... | collective-permute-start | bytes 737288 | tf_op jit(solution)/shard_map/ppermute | solution.py:153
  44.3 36.0 %copy-start = (bf16[1,384,2560]{2,1,0:T(8,128)(2,1)S(1)}, bf16[1,384,2560]{2,1,0:T(8,128)(2,1)}, u32[]{:S(2)}) copy-start(bf16[1,384,2560]{2,1,0:T(8,128)(2,1)} %param.13) | copy-start | bytes 5898244
  44.3 36.0 %copy-start.1 = (bf16[1,384,2560]{2,1,0:T(8,128)(2,1)S(1)}, bf16[1,384,2560]{2,1,0:T(8,128)(2,1)}, u32[]{:S(2)}) copy-start(bf16[1,384,2560]{2,1,0:T(8,128)(2,1)} %param.14) | copy-start | bytes 5898244
  44.3 6.8 %collective-permute-start.13 = (bf16[48,2560]{1,0:T(8,128)(2,1)S(1)}, bf16[48,2560]{1,0:T(8,128)(2,1)S(1)}, u32[]{:S(2)}, u32[]{:S(2)}) collective-permute-start(bf16[48,2560]{1,0:T(8,128)(2,1)S(1)} %pad_maximum_fusion.1), channel_id=1, source_target_pairs={{0,2},{1,3},{2,0},{3,1},{4,6},{5,7},{6,4},{7,5},{8,10},{9,11},{10,... | collective-permute-start | bytes 737288 | tf_op jit(solution)/shard_map/ppermute | solution.py:153
  51.2 4.9 %collective-permute-start.16 = (bf16[24,2560]{1,0:T(8,128)(2,1)S(1)}, bf16[24,2560]{1,0:T(8,128)(2,1)S(1)}, u32[]{:S(2)}, u32[]{:S(2)}) collective-permute-start(bf16[24,2560]{1,0:T(8,128)(2,1)S(1)} %split.35), channel_id=1, source_target_pairs={{0,4},{1,5},{2,6},{3,7},{4,0},{5,1},{6,2},{7,3},{8,12},{9,13},{10,... | collective-permute-start | bytes 368648 | tf_op jit(solution)/shard_map/ppermute | solution.py:153
  56.3 7.3 %collective-permute-start.17 = (bf16[24,2560]{1,0:T(8,128)(2,1)S(1)}, bf16[24,2560]{1,0:T(8,128)(2,1)S(1)}, u32[]{:S(2)}, u32[]{:S(2)}) collective-permute-start(bf16[24,2560]{1,0:T(8,128)(2,1)S(1)} %pad_maximum_fusion.5), channel_id=1, source_target_pairs={{0,8},{1,9},{2,10},{3,11},{4,12},{5,13},{6,14},{7,15},{8,0},{9,1},... | collective-permute-start | bytes 368648 | tf_op jit(solution)/shard_map/ppermute | solution.py:153
  63.7 4.9 %collective-permute-start.18 = (bf16[24,2560]{1,0:T(8,128)(2,1)S(1)}, bf16[24,2560]{1,0:T(8,128)(2,1)S(1)}, u32[]{:S(2)}, u32[]{:S(2)}) collective-permute-start(bf16[24,2560]{1,0:T(8,128)(2,1)S(1)} %tanh_convert_fusion), channel_id=1, source_target_pairs={{0,4},{1,5},{2,6},{3,7},{4,0},{5,1},{6,2},{7,3},{8,12},{9,13},{10,... | collective-permute-start | bytes 368648 | tf_op jit(solution)/shard_map/ppermute | solution.py:153
  68.7 7.3 %collective-permute-start.21 = (bf16[48,2560]{1,0:T(8,128)(2,1)S(1)}, bf16[48,2560]{1,0:T(8,128)(2,1)S(1)}, u32[]{:S(2)}, u32[]{:S(2)}) collective-permute-start(bf16[48,2560]{1,0:T(8,128)(2,1)S(1)} %pad_maximum_fusion.3.refs_0_), channel_id=1, source_target_pairs={{0,18},{1,19},{2,16},{3,17},{4,22},{5,23},{6,20},{7,21},{8,26},{9,... | collective-permute-start | bytes 737288 | tf_op jit(solution)/shard_map/ppermute | solution.py:153
  70.5 8.0 %collective-permute-start.20 = (bf16[48,2560]{1,0:T(8,128)(2,1)S(1)}, bf16[48,2560]{1,0:T(8,128)(2,1)S(1)}, u32[]{:S(2)}, u32[]{:S(2)}) collective-permute-start(bf16[48,2560]{1,0:T(8,128)(2,1)S(1)} %pad_maximum_fusion.3.refs_0_), channel_id=1, source_target_pairs={{0,16},{1,17},{2,18},{3,19},{4,20},{5,21},{6,22},{7,23},{8,24},{9,... | collective-permute-start | bytes 737288 | tf_op jit(solution)/shard_map/ppermute | solution.py:153
  71.7 6.9 %collective-permute-start.19 = (bf16[48,2560]{1,0:T(8,128)(2,1)S(1)}, bf16[48,2560]{1,0:T(8,128)(2,1)S(1)}, u32[]{:S(2)}, u32[]{:S(2)}) collective-permute-start(bf16[48,2560]{1,0:T(8,128)(2,1)S(1)} %pad_maximum_fusion.3.refs_0_), channel_id=1, source_target_pairs={{0,2},{1,3},{2,0},{3,1},{4,6},{5,7},{6,4},{7,5},{8,10},{9,11},{10,... | collective-permute-start | bytes 737288 | tf_op jit(solution)/shard_map/ppermute | solution.py:153
  72.2 6.9 %collective-permute-start.22 = (bf16[48,2560]{1,0:T(8,128)(2,1)S(1)}, bf16[48,2560]{1,0:T(8,128)(2,1)S(1)}, u32[]{:S(2)}, u32[]{:S(2)}) collective-permute-start(bf16[48,2560]{1,0:T(8,128)(2,1)S(1)} %pad_maximum_fusion.3.refs_0_), channel_id=1, source_target_pairs={{0,1},{1,0},{2,3},{3,2},{4,5},{5,4},{6,7},{7,6},{8,9},{9,8},{10,11... | collective-permute-start | bytes 737288 | tf_op jit(solution)/shard_map/ppermute | solution.py:153
  75.9 3.2 %collective-permute-start.25 = (bf16[48,2560]{1,0:T(8,128)(2,1)S(1)}, bf16[48,2560]{1,0:T(8,128)(2,1)S(1)}, u32[]{:S(2)}, u32[]{:S(2)}) collective-permute-start(bf16[48,2560]{1,0:T(8,128)(2,1)S(1)} %collective-permute-done.21.refs_3_), channel_id=1, source_target_pairs={{0,1},{1,0},{2,3},{3,2},{4,5},{5,4},{6,7},{7,6},{8,9},{9,8},{10,11... | collective-permute-start | bytes 737288 | tf_op jit(solution)/shard_map/ppermute | solution.py:153
  78.4 1.5 %collective-permute-start.24 = (bf16[48,2560]{1,0:T(8,128)(2,1)S(1)}, bf16[48,2560]{1,0:T(8,128)(2,1)S(1)}, u32[]{:S(2)}, u32[]{:S(2)}) collective-permute-start(bf16[48,2560]{1,0:T(8,128)(2,1)S(1)} %collective-permute-done.20.refs_2_), channel_id=1, source_target_pairs={{0,1},{1,0},{2,3},{3,2},{4,5},{5,4},{6,7},{7,6},{8,9},{9,8},{10,11... | collective-permute-start | bytes 737288 | tf_op jit(solution)/shard_map/ppermute | solution.py:153
  78.6 1.8 %collective-permute-start.23 = (bf16[48,2560]{1,0:T(8,128)(2,1)S(1)}, bf16[48,2560]{1,0:T(8,128)(2,1)S(1)}, u32[]{:S(2)}, u32[]{:S(2)}) collective-permute-start(bf16[48,2560]{1,0:T(8,128)(2,1)S(1)} %collective-permute-done.19.refs_1_), channel_id=1, source_target_pairs={{0,1},{1,0},{2,3},{3,2},{4,5},{5,4},{6,7},{7,6},{8,9},{9,8},{10,11... | collective-permute-start | bytes 737288 | tf_op jit(solution)/shard_map/ppermute | solution.py:153

commit v7 on v6

--- a/solution.py
+++ b/solution.py
@@ -139,7 +139,7 @@
 PLANE = (2, 16, 18)
 LINE = (8, 4, 12)
 BLOCK = 512
-UPDATE_BLOCK = 256
+UPDATE_BLOCK = 512
 PARTS = 4
 LIMIT = 46
 PACK_PARTS = 4
@@ -370,7 +370,7 @@
         first += (1.0 - first_decay) * gradient
         second = second_decay * second_ref[:, span].astype(jnp.float32)
         second += (1.0 - second_decay) * gradient * gradient
-        step = rate * first / (jnp.sqrt(second) + adam_epsilon * root)
+        step = rate * first / (second * lax.rsqrt(second) + adam_epsilon * root)
         down = keep * down_ref[:, span].astype(jnp.float32) - step
         for k, value in enumerate((down, first, second)):
             held[k][:, span] = value.astype(jnp.bfloat16)

time: 85.4 us -> 84.5 us (0.989)
  Pallas kernels: 13.2 us -> 12.3 us
    pallas_call x1, Pallas kernels: 4.93 us -> 4 us  [update(): pl.pallas_call(update_kernel, out_shape=[jax.ShapeDtypeStruct((units, wid...]
where the time goes in v7:
time: 84.5 us; the launch traced here: 84.3 us
  waiting for transfers between devices  46.9 us (56%)
  starting transfers between devices  22.6 us (27%)
  Pallas kernels  12.3 us (15%)
  other arithmetic  1.58 us (2%)
    ppermute x26, waiting for transfers between devices, swap(): return lax.ppermute(block, AXES, [(i, i ^ mask) for i in range(count)])  46.9 us
    ppermute x26, starting transfers between devices, swap(): return lax.ppermute(block, AXES, [(i, i ^ mask) for i in range(count)])  22.6 us
    pallas_call x2, Pallas kernels, expert_terms(): pl.pallas_call(functools.partial(expert_kernel, held), out_shape=out_shap...  6.03 us
    pallas_call x1, Pallas kernels, update(): pl.pallas_call(update_kernel, out_shape=[jax.ShapeDtypeStruct((units, wid...  4 us
    pallas_call x1, Pallas kernels, pack(): pl.pallas_call(functools.partial(pack_kernel, experts), out_shape=jax.Sha...  2.07 us
  transfers between devices with their start and end apart: 26, of which 19 were waited for; matrix products, arithmetic and copies ran while one was open for 0% of the time, Pallas kernels for 5%

profile of v7, /device:TPU:0, one launch (start us, length us, event | category | flops | bytes accessed | tf_op | source)
XLA Modules:
  0.0 84.3 jit_solution(12489909314200360002)
XLA Ops:
  0.6 2.1 %pack.1 = bf16[12,2688]{1,0:T(8,128)(2,1)} custom-call(bf16[128,2560]{1,0:T(8,128)(2,1)} %tokens_ref.1, s32[6,128]{1,0:T(8,128)} %bitcast.16, bf16[6,128]{1,0:T(8,128)(2,1)} %bitcast.17), custom_call_target="tpu_custom_call" | custom-call | tf_op jit(solution)/shard_map/pack/pallas_call | solution.py:239
  2.7 5.1 %collective-permute-start.2 = (bf16[12,2688]{1,0:T(8,128)(2,1)}, bf16[12,2688]{1,0:T(8,128)(2,1)S(1)}, u32[]{:S(2)}, u32[]{:S(2)}) collective-permute-start(bf16[12,2688]{1,0:T(8,128)(2,1)} %pack.1), channel_id=1, source_target_pairs={{0,12},{1,13},{2,14},{3,15},{4,8},{5,9},{6,10},{7,11},{8,4},{9,5},... | collective-permute-start | bytes 193544 | tf_op jit(solution)/shard_map/ppermute | solution.py:153
  7.8 0.0 collective-permute-start.1
  7.8 0.6 collective-permute-start
  8.5 3.0 %collective-permute-done.2 = bf16[12,2688]{1,0:T(8,128)(2,1)S(1)} collective-permute-done((bf16[12,2688]{1,0:T(8,128)(2,1)}, bf16[12,2688]{1,0:T(8,128)(2,1)S(1)}, u32[]{:S(2)}, u32[]{:S(2)}) %collective-permute-start.2) | collective-permute-done | bytes 64544 | tf_op jit(solution)/shard_map/ppermute | solution.py:153
  11.5 2.7 %collective-permute-done.1 = bf16[12,2688]{1,0:T(8,128)(2,1)S(1)} collective-permute-done((bf16[12,2688]{1,0:T(8,128)(2,1)}, bf16[12,2688]{1,0:T(8,128)(2,1)S(1)}, u32[]{:S(2)}, u32[]{:S(2)}) %collective-permute-start.1) | collective-permute-done | bytes 64544 | tf_op jit(solution)/shard_map/ppermute | solution.py:153
  14.2 1.0 %collective-permute-done = bf16[12,2688]{1,0:T(8,128)(2,1)S(1)} collective-permute-done((bf16[12,2688]{1,0:T(8,128)(2,1)}, bf16[12,2688]{1,0:T(8,128)(2,1)S(1)}, u32[]{:S(2)}, u32[]{:S(2)}) %collective-permute-start) | collective-permute-done | bytes 64544 | tf_op jit(solution)/shard_map/ppermute | solution.py:153
  15.2 1.0 %pad_maximum_fusion.refs_0_ = bf16[48,2688]{1,0:T(8,128)(2,1)S(1)} fusion(bf16[12,2688]{1,0:T(8,128)(2,1)S(1)} %collective-permute-done.2, bf16[12,2688]{1,0:T(8,128)(2,1)S(1)} %collective-permute-done.1, bf16[12,2688]{1,0:T(8,128)(2,1)S(1)} %collective-permute-done, bf16[12,2688]{1,0:T(8,128)(2,1)} %pack.1), kind=kLoop, calls=%fused_computation.4 | loop fusion | flops 1032192 | bytes 516096 | tf_op jit(solution)/shard_map/concatenate | solution.py:157
  16.2 2.5 %collective-permute-start.5 = (bf16[48,2688]{1,0:T(8,128)(2,1)S(1)}, bf16[48,2688]{1,0:T(8,128)(2,1)S(1)}, u32[]{:S(2)}, u32[]{:S(2)}) collective-permute-start(bf16[48,2688]{1,0:T(8,128)(2,1)S(1)} %pad_maximum_fusion.refs_0_), channel_id=1, source_target_pairs={{0,18},{1,19},{2,16},{3,17},{4,22},{5,23},{6,20},{7,21},{8,26},{9,... | collective-permute-start | bytes 774152 | tf_op jit(solution)/shard_map/ppermute | solution.py:153
  18.7 0.5 collective-permute-start.4
  19.2 0.5 collective-permute-start.3
  19.8 0.0 collective-permute-start.6
  19.8 6.1 %collective-permute-done.5.refs_3_ = bf16[48,2688]{1,0:T(8,128)(2,1)S(1)} collective-permute-done((bf16[48,2688]{1,0:T(8,128)(2,1)S(1)}, bf16[48,2688]{1,0:T(8,128)(2,1)S(1)}, u32[]{:S(2)}, u32[]{:S(2)}) %collective-permute-start.5) | collective-permute-done | bytes 258080 | tf_op jit(solution)/shard_map/ppermute | solution.py:153
  25.9 0.0 collective-permute-start.9
  25.9 2.7 %collective-permute-done.4.refs_2_ = bf16[48,2688]{1,0:T(8,128)(2,1)S(1)} collective-permute-done((bf16[48,2688]{1,0:T(8,128)(2,1)S(1)}, bf16[48,2688]{1,0:T(8,128)(2,1)S(1)}, u32[]{:S(2)}, u32[]{:S(2)}) %collective-permute-start.4) | collective-permute-done | bytes 258080 | tf_op jit(solution)/shard_map/ppermute | solution.py:153
  28.6 0.0 collective-permute-start.8
  28.6 0.2 collective-permute-done.3.refs_1_
  28.8 0.3 collective-permute-start.7
  29.1 4.0 %expert_terms.2 = (bf16[192,2560]{1,0:T(8,128)(2,1)S(1)}, bf16[192,384]{1,0:T(8,128)(2,1)S(1)}, bf16[384,2560]{1,0:T(8,128)(2,1)S(1)}, bf16[384,2560]{1,0:T(8,128)(2,1)S(1)}, bf16[384,2560]{1,0:T(8,128)(2,1)S(1)}) custom-call(bf16[48,2688]{1,0:T(8,128)(2,1)S(1)} %pad_maximum_fusion.refs_0_, bf16[48,2688]{1,0:T(8,128)(2,1)S(1)} %collective-permute-done.3.refs_1_, ...), custom_call_target="tpu_custom_call" | custom-call | flops 1132462080 | bytes 7864320 | tf_op jit(solution)/shard_map/expert_terms/pallas_call | solution.py:322
  33.2 0.0 collective-permute-done.6.refs_0_
  33.2 0.0 collective-permute-done.9.refs_3_
  33.2 0.0 collective-permute-done.8.refs_2_
  33.2 0.0 collective-permute-done.7.refs_1_
  33.2 2.0 %expert_terms.3 = (bf16[144,2560]{1,0:T(8,128)(2,1)S(1)}, bf16[48,2560]{1,0:T(8,128)(2,1)S(1)}, bf16[192,384]{1,0:T(8,128)(2,1)S(1)}) custom-call(bf16[48,2688]{1,0:T(8,128)(2,1)S(1)} %collective-permute-done.6.refs_0_, bf16[48,2688]{1,0:T(8,128)(2,1)S(1)} %collective-permute-done.7.refs_1_, bf16[48,2688]{1,0:T(8,128)(2,1)S(1)} %collective-permute-done.8.refs_2_, ...), custom_call_target="tpu_custom_call" | custom-call | flops 1132462080 | bytes 7864320 | tf_op jit(solution)/shard_map/expert_terms/pallas_call | solution.py:322
  35.2 0.3 collective-permute-start.11
  35.5 0.3 collective-permute-start.10
  35.8 1.0 %collective-permute-done.11 = bf16[48,2560]{1,0:T(8,128)(2,1)S(1)} collective-permute-done((bf16[48,2560]{1,0:T(8,128)(2,1)S(1)}, bf16[48,2560]{1,0:T(8,128)(2,1)S(1)}, u32[]{:S(2)}, u32[]{:S(2)}) %collective-permute-start.11) | collective-permute-done | bytes 245792 | tf_op jit(solution)/shard_map/ppermute | solution.py:153
  36.8 0.1 add_convert_fusion
  36.9 1.7 %collective-permute-start.12 = (bf16[48,1280]{1,0:T(8,128)(2,1)S(1)}, bf16[48,1280]{1,0:T(8,128)(2,1)S(1)}, u32[]{:S(2)}, u32[]{:S(2)}) collective-permute-start(bf16[48,1280]{1,0:T(8,128)(2,1)S(1)} %get-tuple-element.31), channel_id=1, source_target_pairs={{0,16},{1,17},{2,18},{3,19},{4,20},{5,21},{6,22},{7,23},{8,24},{9,... | collective-permute-start | bytes 368648 | tf_op jit(solution)/shard_map/ppermute | solution.py:153
  38.6 0.7 collective-permute-start.14
  39.3 0.2 fusion.4
  39.5 2.9 %collective-permute-done.12 = bf16[48,1280]{1,0:T(8,128)(2,1)S(1)} collective-permute-done((bf16[48,1280]{1,0:T(8,128)(2,1)S(1)}, bf16[48,1280]{1,0:T(8,128)(2,1)S(1)}, u32[]{:S(2)}, u32[]{:S(2)}) %collective-permute-start.12) | collective-permute-done | bytes 122912 | tf_op jit(solution)/shard_map/ppermute | solution.py:153
  42.4 1.3 %collective-permute-done.14 = bf16[48,1280]{1,0:T(8,128)(2,1)S(1)} collective-permute-done((bf16[48,1280]{1,0:T(8,128)(2,1)S(1)}, bf16[48,1280]{1,0:T(8,128)(2,1)S(1)}, u32[]{:S(2)}, u32[]{:S(2)}) %collective-permute-start.14) | collective-permute-done | bytes 122912 | tf_op jit(solution)/shard_map/ppermute | solution.py:153
  43.7 0.1 fusion.3
  43.7 0.0 copy-start.3
  43.8 0.5 collective-permute-start.15
  44.3 0.0 copy-start
  44.3 0.0 copy-start.1
  44.3 1.6 %collective-permute-start.13 = (bf16[48,2560]{1,0:T(8,128)(2,1)S(1)}, bf16[48,2560]{1,0:T(8,128)(2,1)S(1)}, u32[]{:S(2)}, u32[]{:S(2)}) collective-permute-start(bf16[48,2560]{1,0:T(8,128)(2,1)S(1)} %pad_maximum_fusion.1), channel_id=1, source_target_pairs={{0,2},{1,3},{2,0},{3,1},{4,6},{5,7},{6,4},{7,5},{8,10},{9,11},{10,... | collective-permute-start | bytes 737288 | tf_op jit(solution)/shard_map/ppermute | solution.py:153
  45.9 4.7 %collective-permute-done.15 = bf16[48,2560]{1,0:T(8,128)(2,1)S(1)} collective-permute-done((bf16[48,2560]{1,0:T(8,128)(2,1)S(1)}, bf16[48,2560]{1,0:T(8,128)(2,1)S(1)}, u32[]{:S(2)}, u32[]{:S(2)}) %collective-permute-start.15) | collective-permute-done | bytes 245792 | tf_op jit(solution)/shard_map/ppermute | solution.py:153
  50.7 0.4 collective-permute-done.13
  51.1 0.1 fusion
  51.2 0.7 collective-permute-start.16
  52.0 4.2 %collective-permute-done.16 = bf16[24,2560]{1,0:T(8,128)(2,1)S(1)} collective-permute-done((bf16[24,2560]{1,0:T(8,128)(2,1)S(1)}, bf16[24,2560]{1,0:T(8,128)(2,1)S(1)}, u32[]{:S(2)}, u32[]{:S(2)}) %collective-permute-start.16) | collective-permute-done | bytes 122912 | tf_op jit(solution)/shard_map/ppermute | solution.py:153
  56.3 3.1 %collective-permute-start.17 = (bf16[24,2560]{1,0:T(8,128)(2,1)S(1)}, bf16[24,2560]{1,0:T(8,128)(2,1)S(1)}, u32[]{:S(2)}, u32[]{:S(2)}) collective-permute-start(bf16[24,2560]{1,0:T(8,128)(2,1)S(1)} %pad_maximum_fusion.5), channel_id=1, source_target_pairs={{0,8},{1,9},{2,10},{3,11},{4,12},{5,13},{6,14},{7,15},{8,0},{9,1},... | collective-permute-start | bytes 368648 | tf_op jit(solution)/shard_map/ppermute | solution.py:153
  59.4 4.2 %collective-permute-done.17 = bf16[24,2560]{1,0:T(8,128)(2,1)S(1)} collective-permute-done((bf16[24,2560]{1,0:T(8,128)(2,1)S(1)}, bf16[24,2560]{1,0:T(8,128)(2,1)S(1)}, u32[]{:S(2)}, u32[]{:S(2)}) %collective-permute-start.17) | collective-permute-done | bytes 122912 | tf_op jit(solution)/shard_map/ppermute | solution.py:153
  63.6 0.1 tanh_convert_fusion
  63.7 0.1 collective-permute-start.18
  63.8 4.9 %collective-permute-done.18 = bf16[24,2560]{1,0:T(8,128)(2,1)S(1)} collective-permute-done((bf16[24,2560]{1,0:T(8,128)(2,1)S(1)}, bf16[24,2560]{1,0:T(8,128)(2,1)S(1)}, u32[]{:S(2)}, u32[]{:S(2)}) %collective-permute-start.18) | collective-permute-done | bytes 122912 | tf_op jit(solution)/shard_map/ppermute | solution.py:153
  68.7 1.8 %collective-permute-start.21 = (bf16[48,2560]{1,0:T(8,128)(2,1)S(1)}, bf16[48,2560]{1,0:T(8,128)(2,1)S(1)}, u32[]{:S(2)}, u32[]{:S(2)}) collective-permute-start(bf16[48,2560]{1,0:T(8,128)(2,1)S(1)} %pad_maximum_fusion.3.refs_0_), channel_id=1, source_target_pairs={{0,18},{1,19},{2,16},{3,17},{4,22},{5,23},{6,20},{7,21},{8,26},{9,... | collective-permute-start | bytes 737288 | tf_op jit(solution)/shard_map/ppermute | solution.py:153
  70.5 1.2 %collective-permute-start.20 = (bf16[48,2560]{1,0:T(8,128)(2,1)S(1)}, bf16[48,2560]{1,0:T(8,128)(2,1)S(1)}, u32[]{:S(2)}, u32[]{:S(2)}) collective-permute-start(bf16[48,2560]{1,0:T(8,128)(2,1)S(1)} %pad_maximum_fusion.3.refs_0_), channel_id=1, source_target_pairs={{0,16},{1,17},{2,18},{3,19},{4,20},{5,21},{6,22},{7,23},{8,24},{9,... | collective-permute-start | bytes 737288 | tf_op jit(solution)/shard_map/ppermute | solution.py:153
  71.7 0.5 collective-permute-start.19
  72.2 0.0 collective-permute-start.22
  72.2 3.7 %collective-permute-done.21.refs_3_ = bf16[48,2560]{1,0:T(8,128)(2,1)S(1)} collective-permute-done((bf16[48,2560]{1,0:T(8,128)(2,1)S(1)}, bf16[48,2560]{1,0:T(8,128)(2,1)S(1)}, u32[]{:S(2)}, u32[]{:S(2)}) %collective-permute-start.21) | collective-permute-done | bytes 245792 | tf_op jit(solution)/shard_map/ppermute | solution.py:153
  75.9 0.0 collective-permute-start.25
  75.9 2.5 %collective-permute-done.20.refs_2_ = bf16[48,2560]{1,0:T(8,128)(2,1)S(1)} collective-permute-done((bf16[48,2560]{1,0:T(8,128)(2,1)S(1)}, bf16[48,2560]{1,0:T(8,128)(2,1)S(1)}, u32[]{:S(2)}, u32[]{:S(2)}) %collective-permute-start.20) | collective-permute-done | bytes 245792 | tf_op jit(solution)/shard_map/ppermute | solution.py:153
  78.5 0.1 collective-permute-done.19.refs_1_
  78.6 0.4 collective-permute-start.23
  79.0 0.2 turn.1.refs_8_
  79.1 0.0 collective-permute-done.22.refs_4_
  79.1 0.0 collective-permute-done.25.refs_7_
  79.2 0.8 collective-permute-done.24.refs_6_
  80.0 0.4 collective-permute-done.23.refs_5_
  80.3 4.0 %update.1 = (bf16[384,2560]{1,0:T(8,128)(2,1)}, bf16[384,2560]{1,0:T(8,128)(2,1)}, bf16[384,2560]{1,0:T(8,128)(2,1)}) custom-call(bf16[48,2560]{1,0:T(8,128)(2,1)S(1)} %pad_maximum_fusion.3.refs_0_, bf16[48,2560]{1,0:T(8,128)(2,1)S(1)} %collective-permute-done.19.refs_1_, bf16[48,2560]{1,0:T(8,128)(2,1)S(1)} %collective-permute-done.20.refs_2_, ...), custom_call_target="tpu_custom_call" | custom-call | flops 754974720 | bytes 13762560 | tf_op jit(solution)/shard_map/update/pallas_call | solution.py:390
  (16 shorter events, 0.2 us)
Async XLA Ops:
  2.7 8.8 %collective-permute-start.2 = (bf16[12,2688]{1,0:T(8,128)(2,1)}, bf16[12,2688]{1,0:T(8,128)(2,1)S(1)}, u32[]{:S(2)}, u32[]{:S(2)}) collective-permute-start(bf16[12,2688]{1,0:T(8,128)(2,1)} %pack.1), channel_id=1, source_target_pairs={{0,12},{1,13},{2,14},{3,15},{4,8},{5,9},{6,10},{7,11},{8,4},{9,5},... | collective-permute-start | bytes 193544 | tf_op jit(solution)/shard_map/ppermute | solution.py:153
  7.8 6.4 %collective-permute-start.1 = (bf16[12,2688]{1,0:T(8,128)(2,1)}, bf16[12,2688]{1,0:T(8,128)(2,1)S(1)}, u32[]{:S(2)}, u32[]{:S(2)}) collective-permute-start(bf16[12,2688]{1,0:T(8,128)(2,1)} %pack.1), channel_id=1, source_target_pairs={{0,4},{1,5},{2,6},{3,7},{4,0},{5,1},{6,2},{7,3},{8,12},{9,13},{10,... | collective-permute-start | bytes 193544 | tf_op jit(solution)/shard_map/ppermute | solution.py:153
  7.8 7.4 %collective-permute-start = (bf16[12,2688]{1,0:T(8,128)(2,1)}, bf16[12,2688]{1,0:T(8,128)(2,1)S(1)}, u32[]{:S(2)}, u32[]{:S(2)}) collective-permute-start(bf16[12,2688]{1,0:T(8,128)(2,1)} %pack.1), channel_id=1, source_target_pairs={{0,8},{1,9},{2,10},{3,11},{4,12},{5,13},{6,14},{7,15},{8,0},{9,1},... | collective-permute-start | bytes 193544 | tf_op jit(solution)/shard_map/ppermute | solution.py:153
  16.2 9.7 %collective-permute-start.5 = (bf16[48,2688]{1,0:T(8,128)(2,1)S(1)}, bf16[48,2688]{1,0:T(8,128)(2,1)S(1)}, u32[]{:S(2)}, u32[]{:S(2)}) collective-permute-start(bf16[48,2688]{1,0:T(8,128)(2,1)S(1)} %pad_maximum_fusion.refs_0_), channel_id=1, source_target_pairs={{0,18},{1,19},{2,16},{3,17},{4,22},{5,23},{6,20},{7,21},{8,26},{9,... | collective-permute-start | bytes 774152 | tf_op jit(solution)/shard_map/ppermute | solution.py:153
  18.7 9.9 %collective-permute-start.4 = (bf16[48,2688]{1,0:T(8,128)(2,1)S(1)}, bf16[48,2688]{1,0:T(8,128)(2,1)S(1)}, u32[]{:S(2)}, u32[]{:S(2)}) collective-permute-start(bf16[48,2688]{1,0:T(8,128)(2,1)S(1)} %pad_maximum_fusion.refs_0_), channel_id=1, source_target_pairs={{0,16},{1,17},{2,18},{3,19},{4,20},{5,21},{6,22},{7,23},{8,24},{9,... | collective-permute-start | bytes 774152 | tf_op jit(solution)/shard_map/ppermute | solution.py:153
  19.2 9.6 %collective-permute-start.3 = (bf16[48,2688]{1,0:T(8,128)(2,1)S(1)}, bf16[48,2688]{1,0:T(8,128)(2,1)S(1)}, u32[]{:S(2)}, u32[]{:S(2)}) collective-permute-start(bf16[48,2688]{1,0:T(8,128)(2,1)S(1)} %pad_maximum_fusion.refs_0_), channel_id=1, source_target_pairs={{0,2},{1,3},{2,0},{3,1},{4,6},{5,7},{6,4},{7,5},{8,10},{9,11},{10,... | collective-permute-start | bytes 774152 | tf_op jit(solution)/shard_map/ppermute | solution.py:153
  19.8 13.4 %collective-permute-start.6 = (bf16[48,2688]{1,0:T(8,128)(2,1)S(1)}, bf16[48,2688]{1,0:T(8,128)(2,1)S(1)}, u32[]{:S(2)}, u32[]{:S(2)}) collective-permute-start(bf16[48,2688]{1,0:T(8,128)(2,1)S(1)} %pad_maximum_fusion.refs_0_), channel_id=1, source_target_pairs={{0,1},{1,0},{2,3},{3,2},{4,5},{5,4},{6,7},{7,6},{8,9},{9,8},{10,11... | collective-permute-start | bytes 774152 | tf_op jit(solution)/shard_map/ppermute | solution.py:153
  25.9 7.3 %collective-permute-start.9 = (bf16[48,2688]{1,0:T(8,128)(2,1)S(1)}, bf16[48,2688]{1,0:T(8,128)(2,1)S(1)}, u32[]{:S(2)}, u32[]{:S(2)}) collective-permute-start(bf16[48,2688]{1,0:T(8,128)(2,1)S(1)} %collective-permute-done.5.refs_3_), channel_id=1, source_target_pairs={{0,1},{1,0},{2,3},{3,2},{4,5},{5,4},{6,7},{7,6},{8,9},{9,8},{10,11... | collective-permute-start | bytes 774152 | tf_op jit(solution)/shard_map/ppermute | solution.py:153
  28.6 4.6 %collective-permute-start.8 = (bf16[48,2688]{1,0:T(8,128)(2,1)S(1)}, bf16[48,2688]{1,0:T(8,128)(2,1)S(1)}, u32[]{:S(2)}, u32[]{:S(2)}) collective-permute-start(bf16[48,2688]{1,0:T(8,128)(2,1)S(1)} %collective-permute-done.4.refs_2_), channel_id=1, source_target_pairs={{0,1},{1,0},{2,3},{3,2},{4,5},{5,4},{6,7},{7,6},{8,9},{9,8},{10,11... | collective-permute-start | bytes 774152 | tf_op jit(solution)/shard_map/ppermute | solution.py:153
  28.8 4.4 %collective-permute-start.7 = (bf16[48,2688]{1,0:T(8,128)(2,1)S(1)}, bf16[48,2688]{1,0:T(8,128)(2,1)S(1)}, u32[]{:S(2)}, u32[]{:S(2)}) collective-permute-start(bf16[48,2688]{1,0:T(8,128)(2,1)S(1)} %collective-permute-done.3.refs_1_), channel_id=1, source_target_pairs={{0,1},{1,0},{2,3},{3,2},{4,5},{5,4},{6,7},{7,6},{8,9},{9,8},{10,11... | collective-permute-start | bytes 774152 | tf_op jit(solution)/shard_map/ppermute | solution.py:153
  35.2 1.6 %collective-permute-start.11 = (bf16[48,2560]{1,0:T(8,128)(2,1)S(1)}, bf16[48,2560]{1,0:T(8,128)(2,1)S(1)}, u32[]{:S(2)}, u32[]{:S(2)}) collective-permute-start(bf16[48,2560]{1,0:T(8,128)(2,1)S(1)} %get-tuple-element.19), channel_id=1, source_target_pairs={{0,1},{1,0},{2,3},{3,2},{4,5},{5,4},{6,7},{7,6},{8,9},{9,8},{10,11... | collective-permute-start | bytes 737288 | tf_op jit(solution)/shard_map/ppermute | solution.py:153
  35.5 3.8 %collective-permute-start.10 = (bf16[144,2560]{1,0:T(8,128)(2,1)S(1)}, bf16[144,2560]{1,0:T(8,128)(2,1)S(1)}, u32[]{:S(2)}, u32[]{:S(2)}) collective-permute-start(bf16[144,2560]{1,0:T(8,128)(2,1)S(1)} %get-tuple-element.18), channel_id=1, source_target_pairs={{0,1},{1,0},{2,3},{3,2},{4,5},{5,4},{6,7},{7,6},{8,9},{9,8},{10,11... | collective-permute-start | bytes 2211848 | tf_op jit(solution)/shard_map/ppermute | solution.py:153
  36.9 5.5 %collective-permute-start.12 = (bf16[48,1280]{1,0:T(8,128)(2,1)S(1)}, bf16[48,1280]{1,0:T(8,128)(2,1)S(1)}, u32[]{:S(2)}, u32[]{:S(2)}) collective-permute-start(bf16[48,1280]{1,0:T(8,128)(2,1)S(1)} %get-tuple-element.31), channel_id=1, source_target_pairs={{0,16},{1,17},{2,18},{3,19},{4,20},{5,21},{6,22},{7,23},{8,24},{9,... | collective-permute-start | bytes 368648 | tf_op jit(solution)/shard_map/ppermute | solution.py:153
  38.6 5.1 %collective-permute-start.14 = (bf16[48,1280]{1,0:T(8,128)(2,1)S(1)}, bf16[48,1280]{1,0:T(8,128)(2,1)S(1)}, u32[]{:S(2)}, u32[]{:S(2)}) collective-permute-start(bf16[48,1280]{1,0:T(8,128)(2,1)S(1)} %get-tuple-element.32), channel_id=1, source_target_pairs={{0,2},{1,3},{2,0},{3,1},{4,6},{5,7},{6,4},{7,5},{8,10},{9,11},{10,... | collective-permute-start | bytes 368648 | tf_op jit(solution)/shard_map/ppermute | solution.py:153
  43.7 36.6 %copy-start.2 = (bf16[1,384,2560]{2,1,0:T(8,128)(2,1)S(1)}, bf16[1,384,2560]{2,1,0:T(8,128)(2,1)}, u32[]{:S(2)}) copy-start(bf16[1,384,2560]{2,1,0:T(8,128)(2,1)} %param.15) | copy-start | bytes 5898244
  43.7 19.9 %copy-start.3 = (bf16[12,2688]{1,0:T(8,128)(2,1)S(1)}, bf16[12,2688]{1,0:T(8,128)(2,1)}, u32[]{:S(2)}) copy-start(bf16[12,2688]{1,0:T(8,128)(2,1)} %pack.1) | copy-start | bytes 193540
  43.8 6.9 %collective-permute-start.15 = (bf16[48,2560]{1,0:T(8,128)(2,1)S(1)}, bf16[48,2560]{1,0:T(8,128)(2,1)S(1)}, u32[]{:S(2)}, u32[]{:S(2)}) collective-permute-start(bf16[48,2560]{1,0:T(8,128)(2,1)S(1)} %pad_maximum_fusion.2), channel_id=1, source_target_pairs={{0,16},{1,17},{2,18},{3,19},{4,20},{5,21},{6,22},{7,23},{8,24},{9,... | collective-permute-start | bytes 737288 | tf_op jit(solution)/shard_map/ppermute | solution.py:153
  44.3 36.0 %copy-start = (bf16[1,384,2560]{2,1,0:T(8,128)(2,1)S(1)}, bf16[1,384,2560]{2,1,0:T(8,128)(2,1)}, u32[]{:S(2)}) copy-start(bf16[1,384,2560]{2,1,0:T(8,128)(2,1)} %param.13) | copy-start | bytes 5898244
  44.3 36.0 %copy-start.1 = (bf16[1,384,2560]{2,1,0:T(8,128)(2,1)S(1)}, bf16[1,384,2560]{2,1,0:T(8,128)(2,1)}, u32[]{:S(2)}) copy-start(bf16[1,384,2560]{2,1,0:T(8,128)(2,1)} %param.14) | copy-start | bytes 5898244
  44.3 6.8 %collective-permute-start.13 = (bf16[48,2560]{1,0:T(8,128)(2,1)S(1)}, bf16[48,2560]{1,0:T(8,128)(2,1)S(1)}, u32[]{:S(2)}, u32[]{:S(2)}) collective-permute-start(bf16[48,2560]{1,0:T(8,128)(2,1)S(1)} %pad_maximum_fusion.1), channel_id=1, source_target_pairs={{0,2},{1,3},{2,0},{3,1},{4,6},{5,7},{6,4},{7,5},{8,10},{9,11},{10,... | collective-permute-start | bytes 737288 | tf_op jit(solution)/shard_map/ppermute | solution.py:153
  51.2 4.9 %collective-permute-start.16 = (bf16[24,2560]{1,0:T(8,128)(2,1)S(1)}, bf16[24,2560]{1,0:T(8,128)(2,1)S(1)}, u32[]{:S(2)}, u32[]{:S(2)}) collective-permute-start(bf16[24,2560]{1,0:T(8,128)(2,1)S(1)} %split.35), channel_id=1, source_target_pairs={{0,4},{1,5},{2,6},{3,7},{4,0},{5,1},{6,2},{7,3},{8,12},{9,13},{10,... | collective-permute-start | bytes 368648 | tf_op jit(solution)/shard_map/ppermute | solution.py:153
  56.3 7.3 %collective-permute-start.17 = (bf16[24,2560]{1,0:T(8,128)(2,1)S(1)}, bf16[24,2560]{1,0:T(8,128)(2,1)S(1)}, u32[]{:S(2)}, u32[]{:S(2)}) collective-permute-start(bf16[24,2560]{1,0:T(8,128)(2,1)S(1)} %pad_maximum_fusion.5), channel_id=1, source_target_pairs={{0,8},{1,9},{2,10},{3,11},{4,12},{5,13},{6,14},{7,15},{8,0},{9,1},... | collective-permute-start | bytes 368648 | tf_op jit(solution)/shard_map/ppermute | solution.py:153
  63.7 4.9 %collective-permute-start.18 = (bf16[24,2560]{1,0:T(8,128)(2,1)S(1)}, bf16[24,2560]{1,0:T(8,128)(2,1)S(1)}, u32[]{:S(2)}, u32[]{:S(2)}) collective-permute-start(bf16[24,2560]{1,0:T(8,128)(2,1)S(1)} %tanh_convert_fusion), channel_id=1, source_target_pairs={{0,4},{1,5},{2,6},{3,7},{4,0},{5,1},{6,2},{7,3},{8,12},{9,13},{10,... | collective-permute-start | bytes 368648 | tf_op jit(solution)/shard_map/ppermute | solution.py:153
  68.7 7.3 %collective-permute-start.21 = (bf16[48,2560]{1,0:T(8,128)(2,1)S(1)}, bf16[48,2560]{1,0:T(8,128)(2,1)S(1)}, u32[]{:S(2)}, u32[]{:S(2)}) collective-permute-start(bf16[48,2560]{1,0:T(8,128)(2,1)S(1)} %pad_maximum_fusion.3.refs_0_), channel_id=1, source_target_pairs={{0,18},{1,19},{2,16},{3,17},{4,22},{5,23},{6,20},{7,21},{8,26},{9,... | collective-permute-start | bytes 737288 | tf_op jit(solution)/shard_map/ppermute | solution.py:153
  70.5 8.0 %collective-permute-start.20 = (bf16[48,2560]{1,0:T(8,128)(2,1)S(1)}, bf16[48,2560]{1,0:T(8,128)(2,1)S(1)}, u32[]{:S(2)}, u32[]{:S(2)}) collective-permute-start(bf16[48,2560]{1,0:T(8,128)(2,1)S(1)} %pad_maximum_fusion.3.refs_0_), channel_id=1, source_target_pairs={{0,16},{1,17},{2,18},{3,19},{4,20},{5,21},{6,22},{7,23},{8,24},{9,... | collective-permute-start | bytes 737288 | tf_op jit(solution)/shard_map/ppermute | solution.py:153
  71.7 6.9 %collective-permute-start.19 = (bf16[48,2560]{1,0:T(8,128)(2,1)S(1)}, bf16[48,2560]{1,0:T(8,128)(2,1)S(1)}, u32[]{:S(2)}, u32[]{:S(2)}) collective-permute-start(bf16[48,2560]{1,0:T(8,128)(2,1)S(1)} %pad_maximum_fusion.3.refs_0_), channel_id=1, source_target_pairs={{0,2},{1,3},{2,0},{3,1},{4,6},{5,7},{6,4},{7,5},{8,10},{9,11},{10,... | collective-permute-start | bytes 737288 | tf_op jit(solution)/shard_map/ppermute | solution.py:153
  72.2 6.9 %collective-permute-start.22 = (bf16[48,2560]{1,0:T(8,128)(2,1)S(1)}, bf16[48,2560]{1,0:T(8,128)(2,1)S(1)}, u32[]{:S(2)}, u32[]{:S(2)}) collective-permute-start(bf16[48,2560]{1,0:T(8,128)(2,1)S(1)} %pad_maximum_fusion.3.refs_0_), channel_id=1, source_target_pairs={{0,1},{1,0},{2,3},{3,2},{4,5},{5,4},{6,7},{7,6},{8,9},{9,8},{10,11... | collective-permute-start | bytes 737288 | tf_op jit(solution)/shard_map/ppermute | solution.py:153
  75.9 3.2 %collective-permute-start.25 = (bf16[48,2560]{1,0:T(8,128)(2,1)S(1)}, bf16[48,2560]{1,0:T(8,128)(2,1)S(1)}, u32[]{:S(2)}, u32[]{:S(2)}) collective-permute-start(bf16[48,2560]{1,0:T(8,128)(2,1)S(1)} %collective-permute-done.21.refs_3_), channel_id=1, source_target_pairs={{0,1},{1,0},{2,3},{3,2},{4,5},{5,4},{6,7},{7,6},{8,9},{9,8},{10,11... | collective-permute-start | bytes 737288 | tf_op jit(solution)/shard_map/ppermute | solution.py:153
  78.4 1.5 %collective-permute-start.24 = (bf16[48,2560]{1,0:T(8,128)(2,1)S(1)}, bf16[48,2560]{1,0:T(8,128)(2,1)S(1)}, u32[]{:S(2)}, u32[]{:S(2)}) collective-permute-start(bf16[48,2560]{1,0:T(8,128)(2,1)S(1)} %collective-permute-done.20.refs_2_), channel_id=1, source_target_pairs={{0,1},{1,0},{2,3},{3,2},{4,5},{5,4},{6,7},{7,6},{8,9},{9,8},{10,11... | collective-permute-start | bytes 737288 | tf_op jit(solution)/shard_map/ppermute | solution.py:153
  78.6 1.8 %collective-permute-start.23 = (bf16[48,2560]{1,0:T(8,128)(2,1)S(1)}, bf16[48,2560]{1,0:T(8,128)(2,1)S(1)}, u32[]{:S(2)}, u32[]{:S(2)}) collective-permute-start(bf16[48,2560]{1,0:T(8,128)(2,1)S(1)} %collective-permute-done.19.refs_1_), channel_id=1, source_target_pairs={{0,1},{1,0},{2,3},{3,2},{4,5},{5,4},{6,7},{7,6},{8,9},{9,8},{10,11... | collective-permute-start | bytes 737288 | tf_op jit(solution)/shard_map/ppermute | solution.py:153
